TPU v7x, 512 devices: a whole 4x8x8 slice. The times are simulated.
512 devices in a mesh: inst: 16 (over y_hi, x), cells: 32 (over z, y_lo, core).
Axes of the slice: x: 4, y: 8 (y_hi: 4, y_lo: 2; y = y_hi * 2 + y_lo), z: 8, core: 2. Of those that a mesh axis runs over, the one named last changes fastest.
Arguments:
- adjoint: float32 [16, 5, 128, 16, 128], P('inst', None, 'cells'), may hold values from -6 to 6
- objective_gradient: float32 [16, 5, 128, 16, 128], P('inst', None, 'cells'), may hold values from -6 to 6
- jacobian: float32 [16, 3, 5, 5, 128, 16, 128], P('inst', None, None, None, 'cells'), may hold values from -2.5 to 2.5
- second_coef: float32 [16, 3, 128, 16, 128], P('inst', None, 'cells'), may hold values from 0.05 to 0.5
- fourth_coef: float32 [16, 3, 128, 16, 128], P('inst', None, 'cells'), may hold values from 0.01 to 0.1
- time_step: float32 [16, 128, 16, 128], P('inst', 'cells'), may hold values from 0.03 to 0.15
- frequency: float32 [1], replicated, may hold values from 0.5 to 1.5
- damping: float32 [1], replicated, may hold values from 0.02 to 0.08
Outputs:
- updated: float32 [16, 5, 128, 16, 128], P('inst', None, 'cells')
All inputs are finite; a program needn't handle non-finite values.
Results may differ from a plain program's by a relative error of at most 0.0001.
Values sent between devices are 32-bit elements; how exact they have to be, the bound alone decides.
No kernel may reach another device: no remote copies, remote signals or barrier semaphores. Data moves between devices by JAX's collectives and lax.ppermute only.
A program may use at most 64 MiB of HBM per device.

v0:
```python
import math

import jax
import jax.numpy as jnp
from jax import lax
from jax.sharding import PartitionSpec as P

INSTANCES = 16


def padded_2(array, sides, width):
    for axis, dim in sides:
        devices, length = (lax.axis_size(axis), array.shape[dim])
        up = [(i, (i + 1) % devices) for i in range(devices - 1)]
        down = [(j, i) for i, j in up]
        last = lax.slice_in_dim(array, length - width, length, axis=dim)
        initial = lax.slice_in_dim(array, 0, width, axis=dim)
        before = lax.ppermute(last, axis, up)
        after = lax.ppermute(initial, axis, down)
        array = jnp.concatenate([before, array, after], axis=dim)
    return array


def spectral_coupling(frequency_value, damping_value, count):
    positions = jnp.arange(count, dtype=jnp.int32)
    offsets = positions[:, None] - positions[None, :]
    parity = jnp.where(offsets % 2 == 0, 1.0, -1.0).astype(jnp.float32)
    angle = math.pi / count * offsets.astype(jnp.float32)
    off_diag = offsets != 0
    sine = jnp.where(off_diag, jnp.sin(angle), 1.0)
    slope = jnp.where(off_diag, 0.5 * parity * jnp.cos(angle) / sine, 0.0)
    curve = jnp.where(off_diag, parity * 0.5 / (sine * sine), count * count / 12.0 + 1.0 / 6.0)
    return frequency_value * slope + damping_value * curve


def face_terms(padded, second_pad, fourth_pad, grid_axis):
    length = padded.shape[grid_axis] - 4

    def cut(source, first, size):
        return lax.slice_in_dim(source, first, first + size, axis=grid_axis)

    jumps = cut(padded, 1, length + 3) - cut(padded, 0, length + 3)
    second_flux = cut(second_pad, 0, length + 3) * jumps
    fourth_flux = cut(fourth_pad, 0, length + 3) * jumps
    divided = cut(fourth_flux, 1, length + 2) - cut(fourth_flux, 0, length + 2)
    central = 0.5 * (cut(padded, 1, length) - cut(padded, 3, length))
    damped = cut(second_flux, 1, length) - cut(second_flux, 2, length)
    damped = (
        damped + cut(divided, 2, length) - 2.0 * cut(divided, 1, length) + cut(divided, 0, length)
    )
    return (central, damped)


def on_device(
    adjoint, objective_gradient, jacobian, second_coef, fourth_coef, time_step, frequency, damping
):
    coupling = spectral_coupling(frequency[0], damping[0], INSTANCES)
    local_count = adjoint.shape[0]
    own_first = lax.axis_index("inst") * local_count
    stacked = jnp.stack([second_coef[:, 0], fourth_coef[:, 0]], axis=1)
    coef_rim = padded_2(stacked, (("cells", 2),), 2)
    second_pads = [coef_rim[:, 0:1]]
    fourth_pads = [coef_rim[:, 1:2]]
    for direction in (1, 2):
        widths = [(0, 0), (0, 0), (0, 0), (0, 0), (0, 0)]
        widths[2 + direction] = (2, 2)
        second_pads.append(jnp.pad(second_coef[:, direction][:, None], widths))
        fourth_pads.append(jnp.pad(fourth_coef[:, direction][:, None], widths))
    section_state = adjoint
    for section_coef in (0.25, 1.0 / 6.0, 0.375, 0.5, 1.0):
        summed = jnp.zeros_like(section_state)
        for spatial_direction in range(3):
            grid_axis = 2 + spatial_direction
            if spatial_direction == 0:
                padded = padded_2(section_state, (("cells", 2),), 2)
            else:
                spatial_widths = [(0, 0), (0, 0), (0, 0), (0, 0), (0, 0)]
                spatial_widths[grid_axis] = (2, 2)
                padded = jnp.pad(section_state, spatial_widths)
            central, damped = face_terms(
                padded, second_pads[spatial_direction], fourth_pads[spatial_direction], grid_axis
            )
            summed = (
                summed
                + jnp.sum(jacobian[:, spatial_direction] * central[:, :, None], axis=1)
                + damped
            )
        shard_rows = lax.all_gather(section_state, "inst", axis=0, tiled=True)
        table_rows = lax.dynamic_slice(coupling, (0, own_first), (shard_rows.shape[0], local_count))
        residual = (
            summed
            + jnp.einsum("jk,jvxyz->kvxyz", table_rows, shard_rows, precision=lax.Precision.HIGHEST)
            + objective_gradient
        )
        section_state = adjoint - section_coef * time_step[:, None] * residual
    return section_state


def solution(mesh):
    placed = (
        P("inst", None, "cells", None, None),
        P("inst", None, "cells", None, None),
        P("inst", None, None, None, "cells", None, None),
        P("inst", None, "cells", None, None),
        P("inst", None, "cells", None, None),
        P("inst", "cells", None, None),
        P(),
        P(),
    )
    return jax.shard_map(
        on_device,
        mesh=mesh,
        in_specs=placed,
        out_specs=P("inst", None, "cells", None, None),
        check_vma=False,
    )
```

profile of v0, /device:TPU:1, one launch (start us, length us, event | category | flops | bytes accessed | tf_op | source)
XLA Modules:
  0.0 388.0 jit_solution(4702164567849891640)
XLA Ops:
  8.9 4.6 %collective-permute-start.2 = (f32[1,2,2,16,128]{4,3,2,1,0:T(8,128)S(1)}, f32[1,2,2,16,128]{4,3,2,1,0:T(8,128)S(1)}, u32[]{:S(2)}, u32[]{:S(2)}) collective-permute-start(f32[1,2,2,16,128]{4,3,2,1,0:T(8,128)S(1)} %get-tuple-element.84), channel_id=1, source_target_pairs={{0,1},{1,2},{2,3},{3,4},{4,5},{5,6},{6,7},{7,8},{8,9},{9,10},{10,1... | collective-permute-start | bytes 98312 | tf_op jit(solution)/shard_map/ppermute | solution.py:18
  13.5 5.5 %collective-permute-start.3 = (f32[1,2,2,16,128]{4,3,2,1,0:T(8,128)S(1)}, f32[1,2,2,16,128]{4,3,2,1,0:T(8,128)}, u32[]{:S(2)}, u32[]{:S(2)}) collective-permute-start(f32[1,2,2,16,128]{4,3,2,1,0:T(8,128)S(1)} %get-tuple-element.85), channel_id=1, source_target_pairs={{1,0},{2,1},{3,2},{4,3},{5,4},{6,5},{7,6},{8,7},{9,8},{10,9},{11,1... | collective-permute-start | bytes 98312 | tf_op jit(solution)/shard_map/ppermute | solution.py:19
  22.5 3.6 collective-permute-start
  28.5 2.2 broadcast_multiply_fusion.29
  38.8 45.2 %all-gather.6.cloned.1.call-done = f32[16,5,4,16,128]{4,3,2,1,0:T(8,128)} async-done(((f32[1,5,4,16,128]{4,3,2,1,0:T(8,128)}), f32[16,5,4,16,128]{4,3,2,1,0:T(8,128)}) %all-gather.6.cloned.1.call-update) | async-done | bytes 2621456 | tf_op jit(solution)/shard_map/all_gather | solution.py:88
  84.1 4.6 %fusion.8 = f32[1,5,4,16,128]{4,0,3,2,1:T(1,128)S(1)} fusion(f32[16,5,4,16,128]{4,3,2,1,0:T(8,128)} %all-gather.6.cloned.1.call-done, pred[16,16]{0,1:T(8,128)(4,1)} %fusion.144, s32[]{:T(128)S(6)} %select_n.39, f32[16,16]{0,1:T(8,128)S(1)} %get-tuple-element.90, f32[16,16]{0,1:T(8,128)} %get-tuple-element.91, f32[16,16]{0,1:T(8,128)S(1)} %fusion.149, ...), kind=kOutput, calls=%fused_computation.8 | convolution fusion | flops 7864496 | bytes 2788356 | tf_op jit(solution)/shard_map/jk,jvxyz->kvxyz/dot_general | solution.py:92
  93.4 2.4 collective-permute-start.5
  95.8 2.0 broadcast_multiply_fusion.28
  97.9 2.3 broadcast_multiply_fusion.8
  104.0 53.1 %all-gather.8.cloned.1.call-done = f32[16,5,4,16,128]{4,3,2,1,0:T(8,128)} async-done(((f32[1,5,4,16,128]{4,3,2,1,0:T(8,128)}), f32[16,5,4,16,128]{4,3,2,1,0:T(8,128)}) %all-gather.8.cloned.1.call-update) | async-done | bytes 2621456 | tf_op jit(solution)/shard_map/all_gather | solution.py:88
  157.1 4.6 %fusion.6 = f32[1,5,4,16,128]{4,0,3,2,1:T(1,128)S(1)} fusion(f32[16,5,4,16,128]{4,3,2,1,0:T(8,128)} %all-gather.8.cloned.1.call-done, pred[16,16]{0,1:T(8,128)(4,1)} %fusion.144, s32[]{:T(128)S(6)} %select_n.39, f32[16,16]{0,1:T(8,128)S(1)} %get-tuple-element.90, f32[16,16]{0,1:T(8,128)} %get-tuple-element.91, f32[16,16]{0,1:T(8,128)S(1)} %fusion.149, ...), kind=kOutput, calls=%fused_computation.6 | convolution fusion | flops 7864496 | bytes 2788356 | tf_op jit(solution)/shard_map/jk,jvxyz->kvxyz/dot_general | solution.py:92
  166.4 2.6 collective-permute-start.7
  169.0 2.0 broadcast_multiply_fusion.27
  171.0 2.3 broadcast_multiply_fusion.7
  177.1 52.9 %all-gather.10.cloned.1.call-done = f32[16,5,4,16,128]{4,3,2,1,0:T(8,128)} async-done(((f32[1,5,4,16,128]{4,3,2,1,0:T(8,128)}), f32[16,5,4,16,128]{4,3,2,1,0:T(8,128)}) %all-gather.10.cloned.1.call-update) | async-done | bytes 2621456 | tf_op jit(solution)/shard_map/all_gather | solution.py:88
  230.0 4.6 %fusion.4 = f32[1,5,4,16,128]{4,0,3,2,1:T(1,128)S(1)} fusion(f32[16,5,4,16,128]{4,3,2,1,0:T(8,128)} %all-gather.10.cloned.1.call-done, pred[16,16]{0,1:T(8,128)(4,1)} %fusion.144, s32[]{:T(128)S(6)} %select_n.39, f32[16,16]{0,1:T(8,128)S(1)} %get-tuple-element.90, f32[16,16]{0,1:T(8,128)} %get-tuple-element.91, f32[16,16]{0,1:T(8,128)S(1)} %fusion.149, ...), kind=kOutput, calls=%fused_computation.4 | convolution fusion | flops 7864496 | bytes 2788356 | tf_op jit(solution)/shard_map/jk,jvxyz->kvxyz/dot_general | solution.py:92
  239.4 2.4 collective-permute-start.9
  243.9 2.3 broadcast_multiply_fusion.6
  249.9 53.1 %all-gather.12.cloned.1.call-done = f32[16,5,4,16,128]{4,3,2,1,0:T(8,128)} async-done(((f32[1,5,4,16,128]{4,3,2,1,0:T(8,128)}), f32[16,5,4,16,128]{4,3,2,1,0:T(8,128)}) %all-gather.12.cloned.1.call-update) | async-done | bytes 2621456 | tf_op jit(solution)/shard_map/all_gather | solution.py:88
  303.0 4.6 %fusion.2 = f32[1,5,4,16,128]{4,0,3,2,1:T(1,128)S(1)} fusion(f32[16,5,4,16,128]{4,3,2,1,0:T(8,128)} %all-gather.12.cloned.1.call-done, pred[16,16]{0,1:T(8,128)(4,1)} %fusion.144, s32[]{:T(128)S(6)} %select_n.39, f32[16,16]{0,1:T(8,128)S(1)} %get-tuple-element.90, f32[16,16]{0,1:T(8,128)} %get-tuple-element.91, f32[16,16]{0,1:T(8,128)S(1)} %fusion.149, ...), kind=kOutput, calls=%fused_computation.2 | convolution fusion | flops 7864496 | bytes 2788356 | tf_op jit(solution)/shard_map/jk,jvxyz->kvxyz/dot_general | solution.py:92
  312.4 2.6 collective-permute-start.11
  317.0 2.3 broadcast_multiply_fusion.5
  321.7 54.2 %all-gather.14.cloned.1.call-done = f32[16,5,4,16,128]{4,3,2,1,0:T(8,128)} async-done(((f32[1,5,4,16,128]{4,3,2,1,0:T(8,128)}), f32[16,5,4,16,128]{4,3,2,1,0:T(8,128)}) %all-gather.14.cloned.1.call-update) | async-done | bytes 2621456 | tf_op jit(solution)/shard_map/all_gather | solution.py:88
  376.0 4.4 %fusion = f32[1,5,4,16,128]{4,0,3,2,1:T(1,128)S(1)} fusion(f32[16,5,4,16,128]{4,3,2,1,0:T(8,128)} %all-gather.14.cloned.1.call-done, pred[16,16]{0,1:T(8,128)(4,1)} %fusion.144, s32[]{:T(128)S(6)} %select_n.39, f32[16,16]{0,1:T(8,128)S(1)} %get-tuple-element.90, f32[16,16]{0,1:T(8,128)} %get-tuple-element.91, f32[16,16]{0,1:T(8,128)S(1)} %fusion.149, ...), kind=kOutput, calls=%fused_computation | convolution fusion | flops 7864496 | bytes 2788356 | tf_op jit(solution)/shard_map/jk,jvxyz->kvxyz/dot_general | solution.py:92
  (180 shorter events, 52.0 us)
Async XLA Ops:
  6.5 77.5 %all-gather.6.cloned.1.call-start = ((), (), s32[]{:S(2)}) async-start(), calls=%async_computation | async-start | bytes 2785280 | tf_op jit(solution)/shard_map/all_gather | solution.py:88
  7.3 149.8 %all-gather.8.cloned.1.call-start = ((), (), s32[]{:S(2)}) async-start(), calls=%async_computation.1 | async-start | bytes 2785280 | tf_op jit(solution)/shard_map/all_gather | solution.py:88
  8.9 25.7 %collective-permute-start.2 = (f32[1,2,2,16,128]{4,3,2,1,0:T(8,128)S(1)}, f32[1,2,2,16,128]{4,3,2,1,0:T(8,128)S(1)}, u32[]{:S(2)}, u32[]{:S(2)}) collective-permute-start(f32[1,2,2,16,128]{4,3,2,1,0:T(8,128)S(1)} %get-tuple-element.84), channel_id=1, source_target_pairs={{0,1},{1,2},{2,3},{3,4},{4,5},{5,6},{6,7},{7,8},{8,9},{9,10},{10,1... | collective-permute-start | bytes 98312 | tf_op jit(solution)/shard_map/ppermute | solution.py:18
  13.5 21.7 %collective-permute-start.3 = (f32[1,2,2,16,128]{4,3,2,1,0:T(8,128)S(1)}, f32[1,2,2,16,128]{4,3,2,1,0:T(8,128)}, u32[]{:S(2)}, u32[]{:S(2)}) collective-permute-start(f32[1,2,2,16,128]{4,3,2,1,0:T(8,128)S(1)} %get-tuple-element.85), channel_id=1, source_target_pairs={{1,0},{2,1},{3,2},{4,3},{5,4},{6,5},{7,6},{8,7},{9,8},{10,9},{11,1... | collective-permute-start | bytes 98312 | tf_op jit(solution)/shard_map/ppermute | solution.py:19
  20.6 15.4 %collective-permute-start.1 = (f32[1,5,2,16,128]{4,3,2,1,0:T(8,128)}, f32[1,5,2,16,128]{4,3,2,1,0:T(8,128)S(1)}, u32[]{:S(2)}, u32[]{:S(2)}) collective-permute-start(f32[1,5,2,16,128]{4,3,2,1,0:T(8,128)} %get-tuple-element.70), channel_id=1, source_target_pairs={{1,0},{2,1},{3,2},{4,3},{5,4},{6,5},{7,6},{8,7},{9,8},{10,9},{11,1... | collective-permute-start | bytes 245768 | tf_op jit(solution)/shard_map/ppermute | solution.py:19
  22.5 13.5 %collective-permute-start = (f32[1,5,2,16,128]{4,3,2,1,0:T(8,128)}, f32[1,5,2,16,128]{4,3,2,1,0:T(8,128)S(1)}, u32[]{:S(2)}, u32[]{:S(2)}) collective-permute-start(f32[1,5,2,16,128]{4,3,2,1,0:T(8,128)} %get-tuple-element.71), channel_id=1, source_target_pairs={{0,1},{1,2},{2,3},{3,4},{4,5},{5,6},{6,7},{7,8},{8,9},{9,10},{10,1... | collective-permute-start | bytes 245768 | tf_op jit(solution)/shard_map/ppermute | solution.py:18
  90.5 139.5 %all-gather.10.cloned.1.call-start = ((), (), s32[]{:S(2)}) async-start(), calls=%async_computation.2 | async-start | bytes 2785280 | tf_op jit(solution)/shard_map/all_gather | solution.py:88
  91.5 9.6 %collective-permute-start.4 = (f32[1,5,2,16,128]{4,3,2,1,0:T(8,128)S(1)}, f32[1,5,2,16,128]{4,3,2,1,0:T(8,128)S(1)}, u32[]{:S(2)}, u32[]{:S(2)}) collective-permute-start(f32[1,5,2,16,128]{4,3,2,1,0:T(8,128)S(1)} %get-tuple-element.60), channel_id=1, source_target_pairs={{0,1},{1,2},{2,3},{3,4},{4,5},{5,6},{6,7},{7,8},{8,9},{9,10},{10,1... | collective-permute-start | bytes 245768 | tf_op jit(solution)/shard_map/ppermute | solution.py:18
  93.4 7.7 %collective-permute-start.5 = (f32[1,5,2,16,128]{4,3,2,1,0:T(8,128)S(1)}, f32[1,5,2,16,128]{4,3,2,1,0:T(8,128)S(1)}, u32[]{:S(2)}, u32[]{:S(2)}) collective-permute-start(f32[1,5,2,16,128]{4,3,2,1,0:T(8,128)S(1)} %get-tuple-element.61), channel_id=1, source_target_pairs={{1,0},{2,1},{3,2},{4,3},{5,4},{6,5},{7,6},{8,7},{9,8},{10,9},{11,1... | collective-permute-start | bytes 245768 | tf_op jit(solution)/shard_map/ppermute | solution.py:19
  163.5 139.5 %all-gather.12.cloned.1.call-start = ((), (), s32[]{:S(2)}) async-start(), calls=%async_computation.3 | async-start | bytes 2785280 | tf_op jit(solution)/shard_map/all_gather | solution.py:88
  164.5 9.8 %collective-permute-start.6 = (f32[1,5,2,16,128]{4,3,2,1,0:T(8,128)S(1)}, f32[1,5,2,16,128]{4,3,2,1,0:T(8,128)S(1)}, u32[]{:S(2)}, u32[]{:S(2)}) collective-permute-start(f32[1,5,2,16,128]{4,3,2,1,0:T(8,128)S(1)} %get-tuple-element.51), channel_id=1, source_target_pairs={{0,1},{1,2},{2,3},{3,4},{4,5},{5,6},{6,7},{7,8},{8,9},{9,10},{10,1... | collective-permute-start | bytes 245768 | tf_op jit(solution)/shard_map/ppermute | solution.py:18
  166.4 7.9 %collective-permute-start.7 = (f32[1,5,2,16,128]{4,3,2,1,0:T(8,128)S(1)}, f32[1,5,2,16,128]{4,3,2,1,0:T(8,128)S(1)}, u32[]{:S(2)}, u32[]{:S(2)}) collective-permute-start(f32[1,5,2,16,128]{4,3,2,1,0:T(8,128)S(1)} %get-tuple-element.52), channel_id=1, source_target_pairs={{1,0},{2,1},{3,2},{4,3},{5,4},{6,5},{7,6},{8,7},{9,8},{10,9},{11,1... | collective-permute-start | bytes 245768 | tf_op jit(solution)/shard_map/ppermute | solution.py:19
  236.5 139.5 %all-gather.14.cloned.1.call-start = ((), (), s32[]{:S(2)}) async-start(), calls=%async_computation.4 | async-start | bytes 2785280 | tf_op jit(solution)/shard_map/all_gather | solution.py:88
  237.5 9.6 %collective-permute-start.8 = (f32[1,5,2,16,128]{4,3,2,1,0:T(8,128)S(1)}, f32[1,5,2,16,128]{4,3,2,1,0:T(8,128)S(1)}, u32[]{:S(2)}, u32[]{:S(2)}) collective-permute-start(f32[1,5,2,16,128]{4,3,2,1,0:T(8,128)S(1)} %get-tuple-element.42), channel_id=1, source_target_pairs={{0,1},{1,2},{2,3},{3,4},{4,5},{5,6},{6,7},{7,8},{8,9},{9,10},{10,1... | collective-permute-start | bytes 245768 | tf_op jit(solution)/shard_map/ppermute | solution.py:18
  239.4 7.7 %collective-permute-start.9 = (f32[1,5,2,16,128]{4,3,2,1,0:T(8,128)S(1)}, f32[1,5,2,16,128]{4,3,2,1,0:T(8,128)S(1)}, u32[]{:S(2)}, u32[]{:S(2)}) collective-permute-start(f32[1,5,2,16,128]{4,3,2,1,0:T(8,128)S(1)} %get-tuple-element.43), channel_id=1, source_target_pairs={{1,0},{2,1},{3,2},{4,3},{5,4},{6,5},{7,6},{8,7},{9,8},{10,9},{11,1... | collective-permute-start | bytes 245768 | tf_op jit(solution)/shard_map/ppermute | solution.py:19
  310.4 9.8 %collective-permute-start.10 = (f32[1,5,2,16,128]{4,3,2,1,0:T(8,128)S(1)}, f32[1,5,2,16,128]{4,3,2,1,0:T(8,128)S(1)}, u32[]{:S(2)}, u32[]{:S(2)}) collective-permute-start(f32[1,5,2,16,128]{4,3,2,1,0:T(8,128)S(1)} %get-tuple-element.33), channel_id=1, source_target_pairs={{0,1},{1,2},{2,3},{3,4},{4,5},{5,6},{6,7},{7,8},{8,9},{9,10},{10,1... | collective-permute-start | bytes 245768 | tf_op jit(solution)/shard_map/ppermute | solution.py:18
  312.4 7.9 %collective-permute-start.11 = (f32[1,5,2,16,128]{4,3,2,1,0:T(8,128)S(1)}, f32[1,5,2,16,128]{4,3,2,1,0:T(8,128)S(1)}, u32[]{:S(2)}, u32[]{:S(2)}) collective-permute-start(f32[1,5,2,16,128]{4,3,2,1,0:T(8,128)S(1)} %get-tuple-element.34), channel_id=1, source_target_pairs={{1,0},{2,1},{3,2},{4,3},{5,4},{6,5},{7,6},{8,7},{9,8},{10,9},{11,1... | collective-permute-start | bytes 245768 | tf_op jit(solution)/shard_map/ppermute | solution.py:19
  321.6 58.8 %copy-start.12 = (f32[1,5,4,16,130]{4,3,2,1,0:T(8,128)S(1)}, f32[1,5,4,16,130]{4,3,2,1,0:T(8,128)}, u32[]{:S(2)}) copy-start(f32[1,5,4,16,130]{4,3,2,1,0:T(8,128)} %slice_subtract_fusion) | copy-start | bytes 499204
  321.6 58.8 %copy-start.17 = (f32[1,5,4,19,128]{4,3,2,1,0:T(8,128)S(1)}, f32[1,5,4,19,128]{4,3,2,1,0:T(8,128)}, u32[]{:S(2)}) copy-start(f32[1,5,4,19,128]{4,3,2,1,0:T(8,128)} %get-tuple-element.35) | copy-start | bytes 583684
  321.6 58.8 %copy-start.26 = (f32[1,5,4,16,131]{4,3,2,1,0:T(8,128)S(1)}, f32[1,5,4,16,131]{4,3,2,1,0:T(8,128)}, u32[]{:S(2)}) copy-start(f32[1,5,4,16,131]{4,3,2,1,0:T(8,128)} %get-tuple-element.37) | copy-start | bytes 503044
  321.6 58.8 %copy-start.30 = (f32[5,4,16,128]{3,2,1,0:T(8,128)S(1)}, f32[5,4,16,128]{3,2,1,0:T(8,128)}, u32[]{:S(2)}) copy-start(f32[5,4,16,128]{3,2,1,0:T(8,128)} %get-tuple-element.5) | copy-start | bytes 491524
  321.6 58.8 %copy-start.31 = (f32[5,4,16,128]{3,2,1,0:T(8,128)S(1)}, f32[5,4,16,128]{3,2,1,0:T(8,128)}, u32[]{:S(2)}) copy-start(f32[5,4,16,128]{3,2,1,0:T(8,128)} %get-tuple-element.6) | copy-start | bytes 491524
  321.6 58.8 %copy-start.32 = (f32[5,4,16,128]{3,2,1,0:T(8,128)S(1)}, f32[5,4,16,128]{3,2,1,0:T(8,128)}, u32[]{:S(2)}) copy-start(f32[5,4,16,128]{3,2,1,0:T(8,128)} %get-tuple-element.7) | copy-start | bytes 491524
  321.7 58.8 %copy-start.45 = (f32[1,4,16,128]{3,2,1,0:T(8,128)S(1)}, f32[1,4,16,128]{3,2,1,0:T(8,128)}, u32[]{:S(2)}) copy-start(f32[1,4,16,128]{3,2,1,0:T(8,128)} %param.13) | copy-start | bytes 98308
  (40 other events, 278.0 us)
Sparse Core Ops, SparseCore 0:
  10.4 73.6 all-gather.5
  90.6 66.3 all-gather.7
  163.6 66.3 all-gather.9
  236.6 66.3 all-gather.11
  309.6 66.3 all-gather.13
where the time goes:
time: 389 us; the launch traced here: 388 us
  waiting for transfers between devices  259 us (67%)
  other arithmetic  49.1 us (13%)
  starting transfers between devices  33.5 us (9%)
  matrix products  22.8 us (6%)
  between operations  15.3 us (4%)
  local copies, waits for them, and re-layouts  7.91 us (2%)
    all_gather x5, waiting for transfers between devices, on_device(): shard_rows = lax.all_gather(section_state, 'inst', axis=0, tiled=True)  258 us
    mul x16, other arithmetic, face_terms(): second_flux = cut(second_pad, 0, length + 3) * jumps  24.6 us
    dot_general x5, matrix products, on_device(): jnp.einsum('jk,jvxyz->kvxyz', table_rows, shard_rows, precision=lax.Preci...  22.8 us
    ppermute x6, starting transfers between devices, padded_2(): after = lax.ppermute(initial, axis, down)  17.4 us
    ppermute x6, starting transfers between devices, padded_2(): before = lax.ppermute(last, axis, up)  15.9 us
    sub x5, other arithmetic, on_device(): section_state = adjoint - section_coef * time_step[:, None] * residual  7.79 us
  transfers between devices with their start and end apart: 17, of which 5 were waited for; matrix products, arithmetic and copies ran while one was open for 12% of the time, Pallas kernels for 0%

commit v1 on v0

v1 whole, which is shorter than its diff:
```python
import math

import jax
import jax.numpy as jnp
from jax import lax
from jax.experimental import pallas as pl
from jax.experimental.pallas import tpu as pltpu
from jax.sharding import PartitionSpec as P

INSTANCES = 16
VARS = 5
LAYERS = 4
NY = 16
NZ = 128
DEVICES = 32
F32 = jnp.float32
FACTORS = (0.25, 1.0 / 6.0, 0.375, 0.5, 1.0)

SLOPE = [0.0] * INSTANCES
CURVE = [INSTANCES * INSTANCES / 12.0 + 1.0 / 6.0] * INSTANCES
for offset in range(1, INSTANCES):
    parity = 1.0 if offset % 2 == 0 else -1.0
    angle = math.pi * offset / INSTANCES
    SLOPE[offset] = 0.5 * parity * math.cos(angle) / math.sin(angle)
    CURVE[offset] = 0.5 * parity / math.sin(angle) ** 2

PAIRS_EVEN = [(i, i + 1) for i in range(0, DEVICES, 2)] + [(i + 1, i) for i in range(0, DEVICES, 2)]
PAIRS_ODD = [(i, i + 1) for i in range(1, DEVICES - 1, 2)] + [
    (i + 1, i) for i in range(1, DEVICES - 1, 2)
]

FIELD = (VARS, LAYERS, NY, NZ)
HALO = (VARS, 2, NY, NZ)
VMEM = pl.BlockSpec(memory_space=pltpu.VMEM)
SMEM = pl.BlockSpec(memory_space=pltpu.SMEM)


def shape(*dims):
    return jax.ShapeDtypeStruct(dims, F32)


def call(kernel, outs, args, specs=None, scratch=(), flops=0):
    size = sum(math.prod(x.shape) for x in list(args) + list(outs)) * 4
    return pl.pallas_call(
        kernel,
        out_shape=outs,
        in_specs=specs or [VMEM] * len(args),
        out_specs=[VMEM] * len(outs),
        scratch_shapes=list(scratch),
        compiler_params=pltpu.CompilerParams(vmem_limit_bytes=24 * 1024 * 1024),
        cost_estimate=pl.CostEstimate(flops=flops, bytes_accessed=size, transcendentals=0),
    )(*args)


def even_device():
    return lax.rem(lax.axis_index("cells"), 2) == 0


def write_halos(read, even_ref, odd_ref, rows):
    first = jnp.where(even_device(), 2, 0)
    for row in range(rows):
        for layer in range(2):
            even_ref[row, layer] = read(row, first + layer)
            odd_ref[row, layer] = read(row, 2 - first + layer)


def pack_kernel(adjoint, second, fourth, step, message, even_ref, odd_ref):
    for layer in range(LAYERS):
        for quarter in range(4):
            rows = slice(4 * quarter, 4 * quarter + 4)
            for slot in range(VARS + 1):
                source = step[layer] if slot == VARS else adjoint[slot, layer]
                half = 4 * (slot % 2)
                message[4 * layer + quarter, slot // 2, half : half + 4, :] = source[rows, :]

    def read(row, layer):
        if row < VARS:
            return adjoint[row, layer]
        return second[0, layer] if row == VARS else fourth[0, layer]

    write_halos(read, even_ref, odd_ref, VARS + 2)


def fill_padded(padded, coefs, own, own_second, own_fourth, even, odd, even_first, odd_first):
    after = jnp.where(even_device(), 6, 0)
    for layer in range(2):
        for var in range(VARS):
            padded[var, after + layer] = even[var, layer]
            padded[var, 6 - after + layer] = odd[var, layer]
        for kind in range(2):
            coefs[kind, after + layer] = even_first[VARS + kind, layer]
            coefs[kind, 6 - after + layer] = odd_first[VARS + kind, layer]
    for layer in range(LAYERS):
        for var in range(VARS):
            padded[var, 2 + layer] = own(var, layer)
        coefs[0, 2 + layer] = own_second[0, layer]
        coefs[1, 2 + layer] = own_fourth[0, layer]


def spatial(padded, coefs, second, fourth, jacobian, finish):
    row = lax.broadcasted_iota(jnp.int32, (NY, NZ), 0)
    lane = lax.broadcasted_iota(jnp.int32, (NY, NZ), 1)

    def ahead(x, axis):
        place, count = (row, NY) if axis == 0 else (lane, NZ)
        return jnp.where(place == count - 1, 0.0, pltpu.roll(x, count - 1, axis))

    def behind(x, axis, edge):
        place = row if axis == 0 else lane
        return jnp.where(place == 0, edge, pltpu.roll(x, 1, axis))

    def layer_step(layer, carry):
        central = []
        damped = []
        for var in range(VARS):
            v = [padded[var, layer + i] for i in range(5)]
            jump = [v[i + 1] - v[i] for i in range(4)]
            fourth_flux = [coefs[1, layer + i] * jump[i] for i in range(4)]
            second_below = coefs[0, layer + 1] * jump[1]
            second_above = coefs[0, layer + 2] * jump[2]
            term = (fourth_flux[3] - fourth_flux[0]) + 3.0 * (fourth_flux[1] - fourth_flux[2])
            total = term + (second_below - second_above)
            parts = [v[1] - v[3]]
            mid = v[2]
            for axis in range(2):
                upper = ahead(mid, axis)
                lower = behind(mid, axis, 0.0)
                parts.append(lower - upper)
                step_up = upper - mid
                flux = fourth[1 + axis, layer] * step_up
                face = (
                    ahead(flux, axis)
                    - 2.0 * flux
                    + behind(flux, axis, 0.0)
                    - second[1 + axis, layer] * step_up
                )
                total = total + (face - behind(face, axis, flux))
            central.append(parts)
            damped.append(total)
        for var in range(VARS):
            acc = None
            for direction in range(3):
                for a in range(VARS):
                    term = jacobian[direction, a, var, layer] * central[a][direction]
                    acc = term if acc is None else acc + term
            finish(var, layer, damped[var] + 0.5 * acc)
        return carry

    lax.fori_loop(0, LAYERS, layer_step, 0)


def own_slab(ref):
    return lambda var, layer: ref[var, layer]


def local_kernel(adjoint, second, fourth, jacobian, even, odd, out, padded, coefs):
    fill_padded(padded, coefs, own_slab(adjoint), second, fourth, even, odd, even, odd)

    def finish(var, layer, value):
        out[var, layer] = value

    spatial(padded, coefs, second, fourth, jacobian, finish)


def first_kernel(factor, adjoint, gradient, step, local, back, state, even_ref, odd_ref):
    for layer in range(LAYERS):
        for quarter in range(4):
            rows = slice(4 * quarter, 4 * quarter + 4)
            for var in range(VARS):
                half = 4 * (var % 2)
                state[var, layer, rows, :] = back[
                    4 * layer + quarter, var // 2, half : half + 4, :
                ]
    for layer in range(LAYERS):
        for var in range(VARS):
            residual = local[var, layer] + state[var, layer] + gradient[var, layer]
            state[var, layer] = adjoint[var, layer] - (factor * step[layer]) * residual
    write_halos(lambda row, layer: state[row, layer], even_ref, odd_ref, VARS)


def send_kernel(
    factor,
    adjoint,
    gradient,
    step,
    second,
    fourth,
    jacobian,
    even_first,
    odd_first,
    state,
    even,
    odd,
    message,
    padded,
    coefs,
):
    fill_padded(
        padded, coefs, own_slab(state), second, fourth, even, odd, even_first, odd_first
    )

    def finish(var, layer, value):
        residual = value + gradient[var, layer]
        q = adjoint[var, layer] - (factor * step[layer]) * residual
        u = padded[var, 2 + layer]
        for quarter in range(4):
            rows = slice(4 * quarter, 4 * quarter + 4)
            message[4 * layer + quarter, var, 0:4, :] = u[rows, :]
            message[4 * layer + quarter, var, 4:8, :] = q[rows, :]

    spatial(padded, coefs, second, fourth, jacobian, finish)


def unpack_kernel(back, state, coupled, even_ref, odd_ref):
    for layer in range(LAYERS):
        for quarter in range(4):
            rows = slice(4 * quarter, 4 * quarter + 4)
            for var in range(VARS):
                coupled[var, layer, rows, :] = back[4 * layer + quarter, var, 0:4, :]
                state[var, layer, rows, :] = back[4 * layer + quarter, var, 4:8, :]
    write_halos(lambda row, layer: state[row, layer], even_ref, odd_ref, VARS)


def update_kernel(
    factor,
    last,
    adjoint,
    gradient,
    step,
    second,
    fourth,
    jacobian,
    even_first,
    odd_first,
    state,
    coupled,
    even,
    odd,
    out,
    *rest,
):
    padded, coefs = rest[-2:]
    fill_padded(
        padded, coefs, own_slab(state), second, fourth, even, odd, even_first, odd_first
    )

    def finish(var, layer, value):
        residual = value + coupled[var, layer] + gradient[var, layer]
        out[var, layer] = adjoint[var, layer] - (factor * step[layer]) * residual

    spatial(padded, coefs, second, fourth, jacobian, finish)
    if not last:
        write_halos(lambda row, layer: out[row, layer], rest[0], rest[1], VARS)


def couple(values, frequency, damping):
    weights = [frequency * SLOPE[m] + damping * CURVE[m] for m in range(INSTANCES)]
    out = []
    for k in range(INSTANCES):
        acc = None
        for j in range(INSTANCES):
            term = weights[(j - k) % INSTANCES] * values[j]
            acc = term if acc is None else acc + term
        out.append(acc)
    return out


def couple_kernel(frequency, damping, received, out):
    def tile(index, carry):
        values = [received[j, index] for j in range(INSTANCES)]
        for k, value in enumerate(couple(values, frequency[0], damping[0])):
            out[k, index] = value
        return carry

    lax.fori_loop(0, received.shape[1], tile, 0)


def middle_kernel(factor, frequency, damping, steps, received, out):
    low = lax.broadcasted_iota(jnp.int32, (8, NZ), 0) < 4

    def tile(index, carry):
        values = [received[j, index] for j in range(INSTANCES)]
        first = couple(values, frequency[0], damping[0])
        moved = [
            values[k] - (factor * steps[k, 2]) * pltpu.roll(first[k], 4, 0)
            for k in range(INSTANCES)
        ]
        for k, value in enumerate(couple(moved, frequency[0], damping[0])):
            out[k, index] = jnp.where(low, pltpu.roll(value, 4, 0), moved[k])
        return carry

    lax.fori_loop(0, VARS, tile, 0)


def exchange(even, odd):
    return lax.ppermute(even, "cells", PAIRS_EVEN), lax.ppermute(odd, "cells", PAIRS_ODD)


def across(message):
    return lax.all_to_all(message, "inst", 0, 0, tiled=True)


def on_device(
    adjoint, objective_gradient, jacobian, second_coef, fourth_coef, time_step, frequency, damping
):
    adjoint = adjoint[0]
    gradient = objective_gradient[0]
    jacobian = jacobian[0]
    second = second_coef[0]
    fourth = fourth_coef[0]
    step = time_step[0]
    scratch = (pltpu.VMEM((VARS, 8, NY, NZ), F32), pltpu.VMEM((2, 8, NY, NZ), F32))
    halos = [shape(*HALO), shape(*HALO)]
    scalars = [SMEM, SMEM]
    work = 3 * 10**6

    message, even, odd = call(
        pack_kernel,
        [shape(INSTANCES, 3, 8, NZ), shape(VARS + 2, 2, NY, NZ), shape(VARS + 2, 2, NY, NZ)],
        [adjoint, second, fourth, step],
    )
    steps = across(message)
    even_first, odd_first = exchange(even, odd)
    (local,) = call(
        local_kernel,
        [shape(*FIELD)],
        [adjoint, second, fourth, jacobian, even_first, odd_first],
        scratch=scratch,
        flops=work,
    )
    (coupled,) = call(
        couple_kernel,
        [shape(INSTANCES, 3, 8, NZ)],
        [frequency, damping, steps],
        scalars + [VMEM],
        flops=work,
    )
    state, even, odd = call(
        lambda *refs: first_kernel(FACTORS[0], *refs),
        [shape(*FIELD)] + halos,
        [adjoint, gradient, step, local, across(coupled)],
    )
    fixed = [adjoint, gradient, step, second, fourth, jacobian, even_first, odd_first]
    for section in (1, 3):
        even, odd = exchange(even, odd)
        (message,) = call(
            lambda *refs: send_kernel(FACTORS[section], *refs),
            [shape(INSTANCES, VARS, 8, NZ)],
            fixed + [state, even, odd],
            scratch=scratch,
            flops=work,
        )
        (message,) = call(
            lambda *refs: middle_kernel(FACTORS[section], *refs),
            [shape(INSTANCES, VARS, 8, NZ)],
            [frequency, damping, steps, across(message)],
            scalars + [VMEM, VMEM],
            flops=work,
        )
        state, coupled, even, odd = call(
            unpack_kernel, [shape(*FIELD), shape(*FIELD)] + halos, [across(message)]
        )
        even, odd = exchange(even, odd)
        last = section == 3
        outs = call(
            lambda *refs: update_kernel(FACTORS[section + 1], last, *refs),
            [shape(*FIELD)] + ([] if last else halos),
            fixed + [state, coupled, even, odd],
            scratch=scratch,
            flops=work,
        )
        if last:
            return outs[0][None]
        state, even, odd = outs


def solution(mesh):
    placed = (
        P("inst", None, "cells", None, None),
        P("inst", None, "cells", None, None),
        P("inst", None, None, None, "cells", None, None),
        P("inst", None, "cells", None, None),
        P("inst", None, "cells", None, None),
        P("inst", "cells", None, None),
        P(),
        P(),
    )
    return jax.shard_map(
        on_device,
        mesh=mesh,
        in_specs=placed,
        out_specs=P("inst", None, "cells", None, None),
        check_vma=False,
    )
```

time: 389 us -> 170 us (0.44)
  the two profiles are of different devices: /device:TPU:1 before, /device:TPU:201 now
where the time goes in v1:
time: 170 us; the launch traced here: 169 us
  blocking collectives  69.7 us (41%)
  starting transfers between devices  53.8 us (32%)
  waiting for transfers between devices  24.6 us (14%)
  Pallas kernels  10.2 us (6%)
  local copies, waits for them, and re-layouts  9.45 us (6%)
    all_to_all x4, blocking collectives, across(): return lax.all_to_all(message, 'inst', 0, 0, tiled=True)  69.7 us
    ppermute x5, starting transfers between devices, exchange(): lax.ppermute(odd, 'cells', PAIRS_ODD)  27.2 us
    ppermute x5, waiting for transfers between devices, exchange(): lax.ppermute(odd, 'cells', PAIRS_ODD)  16.4 us
    all_to_all x2, starting transfers between devices, across(): return lax.all_to_all(message, 'inst', 0, 0, tiled=True)  13.8 us
    ppermute x5, starting transfers between devices, exchange(): lax.ppermute(even, 'cells', PAIRS_EVEN)  12.9 us
    pallas_call x12, Pallas kernels, call(): pl.pallas_call(kernel, out_shape=outs, in_specs=specs or [VMEM] * len(arg...  10.2 us
    unnamed x32, local copies, waits for them, and re-layouts  9.45 us
    all_to_all x2, waiting for transfers between devices, across(): return lax.all_to_all(message, 'inst', 0, 0, tiled=True)  8.21 us
  transfers between devices with their start and end apart: 12, of which 6 were waited for; matrix products, arithmetic and copies ran while one was open for 0% of the time, Pallas kernels for 1%

profile of v1, /device:TPU:201, one launch (start us, length us, event | category | flops | bytes accessed | tf_op | source)
XLA Modules:
  0.0 169.3 jit_solution(11948593872842130307)
XLA Ops:
  4.2 8.5 %all-to-all-start = ((f32[16,3,8,128]{3,2,1,0:T(8,128)}), f32[16,3,8,128]{3,2,1,0:T(8,128)S(1)}, u32[]{:S(2)}, u32[]{:S(2)}) async-start(f32[16,3,8,128]{3,2,1,0:T(8,128)} %get-tuple-element.24), calls=%async_computation | async-start | bytes 393216 | tf_op jit(solution)/shard_map/all_to_all | solution.py:300
  14.0 8.2 %all-to-all-done.received.refs_2_ = f32[16,3,8,128]{3,2,1,0:T(8,128)S(1)} async-done(((f32[16,3,8,128]{3,2,1,0:T(8,128)}), f32[16,3,8,128]{3,2,1,0:T(8,128)S(1)}, u32[]{:S(2)}, u32[]{:S(2)}) %all-to-all-start) | async-done | bytes 196640 | tf_op jit(solution)/shard_map/all_to_all | solution.py:300
  23.1 5.3 %all-to-all-start.1 = ((f32[16,3,8,128]{3,2,1,0:T(8,128)}), f32[16,3,8,128]{3,2,1,0:T(8,128)}, u32[]{:S(2)}, u32[]{:S(2)}) async-start(f32[16,3,8,128]{3,2,1,0:T(8,128)} %shard_map.84), calls=%async_computation.1 | async-start | bytes 393216 | tf_op jit(solution)/shard_map/all_to_all | solution.py:300
  28.4 3.8 %collective-permute-start = (f32[7,2,16,128]{3,2,1,0:T(8,128)S(1)}, f32[7,2,16,128]{3,2,1,0:T(8,128)S(1)}, u32[]{:S(2)}, u32[]{:S(2)}) collective-permute-start(f32[7,2,16,128]{3,2,1,0:T(8,128)S(1)} %get-tuple-element.22), channel_id=1, source_target_pairs={{0,1},{2,3},{4,5},{6,7},{8,9},{10,11},{12,13},{14,15},{16,17},{18,... | collective-permute-start | bytes 344072 | tf_op jit(solution)/shard_map/ppermute | solution.py:296
  32.2 5.7 %collective-permute-start.1 = (f32[7,2,16,128]{3,2,1,0:T(8,128)S(1)}, f32[7,2,16,128]{3,2,1,0:T(8,128)S(1)}, u32[]{:S(2)}, u32[]{:S(2)}) collective-permute-start(f32[7,2,16,128]{3,2,1,0:T(8,128)S(1)} %get-tuple-element.23), channel_id=1, source_target_pairs={{1,2},{3,4},{5,6},{7,8},{9,10},{11,12},{13,14},{15,16},{17,18},{19... | collective-permute-start | bytes 344072 | tf_op jit(solution)/shard_map/ppermute | solution.py:296
  38.0 4.0 %collective-permute-done.1.odd.refs_7_ = f32[7,2,16,128]{3,2,1,0:T(8,128)S(1)} collective-permute-done((f32[7,2,16,128]{3,2,1,0:T(8,128)S(1)}, f32[7,2,16,128]{3,2,1,0:T(8,128)S(1)}, u32[]{:S(2)}, u32[]{:S(2)}) %collective-permute-start.1) | collective-permute-done | bytes 114720 | tf_op jit(solution)/shard_map/ppermute | solution.py:296
  42.0 1.7 copy-done
  50.0 1.9 %collective-permute-start.2 = (f32[5,2,16,128]{3,2,1,0:T(8,128)S(1)}, f32[5,2,16,128]{3,2,1,0:T(8,128)S(1)}, u32[]{:S(2)}, u32[]{:S(2)}) collective-permute-start(f32[5,2,16,128]{3,2,1,0:T(8,128)S(1)} %get-tuple-element.26), channel_id=1, source_target_pairs={{0,1},{2,3},{4,5},{6,7},{8,9},{10,11},{12,13},{14,15},{16,17},{18,... | collective-permute-start | bytes 245768 | tf_op jit(solution)/shard_map/ppermute | solution.py:296
  52.0 4.2 %collective-permute-start.3 = (f32[5,2,16,128]{3,2,1,0:T(8,128)S(1)}, f32[5,2,16,128]{3,2,1,0:T(8,128)S(1)}, u32[]{:S(2)}, u32[]{:S(2)}) collective-permute-start(f32[5,2,16,128]{3,2,1,0:T(8,128)S(1)} %get-tuple-element.27), channel_id=1, source_target_pairs={{1,2},{3,4},{5,6},{7,8},{9,10},{11,12},{13,14},{15,16},{17,18},{19... | collective-permute-start | bytes 245768 | tf_op jit(solution)/shard_map/ppermute | solution.py:296
  56.1 4.0 %collective-permute-done.3.refs_10_ = f32[5,2,16,128]{3,2,1,0:T(8,128)S(1)} collective-permute-done((f32[5,2,16,128]{3,2,1,0:T(8,128)S(1)}, f32[5,2,16,128]{3,2,1,0:T(8,128)S(1)}, u32[]{:S(2)}, u32[]{:S(2)}) %collective-permute-start.3) | collective-permute-done | bytes 81952 | tf_op jit(solution)/shard_map/ppermute | solution.py:296
  61.2 20.2 %all_to_all.30.refs_3_ = f32[16,5,8,128]{3,2,1,0:T(8,128)S(1)} all-to-all(f32[16,5,8,128]{3,2,1,0:T(8,128)S(1)} %shard_map.86), channel_id=1, replica_groups=mesh['inst'=16,'cells'=32] {'inst'}, dimensions={0} | all-to-all | bytes 655360 | tf_op jit(solution)/shard_map/all_to_all | solution.py:300
  82.2 17.2 %all_to_all.31.back = f32[16,5,8,128]{3,2,1,0:T(8,128)S(1)} all-to-all(f32[16,5,8,128]{3,2,1,0:T(8,128)S(1)} %shard_map.87), channel_id=1, replica_groups=mesh['inst'=16,'cells'=32] {'inst'}, dimensions={0} | all-to-all | bytes 655360 | tf_op jit(solution)/shard_map/all_to_all | solution.py:300
  99.5 2.5 %collective-permute-start.4 = (f32[5,2,16,128]{3,2,1,0:T(8,128)S(1)}, f32[5,2,16,128]{3,2,1,0:T(8,128)S(1)}, u32[]{:S(2)}, u32[]{:S(2)}) collective-permute-start(f32[5,2,16,128]{3,2,1,0:T(8,128)S(1)} %get-tuple-element.30), channel_id=1, source_target_pairs={{0,1},{2,3},{4,5},{6,7},{8,9},{10,11},{12,13},{14,15},{16,17},{18,... | collective-permute-start | bytes 245768 | tf_op jit(solution)/shard_map/ppermute | solution.py:296
  102.1 6.4 %collective-permute-start.5 = (f32[5,2,16,128]{3,2,1,0:T(8,128)S(1)}, f32[5,2,16,128]{3,2,1,0:T(8,128)S(1)}, u32[]{:S(2)}, u32[]{:S(2)}) collective-permute-start(f32[5,2,16,128]{3,2,1,0:T(8,128)S(1)} %get-tuple-element.31), channel_id=1, source_target_pairs={{1,2},{3,4},{5,6},{7,8},{9,10},{11,12},{13,14},{15,16},{17,18},{19... | collective-permute-start | bytes 245768 | tf_op jit(solution)/shard_map/ppermute | solution.py:296
  108.5 2.8 %collective-permute-done.5.refs_11_ = f32[5,2,16,128]{3,2,1,0:T(8,128)S(1)} collective-permute-done((f32[5,2,16,128]{3,2,1,0:T(8,128)S(1)}, f32[5,2,16,128]{3,2,1,0:T(8,128)S(1)}, u32[]{:S(2)}, u32[]{:S(2)}) %collective-permute-start.5) | collective-permute-done | bytes 81952 | tf_op jit(solution)/shard_map/ppermute | solution.py:296
  112.3 1.9 %collective-permute-start.6 = (f32[5,2,16,128]{3,2,1,0:T(8,128)S(1)}, f32[5,2,16,128]{3,2,1,0:T(8,128)S(1)}, u32[]{:S(2)}, u32[]{:S(2)}) collective-permute-start(f32[5,2,16,128]{3,2,1,0:T(8,128)S(1)} %get-tuple-element.33), channel_id=1, source_target_pairs={{0,1},{2,3},{4,5},{6,7},{8,9},{10,11},{12,13},{14,15},{16,17},{18,... | collective-permute-start | bytes 245768 | tf_op jit(solution)/shard_map/ppermute | solution.py:296
  114.3 5.1 %collective-permute-start.7 = (f32[5,2,16,128]{3,2,1,0:T(8,128)S(1)}, f32[5,2,16,128]{3,2,1,0:T(8,128)S(1)}, u32[]{:S(2)}, u32[]{:S(2)}) collective-permute-start(f32[5,2,16,128]{3,2,1,0:T(8,128)S(1)} %get-tuple-element.34), channel_id=1, source_target_pairs={{1,2},{3,4},{5,6},{7,8},{9,10},{11,12},{13,14},{15,16},{17,18},{19... | collective-permute-start | bytes 245768 | tf_op jit(solution)/shard_map/ppermute | solution.py:296
  119.4 2.8 %collective-permute-done.7.refs_10_ = f32[5,2,16,128]{3,2,1,0:T(8,128)S(1)} collective-permute-done((f32[5,2,16,128]{3,2,1,0:T(8,128)S(1)}, f32[5,2,16,128]{3,2,1,0:T(8,128)S(1)}, u32[]{:S(2)}, u32[]{:S(2)}) %collective-permute-start.7) | collective-permute-done | bytes 81952 | tf_op jit(solution)/shard_map/ppermute | solution.py:296
  123.2 15.2 %all_to_all.32.refs_3_ = f32[16,5,8,128]{3,2,1,0:T(8,128)S(1)} all-to-all(f32[16,5,8,128]{3,2,1,0:T(8,128)S(1)} %shard_map.90), channel_id=1, replica_groups=mesh['inst'=16,'cells'=32] {'inst'}, dimensions={0} | all-to-all | bytes 655360 | tf_op jit(solution)/shard_map/all_to_all | solution.py:300
  139.2 17.0 %all_to_all.33.back = f32[16,5,8,128]{3,2,1,0:T(8,128)S(1)} all-to-all(f32[16,5,8,128]{3,2,1,0:T(8,128)S(1)} %shard_map.91), channel_id=1, replica_groups=mesh['inst'=16,'cells'=32] {'inst'}, dimensions={0} | all-to-all | bytes 655360 | tf_op jit(solution)/shard_map/all_to_all | solution.py:300
  156.3 2.7 %collective-permute-start.8 = (f32[5,2,16,128]{3,2,1,0:T(8,128)S(1)}, f32[5,2,16,128]{3,2,1,0:T(8,128)S(1)}, u32[]{:S(2)}, u32[]{:S(2)}) collective-permute-start(f32[5,2,16,128]{3,2,1,0:T(8,128)S(1)} %get-tuple-element.37), channel_id=1, source_target_pairs={{0,1},{2,3},{4,5},{6,7},{8,9},{10,11},{12,13},{14,15},{16,17},{18,... | collective-permute-start | bytes 245768 | tf_op jit(solution)/shard_map/ppermute | solution.py:296
  159.0 5.8 %collective-permute-start.9 = (f32[5,2,16,128]{3,2,1,0:T(8,128)S(1)}, f32[5,2,16,128]{3,2,1,0:T(8,128)S(1)}, u32[]{:S(2)}, u32[]{:S(2)}) collective-permute-start(f32[5,2,16,128]{3,2,1,0:T(8,128)S(1)} %get-tuple-element.38), channel_id=1, source_target_pairs={{1,2},{3,4},{5,6},{7,8},{9,10},{11,12},{13,14},{15,16},{17,18},{19... | collective-permute-start | bytes 245768 | tf_op jit(solution)/shard_map/ppermute | solution.py:296
  164.8 2.8 %collective-permute-done.9.refs_11_ = f32[5,2,16,128]{3,2,1,0:T(8,128)S(1)} collective-permute-done((f32[5,2,16,128]{3,2,1,0:T(8,128)S(1)}, f32[5,2,16,128]{3,2,1,0:T(8,128)S(1)}, u32[]{:S(2)}, u32[]{:S(2)}) %collective-permute-start.9) | collective-permute-done | bytes 81952 | tf_op jit(solution)/shard_map/ppermute | solution.py:296
  167.6 1.7 %shard_map.93 = f32[5,4,16,128]{3,2,1,0:T(8,128)} custom-call(f32[5,4,16,128]{3,2,1,0:T(8,128)S(1)} %bitcast.18, f32[5,4,16,128]{3,2,1,0:T(8,128)S(1)} %bitcast.23, f32[4,16,128]{2,1,0:T(8,128)S(1)} %bitcast.41, f32[3,4,16,128]{3,2,1,0:T(8,128)S(1)} %bitcast.29, f32[3,4,16,128]{3,2,1,0:T(8,128)S(1)} %bitcast.35, f32[3,5,5,4,16,128]{5,4,3,2,1,0:T(8,128)S(1)} %bitcast.11, ...), custom_call_target="tpu_custom_call" | custom-call | flops 3000000 | bytes 3899392 | tf_op jit(solution)/shard_map/pallas_call | solution.py:44
  (48 shorter events, 16.3 us)
Async XLA Ops:
  0.0 0.9 copy-start.2
  0.9 0.9 copy-start.6
  3.5 44.6 %copy-start.4 = (f32[1,5,4,16,128]{4,3,2,1,0:T(8,128)S(1)}, f32[1,5,4,16,128]{4,3,2,1,0:T(8,128)}, u32[]{:S(2)}) copy-start(f32[1,5,4,16,128]{4,3,2,1,0:T(8,128)} %param.8) | copy-start | bytes 491524
  3.5 44.6 %copy-start.5 = (f32[1,5,4,16,128]{4,3,2,1,0:T(8,128)S(1)}, f32[1,5,4,16,128]{4,3,2,1,0:T(8,128)}, u32[]{:S(2)}) copy-start(f32[1,5,4,16,128]{4,3,2,1,0:T(8,128)} %param.9) | copy-start | bytes 491524
  3.5 44.6 %copy-start.13 = (f32[1,4,16,128]{3,2,1,0:T(8,128)S(1)}, f32[1,4,16,128]{3,2,1,0:T(8,128)}, u32[]{:S(2)}) copy-start(f32[1,4,16,128]{3,2,1,0:T(8,128)} %param.13) | copy-start | bytes 98308
  4.2 18.1 %all-to-all-start = ((f32[16,3,8,128]{3,2,1,0:T(8,128)}), f32[16,3,8,128]{3,2,1,0:T(8,128)S(1)}, u32[]{:S(2)}, u32[]{:S(2)}) async-start(f32[16,3,8,128]{3,2,1,0:T(8,128)} %get-tuple-element.24), calls=%async_computation | async-start | bytes 393216 | tf_op jit(solution)/shard_map/all_to_all | solution.py:300
  12.7 47.5 %copy-start.8 = (f32[1,3,4,16,128]{4,3,2,1,0:T(8,128)S(1)}, f32[1,3,4,16,128]{4,3,2,1,0:T(8,128)}, u32[]{:S(2)}) copy-start(f32[1,3,4,16,128]{4,3,2,1,0:T(8,128)} %param.11) | copy-start | bytes 294916
  12.7 47.5 %copy-start.11 = (f32[1,3,4,16,128]{4,3,2,1,0:T(8,128)S(1)}, f32[1,3,4,16,128]{4,3,2,1,0:T(8,128)}, u32[]{:S(2)}) copy-start(f32[1,3,4,16,128]{4,3,2,1,0:T(8,128)} %param.12) | copy-start | bytes 294916
  23.1 24.9 %all-to-all-start.1 = ((f32[16,3,8,128]{3,2,1,0:T(8,128)}), f32[16,3,8,128]{3,2,1,0:T(8,128)}, u32[]{:S(2)}, u32[]{:S(2)}) async-start(f32[16,3,8,128]{3,2,1,0:T(8,128)} %shard_map.84), calls=%async_computation.1 | async-start | bytes 393216 | tf_op jit(solution)/shard_map/all_to_all | solution.py:300
  28.4 9.5 %collective-permute-start = (f32[7,2,16,128]{3,2,1,0:T(8,128)S(1)}, f32[7,2,16,128]{3,2,1,0:T(8,128)S(1)}, u32[]{:S(2)}, u32[]{:S(2)}) collective-permute-start(f32[7,2,16,128]{3,2,1,0:T(8,128)S(1)} %get-tuple-element.22), channel_id=1, source_target_pairs={{0,1},{2,3},{4,5},{6,7},{8,9},{10,11},{12,13},{14,15},{16,17},{18,... | collective-permute-start | bytes 344072 | tf_op jit(solution)/shard_map/ppermute | solution.py:296
  32.2 9.8 %collective-permute-start.1 = (f32[7,2,16,128]{3,2,1,0:T(8,128)S(1)}, f32[7,2,16,128]{3,2,1,0:T(8,128)S(1)}, u32[]{:S(2)}, u32[]{:S(2)}) collective-permute-start(f32[7,2,16,128]{3,2,1,0:T(8,128)S(1)} %get-tuple-element.23), channel_id=1, source_target_pairs={{1,2},{3,4},{5,6},{7,8},{9,10},{11,12},{13,14},{15,16},{17,18},{19... | collective-permute-start | bytes 344072 | tf_op jit(solution)/shard_map/ppermute | solution.py:296
  42.0 1.7 %copy-start = (f32[1,3,5,5,4,16,128]{6,5,4,3,2,1,0:T(8,128)S(1)}, f32[1,3,5,5,4,16,128]{6,5,4,3,2,1,0:T(8,128)}, u32[]{:S(2)}) copy-start(f32[1,3,5,5,4,16,128]{6,5,4,3,2,1,0:T(8,128)} %param.10) | copy-start | bytes 7372804
  43.7 0.9 copy-start.3
  44.6 0.9 copy-start.7
  46.4 13.7 %copy-start.1 = (f32[1,3,5,5,4,16,128]{6,5,4,3,2,1,0:T(8,128)S(1)}, f32[1,3,5,5,4,16,128]{6,5,4,3,2,1,0:T(8,128)}, u32[]{:S(2)}) copy-start(f32[1,3,5,5,4,16,128]{6,5,4,3,2,1,0:T(8,128)} %param.10) | copy-start | bytes 7372804
  48.1 0.9 copy-start.15
  50.0 6.1 %collective-permute-start.2 = (f32[5,2,16,128]{3,2,1,0:T(8,128)S(1)}, f32[5,2,16,128]{3,2,1,0:T(8,128)S(1)}, u32[]{:S(2)}, u32[]{:S(2)}) collective-permute-start(f32[5,2,16,128]{3,2,1,0:T(8,128)S(1)} %get-tuple-element.26), channel_id=1, source_target_pairs={{0,1},{2,3},{4,5},{6,7},{8,9},{10,11},{12,13},{14,15},{16,17},{18,... | collective-permute-start | bytes 245768 | tf_op jit(solution)/shard_map/ppermute | solution.py:296
  52.0 8.2 %collective-permute-start.3 = (f32[5,2,16,128]{3,2,1,0:T(8,128)S(1)}, f32[5,2,16,128]{3,2,1,0:T(8,128)S(1)}, u32[]{:S(2)}, u32[]{:S(2)}) collective-permute-start(f32[5,2,16,128]{3,2,1,0:T(8,128)S(1)} %get-tuple-element.27), channel_id=1, source_target_pairs={{1,2},{3,4},{5,6},{7,8},{9,10},{11,12},{13,14},{15,16},{17,18},{19... | collective-permute-start | bytes 245768 | tf_op jit(solution)/shard_map/ppermute | solution.py:296
  99.5 9.0 %collective-permute-start.4 = (f32[5,2,16,128]{3,2,1,0:T(8,128)S(1)}, f32[5,2,16,128]{3,2,1,0:T(8,128)S(1)}, u32[]{:S(2)}, u32[]{:S(2)}) collective-permute-start(f32[5,2,16,128]{3,2,1,0:T(8,128)S(1)} %get-tuple-element.30), channel_id=1, source_target_pairs={{0,1},{2,3},{4,5},{6,7},{8,9},{10,11},{12,13},{14,15},{16,17},{18,... | collective-permute-start | bytes 245768 | tf_op jit(solution)/shard_map/ppermute | solution.py:296
  102.1 9.2 %collective-permute-start.5 = (f32[5,2,16,128]{3,2,1,0:T(8,128)S(1)}, f32[5,2,16,128]{3,2,1,0:T(8,128)S(1)}, u32[]{:S(2)}, u32[]{:S(2)}) collective-permute-start(f32[5,2,16,128]{3,2,1,0:T(8,128)S(1)} %get-tuple-element.31), channel_id=1, source_target_pairs={{1,2},{3,4},{5,6},{7,8},{9,10},{11,12},{13,14},{15,16},{17,18},{19... | collective-permute-start | bytes 245768 | tf_op jit(solution)/shard_map/ppermute | solution.py:296
  112.3 7.0 %collective-permute-start.6 = (f32[5,2,16,128]{3,2,1,0:T(8,128)S(1)}, f32[5,2,16,128]{3,2,1,0:T(8,128)S(1)}, u32[]{:S(2)}, u32[]{:S(2)}) collective-permute-start(f32[5,2,16,128]{3,2,1,0:T(8,128)S(1)} %get-tuple-element.33), channel_id=1, source_target_pairs={{0,1},{2,3},{4,5},{6,7},{8,9},{10,11},{12,13},{14,15},{16,17},{18,... | collective-permute-start | bytes 245768 | tf_op jit(solution)/shard_map/ppermute | solution.py:296
  114.3 7.9 %collective-permute-start.7 = (f32[5,2,16,128]{3,2,1,0:T(8,128)S(1)}, f32[5,2,16,128]{3,2,1,0:T(8,128)S(1)}, u32[]{:S(2)}, u32[]{:S(2)}) collective-permute-start(f32[5,2,16,128]{3,2,1,0:T(8,128)S(1)} %get-tuple-element.34), channel_id=1, source_target_pairs={{1,2},{3,4},{5,6},{7,8},{9,10},{11,12},{13,14},{15,16},{17,18},{19... | collective-permute-start | bytes 245768 | tf_op jit(solution)/shard_map/ppermute | solution.py:296
  156.3 8.5 %collective-permute-start.8 = (f32[5,2,16,128]{3,2,1,0:T(8,128)S(1)}, f32[5,2,16,128]{3,2,1,0:T(8,128)S(1)}, u32[]{:S(2)}, u32[]{:S(2)}) collective-permute-start(f32[5,2,16,128]{3,2,1,0:T(8,128)S(1)} %get-tuple-element.37), channel_id=1, source_target_pairs={{0,1},{2,3},{4,5},{6,7},{8,9},{10,11},{12,13},{14,15},{16,17},{18,... | collective-permute-start | bytes 245768 | tf_op jit(solution)/shard_map/ppermute | solution.py:296
  159.0 8.6 %collective-permute-start.9 = (f32[5,2,16,128]{3,2,1,0:T(8,128)S(1)}, f32[5,2,16,128]{3,2,1,0:T(8,128)S(1)}, u32[]{:S(2)}, u32[]{:S(2)}) collective-permute-start(f32[5,2,16,128]{3,2,1,0:T(8,128)S(1)} %get-tuple-element.38), channel_id=1, source_target_pairs={{1,2},{3,4},{5,6},{7,8},{9,10},{11,12},{13,14},{15,16},{17,18},{19... | collective-permute-start | bytes 245768 | tf_op jit(solution)/shard_map/ppermute | solution.py:296
  (4 other events, 3.2 us)

commit v2 on v1

--- a/solution.py
+++ b/solution.py
@@ -33,10 +33,24 @@
 HALO = (VARS, 2, NY, NZ)
 VMEM = pl.BlockSpec(memory_space=pltpu.VMEM)
 SMEM = pl.BlockSpec(memory_space=pltpu.SMEM)
+ANY = pl.BlockSpec(memory_space=pl.ANY)
+HBM = pl.BlockSpec(memory_space=pltpu.HBM)
 
 
 def shape(*dims):
     return jax.ShapeDtypeStruct(dims, F32)
+
+
+def kept(*dims):
+    return pltpu.VMEM(dims, F32)
+
+
+def in_hbm(array):
+    return pltpu.with_memory_space_constraint(array, pltpu.HBM)
+
+
+def in_vmem(array):
+    return pltpu.with_memory_space_constraint(array, pltpu.VMEM)
 
 
 def call(kernel, outs, args, specs=None, scratch=(), flops=0):
@@ -47,7 +61,7 @@
         in_specs=specs or [VMEM] * len(args),
         out_specs=[VMEM] * len(outs),
         scratch_shapes=list(scratch),
-        compiler_params=pltpu.CompilerParams(vmem_limit_bytes=24 * 1024 * 1024),
+        compiler_params=pltpu.CompilerParams(vmem_limit_bytes=8 * 1024 * 1024),
         cost_estimate=pl.CostEstimate(flops=flops, bytes_accessed=size, transcendentals=0),
     )(*args)
 
@@ -56,7 +70,7 @@
     return lax.rem(lax.axis_index("cells"), 2) == 0
 
 
-def write_halos(read, even_ref, odd_ref, rows):
+def write_halos(read, odd_ref, even_ref, rows):
     first = jnp.where(even_device(), 2, 0)
     for row in range(rows):
         for layer in range(2):
@@ -64,7 +78,26 @@
             odd_ref[row, layer] = read(row, 2 - first + layer)
 
 
-def pack_kernel(adjoint, second, fourth, step, message, even_ref, odd_ref):
+def load(sources, targets, sems):
+    copies = [
+        pltpu.make_async_copy(source, target, sems.at[i])
+        for i, (source, target) in enumerate(zip(sources, targets))
+    ]
+    for copy in copies:
+        copy.start()
+    for copy in copies:
+        copy.wait()
+
+
+def load_kernel(*refs):
+    half = len(refs) // 2
+    load(refs[:half], refs[half:-1], refs[-1])
+
+
+def pack_kernel(*refs):
+    message, odd_ref, even_ref = refs[4:7]
+    adjoint, second, fourth, step = refs[7:11]
+    load(refs[:4], refs[7:11], refs[11])
     for layer in range(LAYERS):
         for quarter in range(4):
             rows = slice(4 * quarter, 4 * quarter + 4)
@@ -78,10 +111,10 @@
             return adjoint[row, layer]
         return second[0, layer] if row == VARS else fourth[0, layer]
 
-    write_halos(read, even_ref, odd_ref, VARS + 2)
-
-
-def fill_padded(padded, coefs, own, own_second, own_fourth, even, odd, even_first, odd_first):
+    write_halos(read, odd_ref, even_ref, VARS + 2)
+
+
+def fill_padded(padded, coefs, own, own_second, own_fourth, odd, even, odd_first, even_first):
     after = jnp.where(even_device(), 6, 0)
     for layer in range(2):
         for var in range(VARS):
@@ -153,8 +186,9 @@
     return lambda var, layer: ref[var, layer]
 
 
-def local_kernel(adjoint, second, fourth, jacobian, even, odd, out, padded, coefs):
-    fill_padded(padded, coefs, own_slab(adjoint), second, fourth, even, odd, even, odd)
+def local_kernel(adjoint, second, fourth, jacobian, odd, even, out, token, padded, coefs):
+    token[...] = jnp.zeros_like(token)
+    fill_padded(padded, coefs, own_slab(adjoint), second, fourth, odd, even, odd, even)
 
     def finish(var, layer, value):
         out[var, layer] = value
@@ -162,7 +196,7 @@
     spatial(padded, coefs, second, fourth, jacobian, finish)
 
 
-def first_kernel(factor, adjoint, gradient, step, local, back, state, even_ref, odd_ref):
+def first_kernel(factor, adjoint, gradient, step, local, back, state, odd_ref, even_ref):
     for layer in range(LAYERS):
         for quarter in range(4):
             rows = slice(4 * quarter, 4 * quarter + 4)
@@ -175,7 +209,7 @@
         for var in range(VARS):
             residual = local[var, layer] + state[var, layer] + gradient[var, layer]
             state[var, layer] = adjoint[var, layer] - (factor * step[layer]) * residual
-    write_halos(lambda row, layer: state[row, layer], even_ref, odd_ref, VARS)
+    write_halos(lambda row, layer: state[row, layer], odd_ref, even_ref, VARS)
 
 
 def send_kernel(
@@ -186,17 +220,17 @@
     second,
     fourth,
     jacobian,
+    odd_first,
     even_first,
-    odd_first,
     state,
+    odd,
     even,
-    odd,
     message,
     padded,
     coefs,
 ):
     fill_padded(
-        padded, coefs, own_slab(state), second, fourth, even, odd, even_first, odd_first
+        padded, coefs, own_slab(state), second, fourth, odd, even, odd_first, even_first
     )
 
     def finish(var, layer, value):
@@ -211,14 +245,14 @@
     spatial(padded, coefs, second, fourth, jacobian, finish)
 
 
-def unpack_kernel(back, state, coupled, even_ref, odd_ref):
+def unpack_kernel(back, state, coupled, odd_ref, even_ref):
     for layer in range(LAYERS):
         for quarter in range(4):
             rows = slice(4 * quarter, 4 * quarter + 4)
             for var in range(VARS):
                 coupled[var, layer, rows, :] = back[4 * layer + quarter, var, 0:4, :]
                 state[var, layer, rows, :] = back[4 * layer + quarter, var, 4:8, :]
-    write_halos(lambda row, layer: state[row, layer], even_ref, odd_ref, VARS)
+    write_halos(lambda row, layer: state[row, layer], odd_ref, even_ref, VARS)
 
 
 def update_kernel(
@@ -230,18 +264,18 @@
     second,
     fourth,
     jacobian,
+    odd_first,
     even_first,
-    odd_first,
     state,
     coupled,
+    odd,
     even,
-    odd,
     out,
     *rest,
 ):
     padded, coefs = rest[-2:]
     fill_padded(
-        padded, coefs, own_slab(state), second, fourth, even, odd, even_first, odd_first
+        padded, coefs, own_slab(state), second, fourth, odd, even, odd_first, even_first
     )
 
     def finish(var, layer, value):
@@ -265,7 +299,9 @@
     return out
 
 
-def couple_kernel(frequency, damping, received, out):
+def couple_kernel(frequency, damping, received, *rest):
+    out = rest[-1]
+
     def tile(index, carry):
         values = [received[j, index] for j in range(INSTANCES)]
         for k, value in enumerate(couple(values, frequency[0], damping[0])):
@@ -292,8 +328,8 @@
     lax.fori_loop(0, VARS, tile, 0)
 
 
-def exchange(even, odd):
-    return lax.ppermute(even, "cells", PAIRS_EVEN), lax.ppermute(odd, "cells", PAIRS_ODD)
+def exchange(odd, even):
+    return lax.ppermute(odd, "cells", PAIRS_ODD), lax.ppermute(even, "cells", PAIRS_EVEN)
 
 
 def across(message):
@@ -314,39 +350,50 @@
     scalars = [SMEM, SMEM]
     work = 3 * 10**6
 
-    message, even, odd = call(
+    coef_shape = (3, LAYERS, NY, NZ)
+    message, odd, even, adjoint, second, fourth, step = call(
         pack_kernel,
-        [shape(INSTANCES, 3, 8, NZ), shape(VARS + 2, 2, NY, NZ), shape(VARS + 2, 2, NY, NZ)],
-        [adjoint, second, fourth, step],
+        [shape(INSTANCES, 3, 8, NZ), shape(VARS + 2, 2, NY, NZ), shape(VARS + 2, 2, NY, NZ)]
+        + [kept(*FIELD), kept(*coef_shape), kept(*coef_shape), kept(LAYERS, NY, NZ)],
+        [in_hbm(x) for x in (adjoint, second, fourth, step)],
+        [HBM] * 4,
+        scratch=(pltpu.SemaphoreType.DMA((4,)),),
     )
     steps = across(message)
-    even_first, odd_first = exchange(even, odd)
-    (local,) = call(
+    odd_first, even_first = exchange(odd, even)
+    gradient, jacobian = call(
+        load_kernel,
+        [kept(*FIELD), kept(*jacobian.shape)],
+        [in_hbm(gradient), in_hbm(jacobian)],
+        [HBM] * 2,
+        scratch=(pltpu.SemaphoreType.DMA((2,)),),
+    )
+    local, token = call(
         local_kernel,
-        [shape(*FIELD)],
-        [adjoint, second, fourth, jacobian, even_first, odd_first],
+        [shape(*FIELD), shape(8, NZ)],
+        [adjoint, second, fourth, jacobian, odd_first, even_first],
         scratch=scratch,
         flops=work,
     )
     (coupled,) = call(
         couple_kernel,
         [shape(INSTANCES, 3, 8, NZ)],
-        [frequency, damping, steps],
-        scalars + [VMEM],
+        [frequency, damping, steps, in_hbm(token)],
+        scalars + [VMEM, ANY],
         flops=work,
     )
-    state, even, odd = call(
+    state, odd, even = call(
         lambda *refs: first_kernel(FACTORS[0], *refs),
         [shape(*FIELD)] + halos,
         [adjoint, gradient, step, local, across(coupled)],
     )
-    fixed = [adjoint, gradient, step, second, fourth, jacobian, even_first, odd_first]
+    fixed = [adjoint, gradient, step, second, fourth, jacobian, odd_first, even_first]
     for section in (1, 3):
-        even, odd = exchange(even, odd)
+        odd, even = exchange(odd, even)
         (message,) = call(
             lambda *refs: send_kernel(FACTORS[section], *refs),
             [shape(INSTANCES, VARS, 8, NZ)],
-            fixed + [state, even, odd],
+            fixed + [state, odd, even],
             scratch=scratch,
             flops=work,
         )
@@ -357,21 +404,21 @@
             scalars + [VMEM, VMEM],
             flops=work,
         )
-        state, coupled, even, odd = call(
+        state, coupled, odd, even = call(
             unpack_kernel, [shape(*FIELD), shape(*FIELD)] + halos, [across(message)]
         )
-        even, odd = exchange(even, odd)
+        odd, even = exchange(odd, even)
         last = section == 3
         outs = call(
             lambda *refs: update_kernel(FACTORS[section + 1], last, *refs),
             [shape(*FIELD)] + ([] if last else halos),
-            fixed + [state, coupled, even, odd],
+            fixed + [state, coupled, odd, even],
             scratch=scratch,
             flops=work,
         )
         if last:
             return outs[0][None]
-        state, even, odd = outs
+        state, odd, even = outs
 
 
 def solution(mesh):

time: 170 us -> 151 us (0.89)
  waiting for transfers between devices: 24.6 us -> 5.32 us
  blocking collectives: 69.7 us -> 83 us
  local copies, waits for them, and re-layouts: 9.45 us -> 2.17 us
  starting transfers between devices: 53.8 us -> 47 us
    ppermute x5, waiting for transfers between devices: 16.4 us -> 2.28 us  [exchange(): lax.ppermute(odd, 'cells', PAIRS_ODD)]
    all_to_all x4 -> x5, blocking collectives: 69.7 us -> 83 us  [across(): return lax.all_to_all(message, 'inst', 0, 0, tiled=True)]
    all_to_all x2 -> x1, waiting for transfers between devices: 8.21 us -> 0.01 us  [across(): return lax.all_to_all(message, 'inst', 0, 0, tiled=True)]
    unnamed x32 -> x6, local copies, waits for them, and re-layouts: 9.45 us -> 2.17 us
    all_to_all x2 -> x1, starting transfers between devices: 13.8 us -> 8.5 us  [across(): return lax.all_to_all(message, 'inst', 0, 0, tiled=True)]
    ppermute x5, starting transfers between devices: 12.9 us -> 9.6 us  [exchange(): lax.ppermute(even, 'cells', PAIRS_EVEN)]
    ppermute x5, waiting for transfers between devices: 0.01 us -> 3.04 us  [exchange(): lax.ppermute(even, 'cells', PAIRS_EVEN)]
    ppermute x5, starting transfers between devices: 27.2 us -> 28.9 us  [exchange(): lax.ppermute(odd, 'cells', PAIRS_ODD)]
  transfers between devices with their start and end apart: 12 -> 11, of which waited for: 6 -> 9; matrix products, arithmetic and copies ran while one was open for 0% -> 0% of each run, Pallas kernels for 1% -> 2%
where the time goes in v2:
time: 151 us; the launch traced here: 150 us
  blocking collectives  83 us (55%)
  starting transfers between devices  47 us (31%)
  Pallas kernels  11.5 us (8%)
  waiting for transfers between devices  5.32 us (4%)
  local copies, waits for them, and re-layouts  2.17 us (1%)
    all_to_all x5, blocking collectives, across(): return lax.all_to_all(message, 'inst', 0, 0, tiled=True)  83 us
    ppermute x5, starting transfers between devices, exchange(): lax.ppermute(odd, 'cells', PAIRS_ODD)  28.9 us
    pallas_call x13, Pallas kernels, call(): pl.pallas_call(kernel, out_shape=outs, in_specs=specs or [VMEM] * len(arg...  11.5 us
    ppermute x5, starting transfers between devices, exchange(): lax.ppermute(even, 'cells', PAIRS_EVEN)  9.6 us
    all_to_all x1, starting transfers between devices, across(): return lax.all_to_all(message, 'inst', 0, 0, tiled=True)  8.5 us
    ppermute x5, waiting for transfers between devices, exchange(): lax.ppermute(even, 'cells', PAIRS_EVEN)  3.04 us
  transfers between devices with their start and end apart: 11, of which 9 were waited for; matrix products, arithmetic and copies ran while one was open for 0% of the time, Pallas kernels for 2%

profile of v2, /device:TPU:201, one launch (start us, length us, event | category | flops | bytes accessed | tf_op | source)
XLA Modules:
  0.0 150.5 jit_solution(3756867034286598766)
XLA Ops:
  0.0 1.8 %shard_map.82 = (f32[16,3,8,128]{3,2,1,0:T(8,128)}, f32[7,2,16,128]{3,2,1,0:T(8,128)}, f32[7,2,16,128]{3,2,1,0:T(8,128)S(1)}, f32[5,4,16,128]{3,2,1,0:T(8,128)S(...) custom-call(f32[5,4,16,128]{3,2,1,0:T(8,128)} %bitcast.9, ...), custom_call_target="tpu_custom_call" | custom-call | bytes 1212416 | tf_op jit(solution)/shard_map/pallas_call | solution.py:58
  1.8 8.5 %all-to-all-start = ((f32[16,3,8,128]{3,2,1,0:T(8,128)}), f32[16,3,8,128]{3,2,1,0:T(8,128)S(1)}, u32[]{:S(2)}, u32[]{:S(2)}) async-start(f32[16,3,8,128]{3,2,1,0:T(8,128)} %get-tuple-element.38), calls=%async_computation | async-start | bytes 393216 | tf_op jit(solution)/shard_map/all_to_all | solution.py:336
  10.3 6.8 %collective-permute-start = (f32[7,2,16,128]{3,2,1,0:T(8,128)}, f32[7,2,16,128]{3,2,1,0:T(8,128)S(1)}, u32[]{:S(2)}, u32[]{:S(2)}) collective-permute-start(f32[7,2,16,128]{3,2,1,0:T(8,128)} %get-tuple-element.36), channel_id=1, source_target_pairs={{1,2},{3,4},{5,6},{7,8},{9,10},{11,12},{13,14},{15,16},{17,18},{19... | collective-permute-start | bytes 344072 | tf_op jit(solution)/shard_map/ppermute | solution.py:332
  17.1 1.9 %collective-permute-start.1 = (f32[7,2,16,128]{3,2,1,0:T(8,128)S(1)}, f32[7,2,16,128]{3,2,1,0:T(8,128)S(1)}, u32[]{:S(2)}, u32[]{:S(2)}) collective-permute-start(f32[7,2,16,128]{3,2,1,0:T(8,128)S(1)} %get-tuple-element.37), channel_id=1, source_target_pairs={{0,1},{2,3},{4,5},{6,7},{8,9},{10,11},{12,13},{14,15},{16,17},{18,... | collective-permute-start | bytes 344072 | tf_op jit(solution)/shard_map/ppermute | solution.py:332
  20.4 1.8 %shard_map.83 = (f32[5,4,16,128]{3,2,1,0:T(8,128)S(1)}, f32[3,5,5,4,16,128]{5,4,3,2,1,0:T(8,128)S(1)}) custom-call(f32[5,4,16,128]{3,2,1,0:T(8,128)} %bitcast.8, f32[3,5,5,4,16,128]{5,4,3,2,1,0:T(8,128)} %bitcast.7), custom_call_target="tpu_custom_call" | custom-call | bytes 5242880 | tf_op jit(solution)/shard_map/pallas_call | solution.py:58
  22.5 1.0 shard_map.84
  25.1 18.3 %all_to_all.30.refs_4_ = f32[16,3,8,128]{3,2,1,0:T(8,128)S(1)} all-to-all(f32[16,3,8,128]{3,2,1,0:T(8,128)S(1)} %shard_map.85), channel_id=1, replica_groups=mesh['inst'=16,'cells'=32] {'inst'}, dimensions={0} | all-to-all | bytes 393216 | tf_op jit(solution)/shard_map/all_to_all | solution.py:336
  44.3 5.3 %collective-permute-start.2 = (f32[5,2,16,128]{3,2,1,0:T(8,128)S(1)}, f32[5,2,16,128]{3,2,1,0:T(8,128)S(1)}, u32[]{:S(2)}, u32[]{:S(2)}) collective-permute-start(f32[5,2,16,128]{3,2,1,0:T(8,128)S(1)} %get-tuple-element.42), channel_id=1, source_target_pairs={{1,2},{3,4},{5,6},{7,8},{9,10},{11,12},{13,14},{15,16},{17,18},{19... | collective-permute-start | bytes 245768 | tf_op jit(solution)/shard_map/ppermute | solution.py:332
  49.6 1.9 %collective-permute-start.3 = (f32[5,2,16,128]{3,2,1,0:T(8,128)S(1)}, f32[5,2,16,128]{3,2,1,0:T(8,128)S(1)}, u32[]{:S(2)}, u32[]{:S(2)}) collective-permute-start(f32[5,2,16,128]{3,2,1,0:T(8,128)S(1)} %get-tuple-element.43), channel_id=1, source_target_pairs={{0,1},{2,3},{4,5},{6,7},{8,9},{10,11},{12,13},{14,15},{16,17},{18,... | collective-permute-start | bytes 245768 | tf_op jit(solution)/shard_map/ppermute | solution.py:332
  52.8 1.0 shard_map.87
  53.8 17.3 %all_to_all.31.refs_3_ = f32[16,5,8,128]{3,2,1,0:T(8,128)S(1)} all-to-all(f32[16,5,8,128]{3,2,1,0:T(8,128)S(1)} %shard_map.87), channel_id=1, replica_groups=mesh['inst'=16,'cells'=32] {'inst'}, dimensions={0} | all-to-all | bytes 655360 | tf_op jit(solution)/shard_map/all_to_all | solution.py:336
  71.9 15.4 %all_to_all.32.back = f32[16,5,8,128]{3,2,1,0:T(8,128)S(1)} all-to-all(f32[16,5,8,128]{3,2,1,0:T(8,128)S(1)} %shard_map.88), channel_id=1, replica_groups=mesh['inst'=16,'cells'=32] {'inst'}, dimensions={0} | all-to-all | bytes 655360 | tf_op jit(solution)/shard_map/all_to_all | solution.py:336
  87.3 5.3 %collective-permute-start.4 = (f32[5,2,16,128]{3,2,1,0:T(8,128)S(1)}, f32[5,2,16,128]{3,2,1,0:T(8,128)S(1)}, u32[]{:S(2)}, u32[]{:S(2)}) collective-permute-start(f32[5,2,16,128]{3,2,1,0:T(8,128)S(1)} %get-tuple-element.46), channel_id=1, source_target_pairs={{1,2},{3,4},{5,6},{7,8},{9,10},{11,12},{13,14},{15,16},{17,18},{19... | collective-permute-start | bytes 245768 | tf_op jit(solution)/shard_map/ppermute | solution.py:332
  92.7 1.9 %collective-permute-start.5 = (f32[5,2,16,128]{3,2,1,0:T(8,128)S(1)}, f32[5,2,16,128]{3,2,1,0:T(8,128)S(1)}, u32[]{:S(2)}, u32[]{:S(2)}) collective-permute-start(f32[5,2,16,128]{3,2,1,0:T(8,128)S(1)} %get-tuple-element.47), channel_id=1, source_target_pairs={{0,1},{2,3},{4,5},{6,7},{8,9},{10,11},{12,13},{14,15},{16,17},{18,... | collective-permute-start | bytes 245768 | tf_op jit(solution)/shard_map/ppermute | solution.py:332
  95.9 1.0 shard_map.90
  96.9 5.4 %collective-permute-start.6 = (f32[5,2,16,128]{3,2,1,0:T(8,128)S(1)}, f32[5,2,16,128]{3,2,1,0:T(8,128)S(1)}, u32[]{:S(2)}, u32[]{:S(2)}) collective-permute-start(f32[5,2,16,128]{3,2,1,0:T(8,128)S(1)} %get-tuple-element.49), channel_id=1, source_target_pairs={{1,2},{3,4},{5,6},{7,8},{9,10},{11,12},{13,14},{15,16},{17,18},{19... | collective-permute-start | bytes 245768 | tf_op jit(solution)/shard_map/ppermute | solution.py:332
  102.3 1.9 %collective-permute-start.7 = (f32[5,2,16,128]{3,2,1,0:T(8,128)S(1)}, f32[5,2,16,128]{3,2,1,0:T(8,128)S(1)}, u32[]{:S(2)}, u32[]{:S(2)}) collective-permute-start(f32[5,2,16,128]{3,2,1,0:T(8,128)S(1)} %get-tuple-element.50), channel_id=1, source_target_pairs={{0,1},{2,3},{4,5},{6,7},{8,9},{10,11},{12,13},{14,15},{16,17},{18,... | collective-permute-start | bytes 245768 | tf_op jit(solution)/shard_map/ppermute | solution.py:332
  105.5 1.0 shard_map.91
  106.5 16.1 %all_to_all.33.refs_3_ = f32[16,5,8,128]{3,2,1,0:T(8,128)S(1)} all-to-all(f32[16,5,8,128]{3,2,1,0:T(8,128)S(1)} %shard_map.91), channel_id=1, replica_groups=mesh['inst'=16,'cells'=32] {'inst'}, dimensions={0} | all-to-all | bytes 655360 | tf_op jit(solution)/shard_map/all_to_all | solution.py:336
  123.4 16.0 %all_to_all.34.back = f32[16,5,8,128]{3,2,1,0:T(8,128)S(1)} all-to-all(f32[16,5,8,128]{3,2,1,0:T(8,128)S(1)} %shard_map.92), channel_id=1, replica_groups=mesh['inst'=16,'cells'=32] {'inst'}, dimensions={0} | all-to-all | bytes 655360 | tf_op jit(solution)/shard_map/all_to_all | solution.py:336
  139.5 6.1 %collective-permute-start.8 = (f32[5,2,16,128]{3,2,1,0:T(8,128)S(1)}, f32[5,2,16,128]{3,2,1,0:T(8,128)S(1)}, u32[]{:S(2)}, u32[]{:S(2)}) collective-permute-start(f32[5,2,16,128]{3,2,1,0:T(8,128)S(1)} %get-tuple-element.53), channel_id=1, source_target_pairs={{1,2},{3,4},{5,6},{7,8},{9,10},{11,12},{13,14},{15,16},{17,18},{19... | collective-permute-start | bytes 245768 | tf_op jit(solution)/shard_map/ppermute | solution.py:332
  145.6 1.9 %collective-permute-start.9 = (f32[5,2,16,128]{3,2,1,0:T(8,128)S(1)}, f32[5,2,16,128]{3,2,1,0:T(8,128)S(1)}, u32[]{:S(2)}, u32[]{:S(2)}) collective-permute-start(f32[5,2,16,128]{3,2,1,0:T(8,128)S(1)} %get-tuple-element.54), channel_id=1, source_target_pairs={{0,1},{2,3},{4,5},{6,7},{8,9},{10,11},{12,13},{14,15},{16,17},{18,... | collective-permute-start | bytes 245768 | tf_op jit(solution)/shard_map/ppermute | solution.py:332
  147.7 1.1 collective-permute-done.9.refs_11_
  148.8 1.7 %shard_map.94 = f32[5,4,16,128]{3,2,1,0:T(8,128)} custom-call(f32[5,4,16,128]{3,2,1,0:T(8,128)S(1)} %get-tuple-element.30.adjoint.refs_0_, f32[5,4,16,128]{3,2,1,0:T(8,128)S(1)} %get-tuple-element.31.refs_1_, f32[4,16,128]{2,1,0:T(8,128)S(1)} %get-tuple-element.32.refs_2_, f32[3,4,16,128]{3,2,1,0:T(8,128)S(1)} %get-tuple-element.33.second.refs_3_, ...), custom_call_target="tpu_custom_call" | custom-call | flops 3000000 | bytes 3899392 | tf_op jit(solution)/shard_map/pallas_call | solution.py:58
  (22 shorter events, 8.5 us)
Async XLA Ops:
  1.8 23.0 %all-to-all-start = ((f32[16,3,8,128]{3,2,1,0:T(8,128)}), f32[16,3,8,128]{3,2,1,0:T(8,128)S(1)}, u32[]{:S(2)}, u32[]{:S(2)}) async-start(f32[16,3,8,128]{3,2,1,0:T(8,128)} %get-tuple-element.38), calls=%async_computation | async-start | bytes 393216 | tf_op jit(solution)/shard_map/all_to_all | solution.py:336
  10.3 12.2 %collective-permute-start = (f32[7,2,16,128]{3,2,1,0:T(8,128)}, f32[7,2,16,128]{3,2,1,0:T(8,128)S(1)}, u32[]{:S(2)}, u32[]{:S(2)}) collective-permute-start(f32[7,2,16,128]{3,2,1,0:T(8,128)} %get-tuple-element.36), channel_id=1, source_target_pairs={{1,2},{3,4},{5,6},{7,8},{9,10},{11,12},{13,14},{15,16},{17,18},{19... | collective-permute-start | bytes 344072 | tf_op jit(solution)/shard_map/ppermute | solution.py:332
  17.1 5.4 %collective-permute-start.1 = (f32[7,2,16,128]{3,2,1,0:T(8,128)S(1)}, f32[7,2,16,128]{3,2,1,0:T(8,128)S(1)}, u32[]{:S(2)}, u32[]{:S(2)}) collective-permute-start(f32[7,2,16,128]{3,2,1,0:T(8,128)S(1)} %get-tuple-element.37), channel_id=1, source_target_pairs={{0,1},{2,3},{4,5},{6,7},{8,9},{10,11},{12,13},{14,15},{16,17},{18,... | collective-permute-start | bytes 344072 | tf_op jit(solution)/shard_map/ppermute | solution.py:332
  23.5 0.7 copy-start
  24.2 0.6 copy-start.2
  43.3 0.9 copy-start.1
  44.3 7.9 %collective-permute-start.2 = (f32[5,2,16,128]{3,2,1,0:T(8,128)S(1)}, f32[5,2,16,128]{3,2,1,0:T(8,128)S(1)}, u32[]{:S(2)}, u32[]{:S(2)}) collective-permute-start(f32[5,2,16,128]{3,2,1,0:T(8,128)S(1)} %get-tuple-element.42), channel_id=1, source_target_pairs={{1,2},{3,4},{5,6},{7,8},{9,10},{11,12},{13,14},{15,16},{17,18},{19... | collective-permute-start | bytes 245768 | tf_op jit(solution)/shard_map/ppermute | solution.py:332
  49.6 3.2 %collective-permute-start.3 = (f32[5,2,16,128]{3,2,1,0:T(8,128)S(1)}, f32[5,2,16,128]{3,2,1,0:T(8,128)S(1)}, u32[]{:S(2)}, u32[]{:S(2)}) collective-permute-start(f32[5,2,16,128]{3,2,1,0:T(8,128)S(1)} %get-tuple-element.43), channel_id=1, source_target_pairs={{0,1},{2,3},{4,5},{6,7},{8,9},{10,11},{12,13},{14,15},{16,17},{18,... | collective-permute-start | bytes 245768 | tf_op jit(solution)/shard_map/ppermute | solution.py:332
  87.3 7.9 %collective-permute-start.4 = (f32[5,2,16,128]{3,2,1,0:T(8,128)S(1)}, f32[5,2,16,128]{3,2,1,0:T(8,128)S(1)}, u32[]{:S(2)}, u32[]{:S(2)}) collective-permute-start(f32[5,2,16,128]{3,2,1,0:T(8,128)S(1)} %get-tuple-element.46), channel_id=1, source_target_pairs={{1,2},{3,4},{5,6},{7,8},{9,10},{11,12},{13,14},{15,16},{17,18},{19... | collective-permute-start | bytes 245768 | tf_op jit(solution)/shard_map/ppermute | solution.py:332
  92.7 3.2 %collective-permute-start.5 = (f32[5,2,16,128]{3,2,1,0:T(8,128)S(1)}, f32[5,2,16,128]{3,2,1,0:T(8,128)S(1)}, u32[]{:S(2)}, u32[]{:S(2)}) collective-permute-start(f32[5,2,16,128]{3,2,1,0:T(8,128)S(1)} %get-tuple-element.47), channel_id=1, source_target_pairs={{0,1},{2,3},{4,5},{6,7},{8,9},{10,11},{12,13},{14,15},{16,17},{18,... | collective-permute-start | bytes 245768 | tf_op jit(solution)/shard_map/ppermute | solution.py:332
  96.9 7.9 %collective-permute-start.6 = (f32[5,2,16,128]{3,2,1,0:T(8,128)S(1)}, f32[5,2,16,128]{3,2,1,0:T(8,128)S(1)}, u32[]{:S(2)}, u32[]{:S(2)}) collective-permute-start(f32[5,2,16,128]{3,2,1,0:T(8,128)S(1)} %get-tuple-element.49), channel_id=1, source_target_pairs={{1,2},{3,4},{5,6},{7,8},{9,10},{11,12},{13,14},{15,16},{17,18},{19... | collective-permute-start | bytes 245768 | tf_op jit(solution)/shard_map/ppermute | solution.py:332
  102.3 3.2 %collective-permute-start.7 = (f32[5,2,16,128]{3,2,1,0:T(8,128)S(1)}, f32[5,2,16,128]{3,2,1,0:T(8,128)S(1)}, u32[]{:S(2)}, u32[]{:S(2)}) collective-permute-start(f32[5,2,16,128]{3,2,1,0:T(8,128)S(1)} %get-tuple-element.50), channel_id=1, source_target_pairs={{0,1},{2,3},{4,5},{6,7},{8,9},{10,11},{12,13},{14,15},{16,17},{18,... | collective-permute-start | bytes 245768 | tf_op jit(solution)/shard_map/ppermute | solution.py:332
  139.5 8.2 %collective-permute-start.8 = (f32[5,2,16,128]{3,2,1,0:T(8,128)S(1)}, f32[5,2,16,128]{3,2,1,0:T(8,128)S(1)}, u32[]{:S(2)}, u32[]{:S(2)}) collective-permute-start(f32[5,2,16,128]{3,2,1,0:T(8,128)S(1)} %get-tuple-element.53), channel_id=1, source_target_pairs={{1,2},{3,4},{5,6},{7,8},{9,10},{11,12},{13,14},{15,16},{17,18},{19... | collective-permute-start | bytes 245768 | tf_op jit(solution)/shard_map/ppermute | solution.py:332
  145.6 3.2 %collective-permute-start.9 = (f32[5,2,16,128]{3,2,1,0:T(8,128)S(1)}, f32[5,2,16,128]{3,2,1,0:T(8,128)S(1)}, u32[]{:S(2)}, u32[]{:S(2)}) collective-permute-start(f32[5,2,16,128]{3,2,1,0:T(8,128)S(1)} %get-tuple-element.54), channel_id=1, source_target_pairs={{0,1},{2,3},{4,5},{6,7},{8,9},{10,11},{12,13},{14,15},{16,17},{18,... | collective-permute-start | bytes 245768 | tf_op jit(solution)/shard_map/ppermute | solution.py:332

commit v3 on v2

--- a/solution.py
+++ b/solution.py
@@ -186,29 +186,35 @@
     return lambda var, layer: ref[var, layer]
 
 
-def local_kernel(adjoint, second, fourth, jacobian, odd, even, out, token, padded, coefs):
-    token[...] = jnp.zeros_like(token)
+def first_kernel(
+    factor,
+    adjoint,
+    gradient,
+    step,
+    second,
+    fourth,
+    jacobian,
+    odd,
+    even,
+    back,
+    state,
+    odd_ref,
+    even_ref,
+    padded,
+    coefs,
+):
     fill_padded(padded, coefs, own_slab(adjoint), second, fourth, odd, even, odd, even)
-
-    def finish(var, layer, value):
-        out[var, layer] = value
-
-    spatial(padded, coefs, second, fourth, jacobian, finish)
-
-
-def first_kernel(factor, adjoint, gradient, step, local, back, state, odd_ref, even_ref):
     for layer in range(LAYERS):
         for quarter in range(4):
             rows = slice(4 * quarter, 4 * quarter + 4)
             for var in range(VARS):
-                half = 4 * (var % 2)
-                state[var, layer, rows, :] = back[
-                    4 * layer + quarter, var // 2, half : half + 4, :
-                ]
-    for layer in range(LAYERS):
-        for var in range(VARS):
-            residual = local[var, layer] + state[var, layer] + gradient[var, layer]
-            state[var, layer] = adjoint[var, layer] - (factor * step[layer]) * residual
+                state[var, layer, rows, :] = back[4 * layer + quarter, var]
+
+    def finish(var, layer, value):
+        residual = value + state[var, layer] + gradient[var, layer]
+        state[var, layer] = adjoint[var, layer] - (factor * step[layer]) * residual
+
+    spatial(padded, coefs, second, fourth, jacobian, finish)
     write_halos(lambda row, layer: state[row, layer], odd_ref, even_ref, VARS)
 
 
@@ -287,41 +293,53 @@
         write_halos(lambda row, layer: out[row, layer], rest[0], rest[1], VARS)
 
 
-def couple(values, frequency, damping):
-    weights = [frequency * SLOPE[m] + damping * CURVE[m] for m in range(INSTANCES)]
+def weights_of(frequency, damping):
+    return [frequency * SLOPE[m] + damping * CURVE[m] for m in range(INSTANCES)]
+
+
+def combine(weights, values, wrap):
+    count = len(values)
+    if wrap > 0 and count > 4:
+        half = count // 2
+        plus = [0.5 * (weights[m] + weights[m + half]) for m in range(half)]
+        minus = [0.5 * (weights[m] - weights[m + half]) for m in range(half)]
+        sums = combine(plus, [values[j] + values[j + half] for j in range(half)], 1)
+        gaps = combine(minus, [values[j] - values[j + half] for j in range(half)], -1)
+        return [sums[k] + gaps[k] for k in range(half)] + [sums[k] - gaps[k] for k in range(half)]
     out = []
-    for k in range(INSTANCES):
-        acc = None
-        for j in range(INSTANCES):
-            term = weights[(j - k) % INSTANCES] * values[j]
-            acc = term if acc is None else acc + term
+    for k in range(count):
+        acc = weights[0] * values[k]
+        for j in range(count):
+            if j != k:
+                term = weights[(j - k) % count] * values[j]
+                acc = acc - term if j < k and wrap < 0 else acc + term
         out.append(acc)
     return out
 
 
 def couple_kernel(frequency, damping, received, *rest):
     out = rest[-1]
+    weights = weights_of(frequency[0], damping[0])
+    for index in range(received.shape[1]):
+        values = [received[j, index] for j in range(INSTANCES)]
+        for k, value in enumerate(combine(weights, values, 1)):
+            out[k, 2 * index] = value[0:4, :]
+            if 2 * index + 1 < VARS:
+                out[k, 2 * index + 1] = value[4:8, :]
+
+
+def middle_kernel(factor, frequency, damping, steps, received, out):
+    low = lax.broadcasted_iota(jnp.int32, (8, NZ), 0) < 4
+    weights = weights_of(frequency[0], damping[0])
 
     def tile(index, carry):
         values = [received[j, index] for j in range(INSTANCES)]
-        for k, value in enumerate(couple(values, frequency[0], damping[0])):
-            out[k, index] = value
-        return carry
-
-    lax.fori_loop(0, received.shape[1], tile, 0)
-
-
-def middle_kernel(factor, frequency, damping, steps, received, out):
-    low = lax.broadcasted_iota(jnp.int32, (8, NZ), 0) < 4
-
-    def tile(index, carry):
-        values = [received[j, index] for j in range(INSTANCES)]
-        first = couple(values, frequency[0], damping[0])
+        first = combine(weights, values, 1)
         moved = [
             values[k] - (factor * steps[k, 2]) * pltpu.roll(first[k], 4, 0)
             for k in range(INSTANCES)
         ]
-        for k, value in enumerate(couple(moved, frequency[0], damping[0])):
+        for k, value in enumerate(combine(weights, moved, 1)):
             out[k, index] = jnp.where(low, pltpu.roll(value, 4, 0), moved[k])
         return carry
 
@@ -368,26 +386,21 @@
         [HBM] * 2,
         scratch=(pltpu.SemaphoreType.DMA((2,)),),
     )
-    local, token = call(
-        local_kernel,
-        [shape(*FIELD), shape(8, NZ)],
-        [adjoint, second, fourth, jacobian, odd_first, even_first],
-        scratch=scratch,
-        flops=work,
-    )
     (coupled,) = call(
         couple_kernel,
-        [shape(INSTANCES, 3, 8, NZ)],
-        [frequency, damping, steps, in_hbm(token)],
-        scalars + [VMEM, ANY],
+        [shape(INSTANCES, VARS, 4, NZ)],
+        [frequency, damping, steps, odd_first, even_first, gradient],
+        scalars + [VMEM] + [ANY] * 3,
         flops=work,
     )
+    fixed = [adjoint, gradient, step, second, fourth, jacobian, odd_first, even_first]
     state, odd, even = call(
         lambda *refs: first_kernel(FACTORS[0], *refs),
         [shape(*FIELD)] + halos,
-        [adjoint, gradient, step, local, across(coupled)],
-    )
-    fixed = [adjoint, gradient, step, second, fourth, jacobian, odd_first, even_first]
+        fixed + [across(coupled)],
+        scratch=scratch,
+        flops=work,
+    )
     for section in (1, 3):
         odd, even = exchange(odd, even)
         (message,) = call(

time: 151 us -> 148 us (0.980)
  local copies, waits for them, and re-layouts: 2.17 us -> 0 us
  blocking collectives: 83 us -> 81.4 us
    unnamed x6 -> x0, local copies, waits for them, and re-layouts: 2.17 us -> none
    all_to_all x5, blocking collectives: 83 us -> 81.4 us  [across(): return lax.all_to_all(message, 'inst', 0, 0, tiled=True)]
    pallas_call x13 -> x12, Pallas kernels: 11.5 us -> 10.6 us  [call(): pl.pallas_call(kernel, out_shape=outs, in_specs=specs or [VMEM] * len(arg...]
  transfers between devices with their start and end apart: 11 -> 11, of which waited for: 9 -> 8; matrix products, arithmetic and copies ran while one was open for 0% -> 0% of each run, Pallas kernels for 2% -> 1%
where the time goes in v3:
time: 148 us; the launch traced here: 147 us
  blocking collectives  81.4 us (55%)
  starting transfers between devices  48.1 us (32%)
  Pallas kernels  10.6 us (7%)
  waiting for transfers between devices  5.43 us (4%)
  between operations  1.48 us (1%)
    all_to_all x5, blocking collectives, across(): return lax.all_to_all(message, 'inst', 0, 0, tiled=True)  81.4 us
    ppermute x5, starting transfers between devices, exchange(): lax.ppermute(odd, 'cells', PAIRS_ODD)  30 us
    pallas_call x12, Pallas kernels, call(): pl.pallas_call(kernel, out_shape=outs, in_specs=specs or [VMEM] * len(arg...  10.6 us
    ppermute x5, starting transfers between devices, exchange(): lax.ppermute(even, 'cells', PAIRS_EVEN)  9.6 us
    all_to_all x1, starting transfers between devices, across(): return lax.all_to_all(message, 'inst', 0, 0, tiled=True)  8.5 us
    ppermute x5, waiting for transfers between devices, exchange(): lax.ppermute(odd, 'cells', PAIRS_ODD)  3.68 us
  transfers between devices with their start and end apart: 11, of which 8 were waited for; matrix products, arithmetic and copies ran while one was open for 0% of the time, Pallas kernels for 1%

profile of v3, /device:TPU:201, one launch (start us, length us, event | category | flops | bytes accessed | tf_op | source)
XLA Modules:
  0.0 147.1 jit_solution(16750835453459406969)
XLA Ops:
  0.0 1.8 %shard_map.82 = (f32[16,3,8,128]{3,2,1,0:T(8,128)}, f32[7,2,16,128]{3,2,1,0:T(8,128)}, f32[7,2,16,128]{3,2,1,0:T(8,128)S(1)}, f32[5,4,16,128]{3,2,1,0:T(8,128)S(...) custom-call(f32[5,4,16,128]{3,2,1,0:T(8,128)} %bitcast.9, ...), custom_call_target="tpu_custom_call" | custom-call | bytes 1212416 | tf_op jit(solution)/shard_map/pallas_call | solution.py:58
  1.8 8.5 %all-to-all-start = ((f32[16,3,8,128]{3,2,1,0:T(8,128)}), f32[16,3,8,128]{3,2,1,0:T(8,128)S(1)}, u32[]{:S(2)}, u32[]{:S(2)}) async-start(f32[16,3,8,128]{3,2,1,0:T(8,128)} %get-tuple-element.36), calls=%async_computation | async-start | bytes 393216 | tf_op jit(solution)/shard_map/all_to_all | solution.py:354
  10.3 6.8 %collective-permute-start = (f32[7,2,16,128]{3,2,1,0:T(8,128)}, f32[7,2,16,128]{3,2,1,0:T(8,128)S(1)}, u32[]{:S(2)}, u32[]{:S(2)}) collective-permute-start(f32[7,2,16,128]{3,2,1,0:T(8,128)} %get-tuple-element.34), channel_id=1, source_target_pairs={{1,2},{3,4},{5,6},{7,8},{9,10},{11,12},{13,14},{15,16},{17,18},{19... | collective-permute-start | bytes 344072 | tf_op jit(solution)/shard_map/ppermute | solution.py:350
  17.1 1.9 %collective-permute-start.1 = (f32[7,2,16,128]{3,2,1,0:T(8,128)S(1)}, f32[7,2,16,128]{3,2,1,0:T(8,128)S(1)}, u32[]{:S(2)}, u32[]{:S(2)}) collective-permute-start(f32[7,2,16,128]{3,2,1,0:T(8,128)S(1)} %get-tuple-element.35), channel_id=1, source_target_pairs={{0,1},{2,3},{4,5},{6,7},{8,9},{10,11},{12,13},{14,15},{16,17},{18,... | collective-permute-start | bytes 344072 | tf_op jit(solution)/shard_map/ppermute | solution.py:350
  20.4 1.8 %shard_map.83 = (f32[5,4,16,128]{3,2,1,0:T(8,128)S(1)}, f32[3,5,5,4,16,128]{5,4,3,2,1,0:T(8,128)S(1)}) custom-call(f32[5,4,16,128]{3,2,1,0:T(8,128)} %bitcast.8, f32[3,5,5,4,16,128]{5,4,3,2,1,0:T(8,128)} %bitcast.7), custom_call_target="tpu_custom_call" | custom-call | bytes 5242880 | tf_op jit(solution)/shard_map/pallas_call | solution.py:58
  22.7 18.1 %all_to_all.30.refs_8_ = f32[16,5,4,128]{3,2,1,0:T(4,128)S(1)} all-to-all(f32[16,5,4,128]{3,2,1,0:T(4,128)S(1)} %shard_map.84), channel_id=1, replica_groups=mesh['inst'=16,'cells'=32] {'inst'}, dimensions={0} | all-to-all | bytes 327680 | tf_op jit(solution)/shard_map/all_to_all | solution.py:354
  40.8 1.1 shard_map.85
  41.9 5.0 %collective-permute-start.2 = (f32[5,2,16,128]{3,2,1,0:T(8,128)S(1)}, f32[5,2,16,128]{3,2,1,0:T(8,128)S(1)}, u32[]{:S(2)}, u32[]{:S(2)}) collective-permute-start(f32[5,2,16,128]{3,2,1,0:T(8,128)S(1)} %get-tuple-element.38), channel_id=1, source_target_pairs={{1,2},{3,4},{5,6},{7,8},{9,10},{11,12},{13,14},{15,16},{17,18},{19... | collective-permute-start | bytes 245768 | tf_op jit(solution)/shard_map/ppermute | solution.py:350
  46.8 1.9 %collective-permute-start.3 = (f32[5,2,16,128]{3,2,1,0:T(8,128)S(1)}, f32[5,2,16,128]{3,2,1,0:T(8,128)S(1)}, u32[]{:S(2)}, u32[]{:S(2)}) collective-permute-start(f32[5,2,16,128]{3,2,1,0:T(8,128)S(1)} %get-tuple-element.39), channel_id=1, source_target_pairs={{0,1},{2,3},{4,5},{6,7},{8,9},{10,11},{12,13},{14,15},{16,17},{18,... | collective-permute-start | bytes 245768 | tf_op jit(solution)/shard_map/ppermute | solution.py:350
  48.8 1.4 collective-permute-done.2.refs_9_
  50.1 1.0 shard_map.86
  51.1 17.1 %all_to_all.31.refs_3_ = f32[16,5,8,128]{3,2,1,0:T(8,128)S(1)} all-to-all(f32[16,5,8,128]{3,2,1,0:T(8,128)S(1)} %shard_map.86), channel_id=1, replica_groups=mesh['inst'=16,'cells'=32] {'inst'}, dimensions={0} | all-to-all | bytes 655360 | tf_op jit(solution)/shard_map/all_to_all | solution.py:354
  68.6 15.4 %all_to_all.32.back = f32[16,5,8,128]{3,2,1,0:T(8,128)S(1)} all-to-all(f32[16,5,8,128]{3,2,1,0:T(8,128)S(1)} %shard_map.87), channel_id=1, replica_groups=mesh['inst'=16,'cells'=32] {'inst'}, dimensions={0} | all-to-all | bytes 655360 | tf_op jit(solution)/shard_map/all_to_all | solution.py:354
  84.1 5.3 %collective-permute-start.4 = (f32[5,2,16,128]{3,2,1,0:T(8,128)S(1)}, f32[5,2,16,128]{3,2,1,0:T(8,128)S(1)}, u32[]{:S(2)}, u32[]{:S(2)}) collective-permute-start(f32[5,2,16,128]{3,2,1,0:T(8,128)S(1)} %get-tuple-element.42), channel_id=1, source_target_pairs={{1,2},{3,4},{5,6},{7,8},{9,10},{11,12},{13,14},{15,16},{17,18},{19... | collective-permute-start | bytes 245768 | tf_op jit(solution)/shard_map/ppermute | solution.py:350
  89.4 1.9 %collective-permute-start.5 = (f32[5,2,16,128]{3,2,1,0:T(8,128)S(1)}, f32[5,2,16,128]{3,2,1,0:T(8,128)S(1)}, u32[]{:S(2)}, u32[]{:S(2)}) collective-permute-start(f32[5,2,16,128]{3,2,1,0:T(8,128)S(1)} %get-tuple-element.43), channel_id=1, source_target_pairs={{0,1},{2,3},{4,5},{6,7},{8,9},{10,11},{12,13},{14,15},{16,17},{18,... | collective-permute-start | bytes 245768 | tf_op jit(solution)/shard_map/ppermute | solution.py:350
  92.6 1.0 shard_map.89
  93.6 5.0 %collective-permute-start.6 = (f32[5,2,16,128]{3,2,1,0:T(8,128)S(1)}, f32[5,2,16,128]{3,2,1,0:T(8,128)S(1)}, u32[]{:S(2)}, u32[]{:S(2)}) collective-permute-start(f32[5,2,16,128]{3,2,1,0:T(8,128)S(1)} %get-tuple-element.45), channel_id=1, source_target_pairs={{1,2},{3,4},{5,6},{7,8},{9,10},{11,12},{13,14},{15,16},{17,18},{19... | collective-permute-start | bytes 245768 | tf_op jit(solution)/shard_map/ppermute | solution.py:350
  98.6 1.9 %collective-permute-start.7 = (f32[5,2,16,128]{3,2,1,0:T(8,128)S(1)}, f32[5,2,16,128]{3,2,1,0:T(8,128)S(1)}, u32[]{:S(2)}, u32[]{:S(2)}) collective-permute-start(f32[5,2,16,128]{3,2,1,0:T(8,128)S(1)} %get-tuple-element.46), channel_id=1, source_target_pairs={{0,1},{2,3},{4,5},{6,7},{8,9},{10,11},{12,13},{14,15},{16,17},{18,... | collective-permute-start | bytes 245768 | tf_op jit(solution)/shard_map/ppermute | solution.py:350
  102.8 15.8 %all_to_all.33.refs_3_ = f32[16,5,8,128]{3,2,1,0:T(8,128)S(1)} all-to-all(f32[16,5,8,128]{3,2,1,0:T(8,128)S(1)} %shard_map.90), channel_id=1, replica_groups=mesh['inst'=16,'cells'=32] {'inst'}, dimensions={0} | all-to-all | bytes 655360 | tf_op jit(solution)/shard_map/all_to_all | solution.py:354
  119.1 15.0 %all_to_all.34.back = f32[16,5,8,128]{3,2,1,0:T(8,128)S(1)} all-to-all(f32[16,5,8,128]{3,2,1,0:T(8,128)S(1)} %shard_map.91), channel_id=1, replica_groups=mesh['inst'=16,'cells'=32] {'inst'}, dimensions={0} | all-to-all | bytes 655360 | tf_op jit(solution)/shard_map/all_to_all | solution.py:354
  134.3 7.9 %collective-permute-start.8 = (f32[5,2,16,128]{3,2,1,0:T(8,128)S(1)}, f32[5,2,16,128]{3,2,1,0:T(8,128)S(1)}, u32[]{:S(2)}, u32[]{:S(2)}) collective-permute-start(f32[5,2,16,128]{3,2,1,0:T(8,128)S(1)} %get-tuple-element.49), channel_id=1, source_target_pairs={{1,2},{3,4},{5,6},{7,8},{9,10},{11,12},{13,14},{15,16},{17,18},{19... | collective-permute-start | bytes 245768 | tf_op jit(solution)/shard_map/ppermute | solution.py:350
  142.2 1.9 %collective-permute-start.9 = (f32[5,2,16,128]{3,2,1,0:T(8,128)S(1)}, f32[5,2,16,128]{3,2,1,0:T(8,128)S(1)}, u32[]{:S(2)}, u32[]{:S(2)}) collective-permute-start(f32[5,2,16,128]{3,2,1,0:T(8,128)S(1)} %get-tuple-element.50), channel_id=1, source_target_pairs={{0,1},{2,3},{4,5},{6,7},{8,9},{10,11},{12,13},{14,15},{16,17},{18,... | collective-permute-start | bytes 245768 | tf_op jit(solution)/shard_map/ppermute | solution.py:350
  144.3 1.1 collective-permute-done.9.refs_11_
  145.4 1.7 %shard_map.93 = f32[5,4,16,128]{3,2,1,0:T(8,128)} custom-call(f32[5,4,16,128]{3,2,1,0:T(8,128)S(1)} %get-tuple-element.28.refs_0_, f32[5,4,16,128]{3,2,1,0:T(8,128)S(1)} %get-tuple-element.29.rest_2_.refs_1_, f32[4,16,128]{2,1,0:T(8,128)S(1)} %get-tuple-element.30.refs_2_, f32[3,4,16,128]{3,2,1,0:T(8,128)S(1)} %get-tuple-element.31.refs_3_, ...), custom_call_target="tpu_custom_call" | custom-call | flops 3000000 | bytes 3899392 | tf_op jit(solution)/shard_map/pallas_call | solution.py:58
  (15 shorter events, 5.2 us)
Async XLA Ops:
  1.8 20.7 %all-to-all-start = ((f32[16,3,8,128]{3,2,1,0:T(8,128)}), f32[16,3,8,128]{3,2,1,0:T(8,128)S(1)}, u32[]{:S(2)}, u32[]{:S(2)}) async-start(f32[16,3,8,128]{3,2,1,0:T(8,128)} %get-tuple-element.36), calls=%async_computation | async-start | bytes 393216 | tf_op jit(solution)/shard_map/all_to_all | solution.py:354
  10.3 12.2 %collective-permute-start = (f32[7,2,16,128]{3,2,1,0:T(8,128)}, f32[7,2,16,128]{3,2,1,0:T(8,128)S(1)}, u32[]{:S(2)}, u32[]{:S(2)}) collective-permute-start(f32[7,2,16,128]{3,2,1,0:T(8,128)} %get-tuple-element.34), channel_id=1, source_target_pairs={{1,2},{3,4},{5,6},{7,8},{9,10},{11,12},{13,14},{15,16},{17,18},{19... | collective-permute-start | bytes 344072 | tf_op jit(solution)/shard_map/ppermute | solution.py:350
  17.1 5.4 %collective-permute-start.1 = (f32[7,2,16,128]{3,2,1,0:T(8,128)S(1)}, f32[7,2,16,128]{3,2,1,0:T(8,128)S(1)}, u32[]{:S(2)}, u32[]{:S(2)}) collective-permute-start(f32[7,2,16,128]{3,2,1,0:T(8,128)S(1)} %get-tuple-element.35), channel_id=1, source_target_pairs={{0,1},{2,3},{4,5},{6,7},{8,9},{10,11},{12,13},{14,15},{16,17},{18,... | collective-permute-start | bytes 344072 | tf_op jit(solution)/shard_map/ppermute | solution.py:350
  41.9 8.3 %collective-permute-start.2 = (f32[5,2,16,128]{3,2,1,0:T(8,128)S(1)}, f32[5,2,16,128]{3,2,1,0:T(8,128)S(1)}, u32[]{:S(2)}, u32[]{:S(2)}) collective-permute-start(f32[5,2,16,128]{3,2,1,0:T(8,128)S(1)} %get-tuple-element.38), channel_id=1, source_target_pairs={{1,2},{3,4},{5,6},{7,8},{9,10},{11,12},{13,14},{15,16},{17,18},{19... | collective-permute-start | bytes 245768 | tf_op jit(solution)/shard_map/ppermute | solution.py:350
  46.8 3.3 %collective-permute-start.3 = (f32[5,2,16,128]{3,2,1,0:T(8,128)S(1)}, f32[5,2,16,128]{3,2,1,0:T(8,128)S(1)}, u32[]{:S(2)}, u32[]{:S(2)}) collective-permute-start(f32[5,2,16,128]{3,2,1,0:T(8,128)S(1)} %get-tuple-element.39), channel_id=1, source_target_pairs={{0,1},{2,3},{4,5},{6,7},{8,9},{10,11},{12,13},{14,15},{16,17},{18,... | collective-permute-start | bytes 245768 | tf_op jit(solution)/shard_map/ppermute | solution.py:350
  84.1 8.1 %collective-permute-start.4 = (f32[5,2,16,128]{3,2,1,0:T(8,128)S(1)}, f32[5,2,16,128]{3,2,1,0:T(8,128)S(1)}, u32[]{:S(2)}, u32[]{:S(2)}) collective-permute-start(f32[5,2,16,128]{3,2,1,0:T(8,128)S(1)} %get-tuple-element.42), channel_id=1, source_target_pairs={{1,2},{3,4},{5,6},{7,8},{9,10},{11,12},{13,14},{15,16},{17,18},{19... | collective-permute-start | bytes 245768 | tf_op jit(solution)/shard_map/ppermute | solution.py:350
  89.4 3.2 %collective-permute-start.5 = (f32[5,2,16,128]{3,2,1,0:T(8,128)S(1)}, f32[5,2,16,128]{3,2,1,0:T(8,128)S(1)}, u32[]{:S(2)}, u32[]{:S(2)}) collective-permute-start(f32[5,2,16,128]{3,2,1,0:T(8,128)S(1)} %get-tuple-element.43), channel_id=1, source_target_pairs={{0,1},{2,3},{4,5},{6,7},{8,9},{10,11},{12,13},{14,15},{16,17},{18,... | collective-permute-start | bytes 245768 | tf_op jit(solution)/shard_map/ppermute | solution.py:350
  93.6 7.9 %collective-permute-start.6 = (f32[5,2,16,128]{3,2,1,0:T(8,128)S(1)}, f32[5,2,16,128]{3,2,1,0:T(8,128)S(1)}, u32[]{:S(2)}, u32[]{:S(2)}) collective-permute-start(f32[5,2,16,128]{3,2,1,0:T(8,128)S(1)} %get-tuple-element.45), channel_id=1, source_target_pairs={{1,2},{3,4},{5,6},{7,8},{9,10},{11,12},{13,14},{15,16},{17,18},{19... | collective-permute-start | bytes 245768 | tf_op jit(solution)/shard_map/ppermute | solution.py:350
  98.6 3.2 %collective-permute-start.7 = (f32[5,2,16,128]{3,2,1,0:T(8,128)S(1)}, f32[5,2,16,128]{3,2,1,0:T(8,128)S(1)}, u32[]{:S(2)}, u32[]{:S(2)}) collective-permute-start(f32[5,2,16,128]{3,2,1,0:T(8,128)S(1)} %get-tuple-element.46), channel_id=1, source_target_pairs={{0,1},{2,3},{4,5},{6,7},{8,9},{10,11},{12,13},{14,15},{16,17},{18,... | collective-permute-start | bytes 245768 | tf_op jit(solution)/shard_map/ppermute | solution.py:350
  134.3 10.0 %collective-permute-start.8 = (f32[5,2,16,128]{3,2,1,0:T(8,128)S(1)}, f32[5,2,16,128]{3,2,1,0:T(8,128)S(1)}, u32[]{:S(2)}, u32[]{:S(2)}) collective-permute-start(f32[5,2,16,128]{3,2,1,0:T(8,128)S(1)} %get-tuple-element.49), channel_id=1, source_target_pairs={{1,2},{3,4},{5,6},{7,8},{9,10},{11,12},{13,14},{15,16},{17,18},{19... | collective-permute-start | bytes 245768 | tf_op jit(solution)/shard_map/ppermute | solution.py:350
  142.2 3.2 %collective-permute-start.9 = (f32[5,2,16,128]{3,2,1,0:T(8,128)S(1)}, f32[5,2,16,128]{3,2,1,0:T(8,128)S(1)}, u32[]{:S(2)}, u32[]{:S(2)}) collective-permute-start(f32[5,2,16,128]{3,2,1,0:T(8,128)S(1)} %get-tuple-element.50), channel_id=1, source_target_pairs={{0,1},{2,3},{4,5},{6,7},{8,9},{10,11},{12,13},{14,15},{16,17},{18,... | collective-permute-start | bytes 245768 | tf_op jit(solution)/shard_map/ppermute | solution.py:350

commit v4 on v3

--- a/solution.py
+++ b/solution.py
@@ -53,13 +53,13 @@
     return pltpu.with_memory_space_constraint(array, pltpu.VMEM)
 
 
-def call(kernel, outs, args, specs=None, scratch=(), flops=0):
+def call(kernel, outs, args, specs=None, scratch=(), flops=0, out_specs=None):
     size = sum(math.prod(x.shape) for x in list(args) + list(outs)) * 4
     return pl.pallas_call(
         kernel,
         out_shape=outs,
         in_specs=specs or [VMEM] * len(args),
-        out_specs=[VMEM] * len(outs),
+        out_specs=out_specs or [VMEM] * len(outs),
         scratch_shapes=list(scratch),
         compiler_params=pltpu.CompilerParams(vmem_limit_bytes=8 * 1024 * 1024),
         cost_estimate=pl.CostEstimate(flops=flops, bytes_accessed=size, transcendentals=0),
@@ -114,23 +114,15 @@
     write_halos(read, odd_ref, even_ref, VARS + 2)
 
 
-def fill_padded(padded, coefs, own, own_second, own_fourth, odd, even, odd_first, even_first):
-    after = jnp.where(even_device(), 6, 0)
+def stage_halos(staged, odd, even):
+    above = jnp.where(even_device(), 2, 0)
     for layer in range(2):
         for var in range(VARS):
-            padded[var, after + layer] = even[var, layer]
-            padded[var, 6 - after + layer] = odd[var, layer]
-        for kind in range(2):
-            coefs[kind, after + layer] = even_first[VARS + kind, layer]
-            coefs[kind, 6 - after + layer] = odd_first[VARS + kind, layer]
-    for layer in range(LAYERS):
-        for var in range(VARS):
-            padded[var, 2 + layer] = own(var, layer)
-        coefs[0, 2 + layer] = own_second[0, layer]
-        coefs[1, 2 + layer] = own_fourth[0, layer]
-
-
-def spatial(padded, coefs, second, fourth, jacobian, finish):
+            staged[var, above + layer] = even[var, layer]
+            staged[var, 2 - above + layer] = odd[var, layer]
+
+
+def spatial_yz(field, second, fourth, jacobian, finish):
     row = lax.broadcasted_iota(jnp.int32, (NY, NZ), 0)
     lane = lax.broadcasted_iota(jnp.int32, (NY, NZ), 1)
 
@@ -146,19 +138,12 @@
         central = []
         damped = []
         for var in range(VARS):
-            v = [padded[var, layer + i] for i in range(5)]
-            jump = [v[i + 1] - v[i] for i in range(4)]
-            fourth_flux = [coefs[1, layer + i] * jump[i] for i in range(4)]
-            second_below = coefs[0, layer + 1] * jump[1]
-            second_above = coefs[0, layer + 2] * jump[2]
-            term = (fourth_flux[3] - fourth_flux[0]) + 3.0 * (fourth_flux[1] - fourth_flux[2])
-            total = term + (second_below - second_above)
-            parts = [v[1] - v[3]]
-            mid = v[2]
+            mid = field[var, layer]
+            parts = []
+            total = None
             for axis in range(2):
                 upper = ahead(mid, axis)
-                lower = behind(mid, axis, 0.0)
-                parts.append(lower - upper)
+                parts.append(behind(mid, axis, 0.0) - upper)
                 step_up = upper - mid
                 flux = fourth[1 + axis, layer] * step_up
                 face = (
@@ -167,14 +152,15 @@
                     + behind(flux, axis, 0.0)
                     - second[1 + axis, layer] * step_up
                 )
-                total = total + (face - behind(face, axis, flux))
+                term = face - behind(face, axis, flux)
+                total = term if total is None else total + term
             central.append(parts)
             damped.append(total)
         for var in range(VARS):
             acc = None
-            for direction in range(3):
+            for axis in range(2):
                 for a in range(VARS):
-                    term = jacobian[direction, a, var, layer] * central[a][direction]
+                    term = jacobian[1 + axis, a, var, layer] * central[a][axis]
                     acc = term if acc is None else acc + term
             finish(var, layer, damped[var] + 0.5 * acc)
         return carry
@@ -182,8 +168,35 @@
     lax.fori_loop(0, LAYERS, layer_step, 0)
 
 
-def own_slab(ref):
-    return lambda var, layer: ref[var, layer]
+def spatial_x(field, staged, coefs, jacobian, damped, finish):
+    for var in range(VARS):
+        v = (
+            [staged[var, 0], staged[var, 1]]
+            + [field[var, layer] for layer in range(LAYERS)]
+            + [staged[var, 2], staged[var, 3]]
+        )
+        jump = [v[i + 1] - v[i] for i in range(LAYERS + 3)]
+        flux = [coefs[1, i] * jump[i] for i in range(LAYERS + 3)]
+        face = [
+            flux[i + 1] - 2.0 * flux[i] + flux[i - 1] - coefs[0, i] * jump[i]
+            for i in range(1, LAYERS + 2)
+        ]
+        for layer in range(LAYERS):
+            damped[0, var, layer] = v[layer + 1] - v[layer + 3]
+            damped[1, var, layer] = face[layer + 1] - face[layer]
+
+    for var in range(VARS):
+        for layer in range(LAYERS):
+            acc = None
+            for a in range(VARS):
+                term = jacobian[0, a, var, layer] * damped[0, a, layer]
+                acc = term if acc is None else acc + term
+            finish(var, layer, damped[1, var, layer] + 0.5 * acc)
+
+
+def quarters(layer):
+    for quarter in range(4):
+        yield 4 * layer + quarter, slice(4 * quarter, 4 * quarter + 4)
 
 
 def first_kernel(
@@ -197,100 +210,103 @@
     odd,
     even,
     back,
+    coefs,
     state,
     odd_ref,
     even_ref,
-    padded,
-    coefs,
+    staged,
+    damped,
 ):
-    fill_padded(padded, coefs, own_slab(adjoint), second, fourth, odd, even, odd, even)
+    above = jnp.where(even_device(), 6, 0)
+    for kind in range(2):
+        for layer in range(2):
+            coefs[kind, above + layer] = even[VARS + kind, layer]
+            coefs[kind, 6 - above + layer] = odd[VARS + kind, layer]
     for layer in range(LAYERS):
-        for quarter in range(4):
-            rows = slice(4 * quarter, 4 * quarter + 4)
+        coefs[0, 2 + layer] = second[0, layer]
+        coefs[1, 2 + layer] = fourth[0, layer]
+        for chunk, rows in quarters(layer):
             for var in range(VARS):
-                state[var, layer, rows, :] = back[4 * layer + quarter, var]
-
-    def finish(var, layer, value):
+                state[var, layer, rows, :] = back[chunk, var]
+    stage_halos(staged, odd, even)
+
+    def base(var, layer, value):
         residual = value + state[var, layer] + gradient[var, layer]
         state[var, layer] = adjoint[var, layer] - (factor * step[layer]) * residual
 
-    spatial(padded, coefs, second, fourth, jacobian, finish)
+    spatial_yz(adjoint, second, fourth, jacobian, base)
+
+    def finish(var, layer, value):
+        state[var, layer] = state[var, layer] - (factor * step[layer]) * value
+
+    spatial_x(adjoint, staged, coefs, jacobian, damped, finish)
     write_halos(lambda row, layer: state[row, layer], odd_ref, even_ref, VARS)
 
 
-def send_kernel(
-    factor,
-    adjoint,
-    gradient,
-    step,
-    second,
-    fourth,
-    jacobian,
-    odd_first,
-    even_first,
-    state,
-    odd,
-    even,
-    message,
-    padded,
-    coefs,
+def inner_kernel(
+    factor, adjoint, gradient, step, second, fourth, jacobian, state, *rest
 ):
-    fill_padded(
-        padded, coefs, own_slab(state), second, fourth, odd, even, odd_first, even_first
-    )
+    coupled, out = rest if len(rest) == 2 else (None, rest[0])
+
+    def base(var, layer, value):
+        residual = value + gradient[var, layer]
+        if coupled is not None:
+            residual = residual + coupled[var, layer]
+        out[var, layer] = adjoint[var, layer] - (factor * step[layer]) * residual
+
+    spatial_yz(state, second, fourth, jacobian, base)
+
+
+def send_kernel(factor, step, jacobian, coefs, state, base, odd, even, message, staged, damped):
+    stage_halos(staged, odd, even)
 
     def finish(var, layer, value):
-        residual = value + gradient[var, layer]
-        q = adjoint[var, layer] - (factor * step[layer]) * residual
-        u = padded[var, 2 + layer]
-        for quarter in range(4):
-            rows = slice(4 * quarter, 4 * quarter + 4)
-            message[4 * layer + quarter, var, 0:4, :] = u[rows, :]
-            message[4 * layer + quarter, var, 4:8, :] = q[rows, :]
-
-    spatial(padded, coefs, second, fourth, jacobian, finish)
+        q = base[var, layer] - (factor * step[layer]) * value
+        u = state[var, layer]
+        for chunk, rows in quarters(layer):
+            message[chunk, var, 0:4, :] = u[rows, :]
+            message[chunk, var, 4:8, :] = q[rows, :]
+
+    spatial_x(state, staged, coefs, jacobian, damped, finish)
 
 
 def unpack_kernel(back, state, coupled, odd_ref, even_ref):
     for layer in range(LAYERS):
-        for quarter in range(4):
-            rows = slice(4 * quarter, 4 * quarter + 4)
+        for chunk, rows in quarters(layer):
             for var in range(VARS):
-                coupled[var, layer, rows, :] = back[4 * layer + quarter, var, 0:4, :]
-                state[var, layer, rows, :] = back[4 * layer + quarter, var, 4:8, :]
+                coupled[var, layer, rows, :] = back[chunk, var, 0:4, :]
+                state[var, layer, rows, :] = back[chunk, var, 4:8, :]
     write_halos(lambda row, layer: state[row, layer], odd_ref, even_ref, VARS)
 
 
 def update_kernel(
-    factor,
-    last,
-    adjoint,
-    gradient,
-    step,
-    second,
-    fourth,
-    jacobian,
-    odd_first,
-    even_first,
-    state,
-    coupled,
-    odd,
-    even,
-    out,
-    *rest,
+    factor, step, jacobian, coefs, state, base, odd, even, out, odd_ref, even_ref, staged, damped
 ):
-    padded, coefs = rest[-2:]
-    fill_padded(
-        padded, coefs, own_slab(state), second, fourth, odd, even, odd_first, even_first
-    )
+    stage_halos(staged, odd, even)
 
     def finish(var, layer, value):
-        residual = value + coupled[var, layer] + gradient[var, layer]
-        out[var, layer] = adjoint[var, layer] - (factor * step[layer]) * residual
-
-    spatial(padded, coefs, second, fourth, jacobian, finish)
-    if not last:
-        write_halos(lambda row, layer: out[row, layer], rest[0], rest[1], VARS)
+        out[var, layer] = base[var, layer] - (factor * step[layer]) * value
+
+    spatial_x(state, staged, coefs, jacobian, damped, finish)
+    write_halos(lambda row, layer: out[row, layer], odd_ref, even_ref, VARS)
+
+
+def last_kernel(
+    factor, step, jacobian, coefs, state, base, odd, even, out, staged, damped, result, sems
+):
+    stage_halos(staged, odd, even)
+    copies = [
+        pltpu.make_async_copy(result.at[var], out.at[var], sems.at[var]) for var in range(VARS)
+    ]
+
+    def finish(var, layer, value):
+        result[var, layer] = base[var, layer] - (factor * step[layer]) * value
+        if layer == LAYERS - 1:
+            copies[var].start()
+
+    spatial_x(state, staged, coefs, jacobian, damped, finish)
+    for copy in copies:
+        copy.wait()
 
 
 def weights_of(frequency, damping):
@@ -363,7 +379,7 @@
     second = second_coef[0]
     fourth = fourth_coef[0]
     step = time_step[0]
-    scratch = (pltpu.VMEM((VARS, 8, NY, NZ), F32), pltpu.VMEM((2, 8, NY, NZ), F32))
+    scratch = (pltpu.VMEM((VARS, 4, NY, NZ), F32), pltpu.VMEM((2,) + FIELD, F32))
     halos = [shape(*HALO), shape(*HALO)]
     scalars = [SMEM, SMEM]
     work = 3 * 10**6
@@ -393,25 +409,36 @@
         scalars + [VMEM] + [ANY] * 3,
         flops=work,
     )
-    fixed = [adjoint, gradient, step, second, fourth, jacobian, odd_first, even_first]
-    state, odd, even = call(
+    fixed = [adjoint, gradient, step, second, fourth, jacobian]
+    coefs, state, odd, even = call(
         lambda *refs: first_kernel(FACTORS[0], *refs),
-        [shape(*FIELD)] + halos,
-        fixed + [across(coupled)],
+        [kept(2, 8, NY, NZ), shape(*FIELD)] + halos,
+        fixed + [odd_first, even_first, across(coupled)],
         scratch=scratch,
         flops=work,
     )
+
+    def inner(factor, operands):
+        return call(
+            lambda *refs: inner_kernel(factor, *refs),
+            [shape(*FIELD)],
+            fixed + operands,
+            flops=work,
+        )
+
     for section in (1, 3):
+        factor = FACTORS[section]
         odd, even = exchange(odd, even)
+        base = inner(factor, [state])
         (message,) = call(
-            lambda *refs: send_kernel(FACTORS[section], *refs),
+            lambda *refs: send_kernel(factor, *refs),
             [shape(INSTANCES, VARS, 8, NZ)],
-            fixed + [state, odd, even],
+            [step, jacobian, coefs, state, *base, odd, even],
             scratch=scratch,
             flops=work,
         )
         (message,) = call(
-            lambda *refs: middle_kernel(FACTORS[section], *refs),
+            lambda *refs: middle_kernel(factor, *refs),
             [shape(INSTANCES, VARS, 8, NZ)],
             [frequency, damping, steps, across(message)],
             scalars + [VMEM, VMEM],
@@ -420,18 +447,27 @@
         state, coupled, odd, even = call(
             unpack_kernel, [shape(*FIELD), shape(*FIELD)] + halos, [across(message)]
         )
+        factor = FACTORS[section + 1]
         odd, even = exchange(odd, even)
-        last = section == 3
-        outs = call(
-            lambda *refs: update_kernel(FACTORS[section + 1], last, *refs),
-            [shape(*FIELD)] + ([] if last else halos),
-            fixed + [state, coupled, odd, even],
-            scratch=scratch,
-            flops=work,
-        )
-        if last:
-            return outs[0][None]
-        state, odd, even = outs
+        base = inner(factor, [state, coupled])
+        operands = [step, jacobian, coefs, state, *base, odd, even]
+        if section == 1:
+            state, odd, even = call(
+                lambda *refs: update_kernel(factor, *refs),
+                [shape(*FIELD)] + halos,
+                operands,
+                scratch=scratch,
+                flops=work,
+            )
+    (updated,) = call(
+        lambda *refs: last_kernel(factor, *refs),
+        [shape(*FIELD)],
+        operands,
+        scratch=scratch + (pltpu.VMEM(FIELD, F32), pltpu.SemaphoreType.DMA((VARS,))),
+        flops=work,
+        out_specs=[HBM],
+    )
+    return updated[None]
 
 
 def solution(mesh):

time: 148 us -> 145 us (0.980)
  waiting for transfers between devices: 5.43 us -> 1.54 us
  starting transfers between devices: 48.1 us -> 49.7 us
  blocking collectives: 81.4 us -> 79.9 us
    ppermute x5, waiting for transfers between devices: 3.68 us -> 1.01 us  [exchange(): lax.ppermute(odd, 'cells', PAIRS_ODD)]
    ppermute x5, starting transfers between devices: 30 us -> 31.6 us  [exchange(): lax.ppermute(odd, 'cells', PAIRS_ODD)]
    all_to_all x5, blocking collectives: 81.4 us -> 79.9 us  [across(): return lax.all_to_all(message, 'inst', 0, 0, tiled=True)]
    pallas_call x12 -> x16, Pallas kernels: 10.6 us -> 11.1 us  [call(): pl.pallas_call(kernel, out_shape=outs, in_specs=specs or [VMEM] * len(arg...]
  transfers between devices with their start and end apart: 11 -> 11, of which waited for: 8 -> 5; matrix products, arithmetic and copies ran while one was open for 0% -> 0% of each run, Pallas kernels for 1% -> 4%
where the time goes in v4:
time: 145 us; the launch traced here: 144 us
  blocking collectives  79.9 us (55%)
  starting transfers between devices  49.7 us (34%)
  Pallas kernels  11.1 us (8%)
  waiting for transfers between devices  1.54 us (1%)
  between operations  1.5 us (1%)
    all_to_all x5, blocking collectives, across(): return lax.all_to_all(message, 'inst', 0, 0, tiled=True)  79.9 us
    ppermute x5, starting transfers between devices, exchange(): lax.ppermute(odd, 'cells', PAIRS_ODD)  31.6 us
    pallas_call x16, Pallas kernels, call(): pl.pallas_call(kernel, out_shape=outs, in_specs=specs or [VMEM] * len(arg...  11.1 us
    ppermute x5, starting transfers between devices, exchange(): lax.ppermute(even, 'cells', PAIRS_EVEN)  9.6 us
    all_to_all x1, starting transfers between devices, across(): return lax.all_to_all(message, 'inst', 0, 0, tiled=True)  8.5 us
  transfers between devices with their start and end apart: 11, of which 5 were waited for; matrix products, arithmetic and copies ran while one was open for 0% of the time, Pallas kernels for 4%

profile of v4, /device:TPU:201, one launch (start us, length us, event | category | flops | bytes accessed | tf_op | source)
XLA Modules:
  0.0 143.8 jit_solution(17255129167436211911)
XLA Ops:
  0.0 1.8 %shard_map.82 = (f32[16,3,8,128]{3,2,1,0:T(8,128)}, f32[7,2,16,128]{3,2,1,0:T(8,128)}, f32[7,2,16,128]{3,2,1,0:T(8,128)S(1)}, f32[5,4,16,128]{3,2,1,0:T(8,128)S(...) custom-call(f32[5,4,16,128]{3,2,1,0:T(8,128)} %bitcast.9, ...), custom_call_target="tpu_custom_call" | custom-call | bytes 1212416 | tf_op jit(solution)/shard_map/pallas_call | solution.py:58
  1.8 8.5 %all-to-all-start = ((f32[16,3,8,128]{3,2,1,0:T(8,128)}), f32[16,3,8,128]{3,2,1,0:T(8,128)S(1)}, u32[]{:S(2)}, u32[]{:S(2)}) async-start(f32[16,3,8,128]{3,2,1,0:T(8,128)} %get-tuple-element.37), calls=%async_computation | async-start | bytes 393216 | tf_op jit(solution)/shard_map/all_to_all | solution.py:370
  10.3 6.8 %collective-permute-start = (f32[7,2,16,128]{3,2,1,0:T(8,128)}, f32[7,2,16,128]{3,2,1,0:T(8,128)S(1)}, u32[]{:S(2)}, u32[]{:S(2)}) collective-permute-start(f32[7,2,16,128]{3,2,1,0:T(8,128)} %get-tuple-element.35), channel_id=1, source_target_pairs={{1,2},{3,4},{5,6},{7,8},{9,10},{11,12},{13,14},{15,16},{17,18},{19... | collective-permute-start | bytes 344072 | tf_op jit(solution)/shard_map/ppermute | solution.py:366
  17.1 1.9 %collective-permute-start.1 = (f32[7,2,16,128]{3,2,1,0:T(8,128)S(1)}, f32[7,2,16,128]{3,2,1,0:T(8,128)S(1)}, u32[]{:S(2)}, u32[]{:S(2)}) collective-permute-start(f32[7,2,16,128]{3,2,1,0:T(8,128)S(1)} %get-tuple-element.36), channel_id=1, source_target_pairs={{0,1},{2,3},{4,5},{6,7},{8,9},{10,11},{12,13},{14,15},{16,17},{18,... | collective-permute-start | bytes 344072 | tf_op jit(solution)/shard_map/ppermute | solution.py:366
  20.4 1.8 %shard_map.83 = (f32[5,4,16,128]{3,2,1,0:T(8,128)S(1)}, f32[3,5,5,4,16,128]{5,4,3,2,1,0:T(8,128)S(1)}) custom-call(f32[5,4,16,128]{3,2,1,0:T(8,128)} %bitcast.8, f32[3,5,5,4,16,128]{5,4,3,2,1,0:T(8,128)} %bitcast.7), custom_call_target="tpu_custom_call" | custom-call | bytes 5242880 | tf_op jit(solution)/shard_map/pallas_call | solution.py:58
  22.7 18.1 %all_to_all.30.refs_8_ = f32[16,5,4,128]{3,2,1,0:T(4,128)S(1)} all-to-all(f32[16,5,4,128]{3,2,1,0:T(4,128)S(1)} %shard_map.84), channel_id=1, replica_groups=mesh['inst'=16,'cells'=32] {'inst'}, dimensions={0} | all-to-all | bytes 327680 | tf_op jit(solution)/shard_map/all_to_all | solution.py:370
  40.8 1.2 shard_map.85
  42.0 5.0 %collective-permute-start.2 = (f32[5,2,16,128]{3,2,1,0:T(8,128)S(1)}, f32[5,2,16,128]{3,2,1,0:T(8,128)S(1)}, u32[]{:S(2)}, u32[]{:S(2)}) collective-permute-start(f32[5,2,16,128]{3,2,1,0:T(8,128)S(1)} %get-tuple-element.40), channel_id=1, source_target_pairs={{1,2},{3,4},{5,6},{7,8},{9,10},{11,12},{13,14},{15,16},{17,18},{19... | collective-permute-start | bytes 245768 | tf_op jit(solution)/shard_map/ppermute | solution.py:366
  46.9 1.9 %collective-permute-start.3 = (f32[5,2,16,128]{3,2,1,0:T(8,128)S(1)}, f32[5,2,16,128]{3,2,1,0:T(8,128)S(1)}, u32[]{:S(2)}, u32[]{:S(2)}) collective-permute-start(f32[5,2,16,128]{3,2,1,0:T(8,128)S(1)} %get-tuple-element.41), channel_id=1, source_target_pairs={{0,1},{2,3},{4,5},{6,7},{8,9},{10,11},{12,13},{14,15},{16,17},{18,... | collective-permute-start | bytes 245768 | tf_op jit(solution)/shard_map/ppermute | solution.py:366
  48.9 1.0 shard_map.86.refs_4_
  50.4 17.1 %all_to_all.31.refs_3_ = f32[16,5,8,128]{3,2,1,0:T(8,128)S(1)} all-to-all(f32[16,5,8,128]{3,2,1,0:T(8,128)S(1)} %shard_map.87), channel_id=1, replica_groups=mesh['inst'=16,'cells'=32] {'inst'}, dimensions={0} | all-to-all | bytes 655360 | tf_op jit(solution)/shard_map/all_to_all | solution.py:370
  68.0 14.0 %all_to_all.32.back = f32[16,5,8,128]{3,2,1,0:T(8,128)S(1)} all-to-all(f32[16,5,8,128]{3,2,1,0:T(8,128)S(1)} %shard_map.88), channel_id=1, replica_groups=mesh['inst'=16,'cells'=32] {'inst'}, dimensions={0} | all-to-all | bytes 655360 | tf_op jit(solution)/shard_map/all_to_all | solution.py:370
  82.0 7.0 %collective-permute-start.4 = (f32[5,2,16,128]{3,2,1,0:T(8,128)S(1)}, f32[5,2,16,128]{3,2,1,0:T(8,128)S(1)}, u32[]{:S(2)}, u32[]{:S(2)}) collective-permute-start(f32[5,2,16,128]{3,2,1,0:T(8,128)S(1)} %get-tuple-element.44), channel_id=1, source_target_pairs={{1,2},{3,4},{5,6},{7,8},{9,10},{11,12},{13,14},{15,16},{17,18},{19... | collective-permute-start | bytes 245768 | tf_op jit(solution)/shard_map/ppermute | solution.py:366
  89.0 1.9 %collective-permute-start.5 = (f32[5,2,16,128]{3,2,1,0:T(8,128)S(1)}, f32[5,2,16,128]{3,2,1,0:T(8,128)S(1)}, u32[]{:S(2)}, u32[]{:S(2)}) collective-permute-start(f32[5,2,16,128]{3,2,1,0:T(8,128)S(1)} %get-tuple-element.45), channel_id=1, source_target_pairs={{0,1},{2,3},{4,5},{6,7},{8,9},{10,11},{12,13},{14,15},{16,17},{18,... | collective-permute-start | bytes 245768 | tf_op jit(solution)/shard_map/ppermute | solution.py:366
  90.9 1.0 shard_map.90.refs_4_
  92.4 4.7 %collective-permute-start.6 = (f32[5,2,16,128]{3,2,1,0:T(8,128)S(1)}, f32[5,2,16,128]{3,2,1,0:T(8,128)S(1)}, u32[]{:S(2)}, u32[]{:S(2)}) collective-permute-start(f32[5,2,16,128]{3,2,1,0:T(8,128)S(1)} %get-tuple-element.47), channel_id=1, source_target_pairs={{1,2},{3,4},{5,6},{7,8},{9,10},{11,12},{13,14},{15,16},{17,18},{19... | collective-permute-start | bytes 245768 | tf_op jit(solution)/shard_map/ppermute | solution.py:366
  97.1 1.9 %collective-permute-start.7 = (f32[5,2,16,128]{3,2,1,0:T(8,128)S(1)}, f32[5,2,16,128]{3,2,1,0:T(8,128)S(1)}, u32[]{:S(2)}, u32[]{:S(2)}) collective-permute-start(f32[5,2,16,128]{3,2,1,0:T(8,128)S(1)} %get-tuple-element.48), channel_id=1, source_target_pairs={{0,1},{2,3},{4,5},{6,7},{8,9},{10,11},{12,13},{14,15},{16,17},{18,... | collective-permute-start | bytes 245768 | tf_op jit(solution)/shard_map/ppermute | solution.py:366
  99.0 1.0 shard_map.92.refs_4_
  100.4 16.7 %all_to_all.33.refs_3_ = f32[16,5,8,128]{3,2,1,0:T(8,128)S(1)} all-to-all(f32[16,5,8,128]{3,2,1,0:T(8,128)S(1)} %shard_map.93), channel_id=1, replica_groups=mesh['inst'=16,'cells'=32] {'inst'}, dimensions={0} | all-to-all | bytes 655360 | tf_op jit(solution)/shard_map/all_to_all | solution.py:370
  117.5 14.0 %all_to_all.34.back = f32[16,5,8,128]{3,2,1,0:T(8,128)S(1)} all-to-all(f32[16,5,8,128]{3,2,1,0:T(8,128)S(1)} %shard_map.94), channel_id=1, replica_groups=mesh['inst'=16,'cells'=32] {'inst'}, dimensions={0} | all-to-all | bytes 655360 | tf_op jit(solution)/shard_map/all_to_all | solution.py:370
  131.6 8.2 %collective-permute-start.8 = (f32[5,2,16,128]{3,2,1,0:T(8,128)S(1)}, f32[5,2,16,128]{3,2,1,0:T(8,128)S(1)}, u32[]{:S(2)}, u32[]{:S(2)}) collective-permute-start(f32[5,2,16,128]{3,2,1,0:T(8,128)S(1)} %get-tuple-element.51), channel_id=1, source_target_pairs={{1,2},{3,4},{5,6},{7,8},{9,10},{11,12},{13,14},{15,16},{17,18},{19... | collective-permute-start | bytes 245768 | tf_op jit(solution)/shard_map/ppermute | solution.py:366
  139.8 1.9 %collective-permute-start.9 = (f32[5,2,16,128]{3,2,1,0:T(8,128)S(1)}, f32[5,2,16,128]{3,2,1,0:T(8,128)S(1)}, u32[]{:S(2)}, u32[]{:S(2)}) collective-permute-start(f32[5,2,16,128]{3,2,1,0:T(8,128)S(1)} %get-tuple-element.52), channel_id=1, source_target_pairs={{0,1},{2,3},{4,5},{6,7},{8,9},{10,11},{12,13},{14,15},{16,17},{18,... | collective-permute-start | bytes 245768 | tf_op jit(solution)/shard_map/ppermute | solution.py:366
  141.8 1.0 shard_map.96.refs_4_
  143.0 0.8 shard_map.97
  (19 shorter events, 3.2 us)
Async XLA Ops:
  1.8 20.7 %all-to-all-start = ((f32[16,3,8,128]{3,2,1,0:T(8,128)}), f32[16,3,8,128]{3,2,1,0:T(8,128)S(1)}, u32[]{:S(2)}, u32[]{:S(2)}) async-start(f32[16,3,8,128]{3,2,1,0:T(8,128)} %get-tuple-element.37), calls=%async_computation | async-start | bytes 393216 | tf_op jit(solution)/shard_map/all_to_all | solution.py:370
  10.3 12.2 %collective-permute-start = (f32[7,2,16,128]{3,2,1,0:T(8,128)}, f32[7,2,16,128]{3,2,1,0:T(8,128)S(1)}, u32[]{:S(2)}, u32[]{:S(2)}) collective-permute-start(f32[7,2,16,128]{3,2,1,0:T(8,128)} %get-tuple-element.35), channel_id=1, source_target_pairs={{1,2},{3,4},{5,6},{7,8},{9,10},{11,12},{13,14},{15,16},{17,18},{19... | collective-permute-start | bytes 344072 | tf_op jit(solution)/shard_map/ppermute | solution.py:366
  17.1 5.4 %collective-permute-start.1 = (f32[7,2,16,128]{3,2,1,0:T(8,128)S(1)}, f32[7,2,16,128]{3,2,1,0:T(8,128)S(1)}, u32[]{:S(2)}, u32[]{:S(2)}) collective-permute-start(f32[7,2,16,128]{3,2,1,0:T(8,128)S(1)} %get-tuple-element.36), channel_id=1, source_target_pairs={{0,1},{2,3},{4,5},{6,7},{8,9},{10,11},{12,13},{14,15},{16,17},{18,... | collective-permute-start | bytes 344072 | tf_op jit(solution)/shard_map/ppermute | solution.py:366
  42.0 8.3 %collective-permute-start.2 = (f32[5,2,16,128]{3,2,1,0:T(8,128)S(1)}, f32[5,2,16,128]{3,2,1,0:T(8,128)S(1)}, u32[]{:S(2)}, u32[]{:S(2)}) collective-permute-start(f32[5,2,16,128]{3,2,1,0:T(8,128)S(1)} %get-tuple-element.40), channel_id=1, source_target_pairs={{1,2},{3,4},{5,6},{7,8},{9,10},{11,12},{13,14},{15,16},{17,18},{19... | collective-permute-start | bytes 245768 | tf_op jit(solution)/shard_map/ppermute | solution.py:366
  46.9 3.3 %collective-permute-start.3 = (f32[5,2,16,128]{3,2,1,0:T(8,128)S(1)}, f32[5,2,16,128]{3,2,1,0:T(8,128)S(1)}, u32[]{:S(2)}, u32[]{:S(2)}) collective-permute-start(f32[5,2,16,128]{3,2,1,0:T(8,128)S(1)} %get-tuple-element.41), channel_id=1, source_target_pairs={{0,1},{2,3},{4,5},{6,7},{8,9},{10,11},{12,13},{14,15},{16,17},{18,... | collective-permute-start | bytes 245768 | tf_op jit(solution)/shard_map/ppermute | solution.py:366
  82.0 9.9 %collective-permute-start.4 = (f32[5,2,16,128]{3,2,1,0:T(8,128)S(1)}, f32[5,2,16,128]{3,2,1,0:T(8,128)S(1)}, u32[]{:S(2)}, u32[]{:S(2)}) collective-permute-start(f32[5,2,16,128]{3,2,1,0:T(8,128)S(1)} %get-tuple-element.44), channel_id=1, source_target_pairs={{1,2},{3,4},{5,6},{7,8},{9,10},{11,12},{13,14},{15,16},{17,18},{19... | collective-permute-start | bytes 245768 | tf_op jit(solution)/shard_map/ppermute | solution.py:366
  89.0 3.2 %collective-permute-start.5 = (f32[5,2,16,128]{3,2,1,0:T(8,128)S(1)}, f32[5,2,16,128]{3,2,1,0:T(8,128)S(1)}, u32[]{:S(2)}, u32[]{:S(2)}) collective-permute-start(f32[5,2,16,128]{3,2,1,0:T(8,128)S(1)} %get-tuple-element.45), channel_id=1, source_target_pairs={{0,1},{2,3},{4,5},{6,7},{8,9},{10,11},{12,13},{14,15},{16,17},{18,... | collective-permute-start | bytes 245768 | tf_op jit(solution)/shard_map/ppermute | solution.py:366
  92.4 7.9 %collective-permute-start.6 = (f32[5,2,16,128]{3,2,1,0:T(8,128)S(1)}, f32[5,2,16,128]{3,2,1,0:T(8,128)S(1)}, u32[]{:S(2)}, u32[]{:S(2)}) collective-permute-start(f32[5,2,16,128]{3,2,1,0:T(8,128)S(1)} %get-tuple-element.47), channel_id=1, source_target_pairs={{1,2},{3,4},{5,6},{7,8},{9,10},{11,12},{13,14},{15,16},{17,18},{19... | collective-permute-start | bytes 245768 | tf_op jit(solution)/shard_map/ppermute | solution.py:366
  97.1 3.2 %collective-permute-start.7 = (f32[5,2,16,128]{3,2,1,0:T(8,128)S(1)}, f32[5,2,16,128]{3,2,1,0:T(8,128)S(1)}, u32[]{:S(2)}, u32[]{:S(2)}) collective-permute-start(f32[5,2,16,128]{3,2,1,0:T(8,128)S(1)} %get-tuple-element.48), channel_id=1, source_target_pairs={{0,1},{2,3},{4,5},{6,7},{8,9},{10,11},{12,13},{14,15},{16,17},{18,... | collective-permute-start | bytes 245768 | tf_op jit(solution)/shard_map/ppermute | solution.py:366
  131.6 11.1 %collective-permute-start.8 = (f32[5,2,16,128]{3,2,1,0:T(8,128)S(1)}, f32[5,2,16,128]{3,2,1,0:T(8,128)S(1)}, u32[]{:S(2)}, u32[]{:S(2)}) collective-permute-start(f32[5,2,16,128]{3,2,1,0:T(8,128)S(1)} %get-tuple-element.51), channel_id=1, source_target_pairs={{1,2},{3,4},{5,6},{7,8},{9,10},{11,12},{13,14},{15,16},{17,18},{19... | collective-permute-start | bytes 245768 | tf_op jit(solution)/shard_map/ppermute | solution.py:366
  139.8 3.2 %collective-permute-start.9 = (f32[5,2,16,128]{3,2,1,0:T(8,128)S(1)}, f32[5,2,16,128]{3,2,1,0:T(8,128)S(1)}, u32[]{:S(2)}, u32[]{:S(2)}) collective-permute-start(f32[5,2,16,128]{3,2,1,0:T(8,128)S(1)} %get-tuple-element.52), channel_id=1, source_target_pairs={{0,1},{2,3},{4,5},{6,7},{8,9},{10,11},{12,13},{14,15},{16,17},{18,... | collective-permute-start | bytes 245768 | tf_op jit(solution)/shard_map/ppermute | solution.py:366

commit v5 on v4

--- a/solution.py
+++ b/solution.py
@@ -53,7 +53,7 @@
     return pltpu.with_memory_space_constraint(array, pltpu.VMEM)
 
 
-def call(kernel, outs, args, specs=None, scratch=(), flops=0, out_specs=None):
+def call(kernel, outs, args, specs=None, scratch=(), flops=0, out_specs=None, aliases=None):
     size = sum(math.prod(x.shape) for x in list(args) + list(outs)) * 4
     return pl.pallas_call(
         kernel,
@@ -61,6 +61,7 @@
         in_specs=specs or [VMEM] * len(args),
         out_specs=out_specs or [VMEM] * len(outs),
         scratch_shapes=list(scratch),
+        input_output_aliases=aliases or {},
         compiler_params=pltpu.CompilerParams(vmem_limit_bytes=8 * 1024 * 1024),
         cost_estimate=pl.CostEstimate(flops=flops, bytes_accessed=size, transcendentals=0),
     )(*args)
@@ -244,24 +245,34 @@
 
 
 def inner_kernel(
-    factor, adjoint, gradient, step, second, fourth, jacobian, state, *rest
+    factor, on_even, coupled, adjoint, gradient, step, second, fourth, jacobian, state, *rest
 ):
-    coupled, out = rest if len(rest) == 2 else (None, rest[0])
-
-    def base(var, layer, value):
-        residual = value + gradient[var, layer]
-        if coupled is not None:
-            residual = residual + coupled[var, layer]
-        out[var, layer] = adjoint[var, layer] - (factor * step[layer]) * residual
-
-    spatial_yz(state, second, fourth, jacobian, base)
-
-
-def send_kernel(factor, step, jacobian, coefs, state, base, odd, even, message, staged, damped):
+    out = rest[-2]
+
+    @pl.when(even_device() == on_even)
+    def _():
+        def base(var, layer, value):
+            residual = value + gradient[var, layer]
+            if coupled:
+                residual = residual + rest[0][var, layer]
+            out[var, layer] = adjoint[var, layer] - (factor * step[layer]) * residual
+
+        spatial_yz(state, second, fourth, jacobian, base)
+
+
+def chosen(base_odd, base_even):
+    even = even_device()
+    return lambda var, layer: jnp.where(even, base_even[var, layer], base_odd[var, layer])
+
+
+def send_kernel(
+    factor, step, jacobian, coefs, state, base_odd, base_even, odd, even, message, staged, damped
+):
     stage_halos(staged, odd, even)
+    base = chosen(base_odd, base_even)
 
     def finish(var, layer, value):
-        q = base[var, layer] - (factor * step[layer]) * value
+        q = base(var, layer) - (factor * step[layer]) * value
         u = state[var, layer]
         for chunk, rows in quarters(layer):
             message[chunk, var, 0:4, :] = u[rows, :]
@@ -279,28 +290,29 @@
     write_halos(lambda row, layer: state[row, layer], odd_ref, even_ref, VARS)
 
 
-def update_kernel(
-    factor, step, jacobian, coefs, state, base, odd, even, out, odd_ref, even_ref, staged, damped
-):
+def update_kernel(factor, step, jacobian, coefs, state, base_odd, base_even, odd, even, *rest):
+    out, odd_ref, even_ref, staged, damped = rest[-5:]
     stage_halos(staged, odd, even)
+    base = chosen(base_odd, base_even)
 
     def finish(var, layer, value):
-        out[var, layer] = base[var, layer] - (factor * step[layer]) * value
+        out[var, layer] = base(var, layer) - (factor * step[layer]) * value
 
     spatial_x(state, staged, coefs, jacobian, damped, finish)
     write_halos(lambda row, layer: out[row, layer], odd_ref, even_ref, VARS)
 
 
-def last_kernel(
-    factor, step, jacobian, coefs, state, base, odd, even, out, staged, damped, result, sems
-):
+def last_kernel(factor, step, jacobian, coefs, state, base_odd, base_even, odd, even, *rest):
+    out, staged, damped, result, sems = rest[-5:]
     stage_halos(staged, odd, even)
     copies = [
         pltpu.make_async_copy(result.at[var], out.at[var], sems.at[var]) for var in range(VARS)
     ]
 
+    base = chosen(base_odd, base_even)
+
     def finish(var, layer, value):
-        result[var, layer] = base[var, layer] - (factor * step[layer]) * value
+        result[var, layer] = base(var, layer) - (factor * step[layer]) * value
         if layer == LAYERS - 1:
             copies[var].start()
 
@@ -418,22 +430,31 @@
         flops=work,
     )
 
-    def inner(factor, operands):
+    def inner(factor, on_even, operands, sent):
+        arrays = fixed + operands
         return call(
-            lambda *refs: inner_kernel(factor, *refs),
-            [shape(*FIELD)],
-            fixed + operands,
+            lambda *refs: inner_kernel(factor, on_even, len(operands) == 2, *refs),
+            [shape(*FIELD), shape(*HALO)],
+            arrays + [sent],
+            [VMEM] * len(arrays) + [ANY],
             flops=work,
+            out_specs=[VMEM, ANY],
+            aliases={len(arrays): 1},
         )
+
+    def neighbours(factor, operands, odd, even):
+        base_odd, odd = inner(factor, False, operands, odd)
+        odd = lax.ppermute(odd, "cells", PAIRS_ODD)
+        base_even, even = inner(factor, True, operands, even)
+        return base_odd, base_even, odd, lax.ppermute(even, "cells", PAIRS_EVEN)
 
     for section in (1, 3):
         factor = FACTORS[section]
-        odd, even = exchange(odd, even)
-        base = inner(factor, [state])
+        arrived = neighbours(factor, [state], odd, even)
         (message,) = call(
             lambda *refs: send_kernel(factor, *refs),
             [shape(INSTANCES, VARS, 8, NZ)],
-            [step, jacobian, coefs, state, *base, odd, even],
+            [step, jacobian, coefs, state, *arrived],
             scratch=scratch,
             flops=work,
         )
@@ -448,14 +469,16 @@
             unpack_kernel, [shape(*FIELD), shape(*FIELD)] + halos, [across(message)]
         )
         factor = FACTORS[section + 1]
-        odd, even = exchange(odd, even)
-        base = inner(factor, [state, coupled])
-        operands = [step, jacobian, coefs, state, *base, odd, even]
+        arrived = neighbours(factor, [state, coupled], odd, even)
+        operands = [step, jacobian, coefs, state, *arrived, coupled]
+        operands += [adjoint, gradient, second, fourth]
+        specs = [VMEM] * 8 + [ANY] * 5
         if section == 1:
             state, odd, even = call(
                 lambda *refs: update_kernel(factor, *refs),
                 [shape(*FIELD)] + halos,
                 operands,
+                specs,
                 scratch=scratch,
                 flops=work,
             )
@@ -463,6 +486,7 @@
         lambda *refs: last_kernel(factor, *refs),
         [shape(*FIELD)],
         operands,
+        specs,
         scratch=scratch + (pltpu.VMEM(FIELD, F32), pltpu.SemaphoreType.DMA((VARS,))),
         flops=work,
         out_specs=[HBM],

time: 145 us -> 148 us (1.021)
  waiting for transfers between devices: 1.54 us -> 7.41 us
  starting transfers between devices: 49.7 us -> 46 us
  blocking collectives: 79.9 us -> 81.4 us
    ppermute x0 -> x8, starting transfers between devices: none -> 28.8 us  [the longest x4 21.1 us: neighbours(): odd = lax.ppermute(odd, 'cells', PAIRS_ODD)]
    ppermute x5 -> x1, starting transfers between devices: 31.6 us -> 6.84 us  [exchange(): lax.ppermute(odd, 'cells', PAIRS_ODD)]
    ppermute x5 -> x1, starting transfers between devices: 9.6 us -> 1.92 us  [exchange(): lax.ppermute(even, 'cells', PAIRS_EVEN)]
    ppermute x0 -> x8, waiting for transfers between devices: none -> 7.06 us  [the longest x4 5.47 us: neighbours(): odd = lax.ppermute(odd, 'cells', PAIRS_ODD)]
    all_to_all x5, blocking collectives: 79.9 us -> 81.4 us  [across(): return lax.all_to_all(message, 'inst', 0, 0, tiled=True)]
    pallas_call x16 -> x20, Pallas kernels: 11.1 us -> 11.3 us  [call(): pl.pallas_call(kernel, out_shape=outs, in_specs=specs or [VMEM] * len(arg...]
  transfers between devices with their start and end apart: 11 -> 11, of which waited for: 5 -> 7; matrix products, arithmetic and copies ran while one was open for 0% -> 0% of each run, Pallas kernels for 4% -> 1%
where the time goes in v5:
time: 148 us
  blocking collectives  81.4 us (55%)
  starting transfers between devices  46 us (31%)
  Pallas kernels  11.3 us (8%)
  waiting for transfers between devices  7.41 us (5%)
  between operations  1.52 us (1%)
    all_to_all x5, blocking collectives, across(): return lax.all_to_all(message, 'inst', 0, 0, tiled=True)  81.4 us
    ppermute x4, starting transfers between devices, neighbours(): odd = lax.ppermute(odd, 'cells', PAIRS_ODD)  21.1 us
    pallas_call x20, Pallas kernels, call(): pl.pallas_call(kernel, out_shape=outs, in_specs=specs or [VMEM] * len(arg...  11.3 us
    all_to_all x1, starting transfers between devices, across(): return lax.all_to_all(message, 'inst', 0, 0, tiled=True)  8.5 us
    ppermute x4, starting transfers between devices, neighbours(): return (base_odd, base_even, odd, lax.ppermute(even, 'cells', PAIRS_EVEN))  7.68 us
    ppermute x1, starting transfers between devices, exchange(): lax.ppermute(odd, 'cells', PAIRS_ODD)  6.84 us
    ppermute x4, waiting for transfers between devices, neighbours(): odd = lax.ppermute(odd, 'cells', PAIRS_ODD)  5.47 us
  transfers between devices with their start and end apart: 11, of which 7 were waited for; matrix products, arithmetic and copies ran while one was open for 0% of the time, Pallas kernels for 1%

profile of v5, /device:TPU:201, one launch (start us, length us, event | category | flops | bytes accessed | tf_op | source)
XLA Modules:
  0.0 147.6 jit_solution(18275915544858168083)
XLA Ops:
  0.0 1.8 %shard_map.82 = (f32[16,3,8,128]{3,2,1,0:T(8,128)}, f32[7,2,16,128]{3,2,1,0:T(8,128)}, f32[7,2,16,128]{3,2,1,0:T(8,128)S(1)}, f32[5,4,16,128]{3,2,1,0:T(8,128)S(...) custom-call(f32[5,4,16,128]{3,2,1,0:T(8,128)} %bitcast.9, ...), custom_call_target="tpu_custom_call" | custom-call | bytes 1212416 | tf_op jit(solution)/shard_map/pallas_call | solution.py:58
  1.8 8.5 %all-to-all-start = ((f32[16,3,8,128]{3,2,1,0:T(8,128)}), f32[16,3,8,128]{3,2,1,0:T(8,128)S(1)}, u32[]{:S(2)}, u32[]{:S(2)}) async-start(f32[16,3,8,128]{3,2,1,0:T(8,128)} %get-tuple-element.53), calls=%async_computation | async-start | bytes 393216 | tf_op jit(solution)/shard_map/all_to_all | solution.py:382
  10.3 6.8 %collective-permute-start = (f32[7,2,16,128]{3,2,1,0:T(8,128)}, f32[7,2,16,128]{3,2,1,0:T(8,128)S(1)}, u32[]{:S(2)}, u32[]{:S(2)}) collective-permute-start(f32[7,2,16,128]{3,2,1,0:T(8,128)} %get-tuple-element.51), channel_id=1, source_target_pairs={{1,2},{3,4},{5,6},{7,8},{9,10},{11,12},{13,14},{15,16},{17,18},{19... | collective-permute-start | bytes 344072 | tf_op jit(solution)/shard_map/ppermute | solution.py:378
  17.1 1.9 %collective-permute-start.1 = (f32[7,2,16,128]{3,2,1,0:T(8,128)S(1)}, f32[7,2,16,128]{3,2,1,0:T(8,128)S(1)}, u32[]{:S(2)}, u32[]{:S(2)}) collective-permute-start(f32[7,2,16,128]{3,2,1,0:T(8,128)S(1)} %get-tuple-element.52), channel_id=1, source_target_pairs={{0,1},{2,3},{4,5},{6,7},{8,9},{10,11},{12,13},{14,15},{16,17},{18,... | collective-permute-start | bytes 344072 | tf_op jit(solution)/shard_map/ppermute | solution.py:378
  20.4 1.8 %shard_map.83 = (f32[5,4,16,128]{3,2,1,0:T(8,128)S(1)}, f32[3,5,5,4,16,128]{5,4,3,2,1,0:T(8,128)S(1)}) custom-call(f32[5,4,16,128]{3,2,1,0:T(8,128)} %bitcast.8, f32[3,5,5,4,16,128]{5,4,3,2,1,0:T(8,128)} %bitcast.7), custom_call_target="tpu_custom_call" | custom-call | bytes 5242880 | tf_op jit(solution)/shard_map/pallas_call | solution.py:58
  22.7 18.1 %all_to_all.30.refs_8_ = f32[16,5,4,128]{3,2,1,0:T(4,128)S(1)} all-to-all(f32[16,5,4,128]{3,2,1,0:T(4,128)S(1)} %shard_map.84), channel_id=1, replica_groups=mesh['inst'=16,'cells'=32] {'inst'}, dimensions={0} | all-to-all | bytes 327680 | tf_op jit(solution)/shard_map/all_to_all | solution.py:382
  40.8 1.2 shard_map.85
  42.9 4.0 %collective-permute-start.2 = (f32[5,2,16,128]{3,2,1,0:T(8,128)S(1)}, f32[5,2,16,128]{3,2,1,0:T(8,128)S(1)}, u32[]{:S(2)}, u32[]{:S(2)}) collective-permute-start(f32[5,2,16,128]{3,2,1,0:T(8,128)S(1)} %get-tuple-element.60), channel_id=1, source_target_pairs={{1,2},{3,4},{5,6},{7,8},{9,10},{11,12},{13,14},{15,16},{17,18},{19... | collective-permute-start | bytes 245768 | tf_op jit(solution)/shard_map/ppermute | solution.py:447
  47.0 1.9 %collective-permute-start.3 = (f32[5,2,16,128]{3,2,1,0:T(8,128)S(1)}, f32[5,2,16,128]{3,2,1,0:T(8,128)S(1)}, u32[]{:S(2)}, u32[]{:S(2)}) collective-permute-start(f32[5,2,16,128]{3,2,1,0:T(8,128)S(1)} %get-tuple-element.61), channel_id=1, source_target_pairs={{0,1},{2,3},{4,5},{6,7},{8,9},{10,11},{12,13},{14,15},{16,17},{18,... | collective-permute-start | bytes 245768 | tf_op jit(solution)/shard_map/ppermute | solution.py:449
  48.9 2.4 %collective-permute-done.2.refs_6_ = f32[5,2,16,128]{3,2,1,0:T(8,128)S(1)} collective-permute-done((f32[5,2,16,128]{3,2,1,0:T(8,128)S(1)}, f32[5,2,16,128]{3,2,1,0:T(8,128)S(1)}, u32[]{:S(2)}, u32[]{:S(2)}) %collective-permute-start.2) | collective-permute-done | bytes 81952 | tf_op jit(solution)/shard_map/ppermute | solution.py:447
  51.5 16.1 %all_to_all.31.refs_3_ = f32[16,5,8,128]{3,2,1,0:T(8,128)S(1)} all-to-all(f32[16,5,8,128]{3,2,1,0:T(8,128)S(1)} %shard_map.88), channel_id=1, replica_groups=mesh['inst'=16,'cells'=32] {'inst'}, dimensions={0} | all-to-all | bytes 655360 | tf_op jit(solution)/shard_map/all_to_all | solution.py:382
  68.0 15.3 %all_to_all.32.back = f32[16,5,8,128]{3,2,1,0:T(8,128)S(1)} all-to-all(f32[16,5,8,128]{3,2,1,0:T(8,128)S(1)} %shard_map.89), channel_id=1, replica_groups=mesh['inst'=16,'cells'=32] {'inst'}, dimensions={0} | all-to-all | bytes 655360 | tf_op jit(solution)/shard_map/all_to_all | solution.py:382
  83.3 1.0 shard_map.91
  84.3 6.9 %collective-permute-start.4 = (f32[5,2,16,128]{3,2,1,0:T(8,128)S(1)}, f32[5,2,16,128]{3,2,1,0:T(8,128)S(1)}, u32[]{:S(2)}, u32[]{:S(2)}) collective-permute-start(f32[5,2,16,128]{3,2,1,0:T(8,128)S(1)} %get-tuple-element.68), channel_id=1, source_target_pairs={{1,2},{3,4},{5,6},{7,8},{9,10},{11,12},{13,14},{15,16},{17,18},{19... | collective-permute-start | bytes 245768 | tf_op jit(solution)/shard_map/ppermute | solution.py:447
  91.2 1.9 %collective-permute-start.5 = (f32[5,2,16,128]{3,2,1,0:T(8,128)S(1)}, f32[5,2,16,128]{3,2,1,0:T(8,128)S(1)}, u32[]{:S(2)}, u32[]{:S(2)}) collective-permute-start(f32[5,2,16,128]{3,2,1,0:T(8,128)S(1)} %get-tuple-element.69), channel_id=1, source_target_pairs={{0,1},{2,3},{4,5},{6,7},{8,9},{10,11},{12,13},{14,15},{16,17},{18,... | collective-permute-start | bytes 245768 | tf_op jit(solution)/shard_map/ppermute | solution.py:449
  95.6 3.7 %collective-permute-start.6 = (f32[5,2,16,128]{3,2,1,0:T(8,128)S(1)}, f32[5,2,16,128]{3,2,1,0:T(8,128)S(1)}, u32[]{:S(2)}, u32[]{:S(2)}) collective-permute-start(f32[5,2,16,128]{3,2,1,0:T(8,128)S(1)} %get-tuple-element.75), channel_id=1, source_target_pairs={{1,2},{3,4},{5,6},{7,8},{9,10},{11,12},{13,14},{15,16},{17,18},{19... | collective-permute-start | bytes 245768 | tf_op jit(solution)/shard_map/ppermute | solution.py:447
  99.3 1.9 %collective-permute-start.7 = (f32[5,2,16,128]{3,2,1,0:T(8,128)S(1)}, f32[5,2,16,128]{3,2,1,0:T(8,128)S(1)}, u32[]{:S(2)}, u32[]{:S(2)}) collective-permute-start(f32[5,2,16,128]{3,2,1,0:T(8,128)S(1)} %get-tuple-element.76), channel_id=1, source_target_pairs={{0,1},{2,3},{4,5},{6,7},{8,9},{10,11},{12,13},{14,15},{16,17},{18,... | collective-permute-start | bytes 245768 | tf_op jit(solution)/shard_map/ppermute | solution.py:449
  101.3 2.2 %collective-permute-done.6.refs_6_ = f32[5,2,16,128]{3,2,1,0:T(8,128)S(1)} collective-permute-done((f32[5,2,16,128]{3,2,1,0:T(8,128)S(1)}, f32[5,2,16,128]{3,2,1,0:T(8,128)S(1)}, u32[]{:S(2)}, u32[]{:S(2)}) %collective-permute-start.6) | collective-permute-done | bytes 81952 | tf_op jit(solution)/shard_map/ppermute | solution.py:447
  103.6 15.3 %all_to_all.33.refs_3_ = f32[16,5,8,128]{3,2,1,0:T(8,128)S(1)} all-to-all(f32[16,5,8,128]{3,2,1,0:T(8,128)S(1)} %shard_map.96), channel_id=1, replica_groups=mesh['inst'=16,'cells'=32] {'inst'}, dimensions={0} | all-to-all | bytes 655360 | tf_op jit(solution)/shard_map/all_to_all | solution.py:382
  119.4 16.6 %all_to_all.34.back = f32[16,5,8,128]{3,2,1,0:T(8,128)S(1)} all-to-all(f32[16,5,8,128]{3,2,1,0:T(8,128)S(1)} %shard_map.97), channel_id=1, replica_groups=mesh['inst'=16,'cells'=32] {'inst'}, dimensions={0} | all-to-all | bytes 655360 | tf_op jit(solution)/shard_map/all_to_all | solution.py:382
  136.1 1.0 shard_map.99
  137.1 6.5 %collective-permute-start.8 = (f32[5,2,16,128]{3,2,1,0:T(8,128)S(1)}, f32[5,2,16,128]{3,2,1,0:T(8,128)S(1)}, u32[]{:S(2)}, u32[]{:S(2)}) collective-permute-start(f32[5,2,16,128]{3,2,1,0:T(8,128)S(1)} %get-tuple-element.83), channel_id=1, source_target_pairs={{1,2},{3,4},{5,6},{7,8},{9,10},{11,12},{13,14},{15,16},{17,18},{19... | collective-permute-start | bytes 245768 | tf_op jit(solution)/shard_map/ppermute | solution.py:447
  143.6 1.9 %collective-permute-start.9 = (f32[5,2,16,128]{3,2,1,0:T(8,128)S(1)}, f32[5,2,16,128]{3,2,1,0:T(8,128)S(1)}, u32[]{:S(2)}, u32[]{:S(2)}) collective-permute-start(f32[5,2,16,128]{3,2,1,0:T(8,128)S(1)} %get-tuple-element.84), channel_id=1, source_target_pairs={{0,1},{2,3},{4,5},{6,7},{8,9},{10,11},{12,13},{14,15},{16,17},{18,... | collective-permute-start | bytes 245768 | tf_op jit(solution)/shard_map/ppermute | solution.py:449
  145.7 1.1 collective-permute-done.9.refs_7_
  (23 shorter events, 6.3 us)
Async XLA Ops:
  1.8 20.7 %all-to-all-start = ((f32[16,3,8,128]{3,2,1,0:T(8,128)}), f32[16,3,8,128]{3,2,1,0:T(8,128)S(1)}, u32[]{:S(2)}, u32[]{:S(2)}) async-start(f32[16,3,8,128]{3,2,1,0:T(8,128)} %get-tuple-element.53), calls=%async_computation | async-start | bytes 393216 | tf_op jit(solution)/shard_map/all_to_all | solution.py:382
  10.3 12.2 %collective-permute-start = (f32[7,2,16,128]{3,2,1,0:T(8,128)}, f32[7,2,16,128]{3,2,1,0:T(8,128)S(1)}, u32[]{:S(2)}, u32[]{:S(2)}) collective-permute-start(f32[7,2,16,128]{3,2,1,0:T(8,128)} %get-tuple-element.51), channel_id=1, source_target_pairs={{1,2},{3,4},{5,6},{7,8},{9,10},{11,12},{13,14},{15,16},{17,18},{19... | collective-permute-start | bytes 344072 | tf_op jit(solution)/shard_map/ppermute | solution.py:378
  17.1 5.4 %collective-permute-start.1 = (f32[7,2,16,128]{3,2,1,0:T(8,128)S(1)}, f32[7,2,16,128]{3,2,1,0:T(8,128)S(1)}, u32[]{:S(2)}, u32[]{:S(2)}) collective-permute-start(f32[7,2,16,128]{3,2,1,0:T(8,128)S(1)} %get-tuple-element.52), channel_id=1, source_target_pairs={{0,1},{2,3},{4,5},{6,7},{8,9},{10,11},{12,13},{14,15},{16,17},{18,... | collective-permute-start | bytes 344072 | tf_op jit(solution)/shard_map/ppermute | solution.py:378
  42.9 8.4 %collective-permute-start.2 = (f32[5,2,16,128]{3,2,1,0:T(8,128)S(1)}, f32[5,2,16,128]{3,2,1,0:T(8,128)S(1)}, u32[]{:S(2)}, u32[]{:S(2)}) collective-permute-start(f32[5,2,16,128]{3,2,1,0:T(8,128)S(1)} %get-tuple-element.60), channel_id=1, source_target_pairs={{1,2},{3,4},{5,6},{7,8},{9,10},{11,12},{13,14},{15,16},{17,18},{19... | collective-permute-start | bytes 245768 | tf_op jit(solution)/shard_map/ppermute | solution.py:447
  47.0 4.3 %collective-permute-start.3 = (f32[5,2,16,128]{3,2,1,0:T(8,128)S(1)}, f32[5,2,16,128]{3,2,1,0:T(8,128)S(1)}, u32[]{:S(2)}, u32[]{:S(2)}) collective-permute-start(f32[5,2,16,128]{3,2,1,0:T(8,128)S(1)} %get-tuple-element.61), channel_id=1, source_target_pairs={{0,1},{2,3},{4,5},{6,7},{8,9},{10,11},{12,13},{14,15},{16,17},{18,... | collective-permute-start | bytes 245768 | tf_op jit(solution)/shard_map/ppermute | solution.py:449
  84.3 9.6 %collective-permute-start.4 = (f32[5,2,16,128]{3,2,1,0:T(8,128)S(1)}, f32[5,2,16,128]{3,2,1,0:T(8,128)S(1)}, u32[]{:S(2)}, u32[]{:S(2)}) collective-permute-start(f32[5,2,16,128]{3,2,1,0:T(8,128)S(1)} %get-tuple-element.68), channel_id=1, source_target_pairs={{1,2},{3,4},{5,6},{7,8},{9,10},{11,12},{13,14},{15,16},{17,18},{19... | collective-permute-start | bytes 245768 | tf_op jit(solution)/shard_map/ppermute | solution.py:447
  91.2 3.2 %collective-permute-start.5 = (f32[5,2,16,128]{3,2,1,0:T(8,128)S(1)}, f32[5,2,16,128]{3,2,1,0:T(8,128)S(1)}, u32[]{:S(2)}, u32[]{:S(2)}) collective-permute-start(f32[5,2,16,128]{3,2,1,0:T(8,128)S(1)} %get-tuple-element.69), channel_id=1, source_target_pairs={{0,1},{2,3},{4,5},{6,7},{8,9},{10,11},{12,13},{14,15},{16,17},{18,... | collective-permute-start | bytes 245768 | tf_op jit(solution)/shard_map/ppermute | solution.py:449
  95.6 7.9 %collective-permute-start.6 = (f32[5,2,16,128]{3,2,1,0:T(8,128)S(1)}, f32[5,2,16,128]{3,2,1,0:T(8,128)S(1)}, u32[]{:S(2)}, u32[]{:S(2)}) collective-permute-start(f32[5,2,16,128]{3,2,1,0:T(8,128)S(1)} %get-tuple-element.75), channel_id=1, source_target_pairs={{1,2},{3,4},{5,6},{7,8},{9,10},{11,12},{13,14},{15,16},{17,18},{19... | collective-permute-start | bytes 245768 | tf_op jit(solution)/shard_map/ppermute | solution.py:447
  99.3 4.1 %collective-permute-start.7 = (f32[5,2,16,128]{3,2,1,0:T(8,128)S(1)}, f32[5,2,16,128]{3,2,1,0:T(8,128)S(1)}, u32[]{:S(2)}, u32[]{:S(2)}) collective-permute-start(f32[5,2,16,128]{3,2,1,0:T(8,128)S(1)} %get-tuple-element.76), channel_id=1, source_target_pairs={{0,1},{2,3},{4,5},{6,7},{8,9},{10,11},{12,13},{14,15},{16,17},{18,... | collective-permute-start | bytes 245768 | tf_op jit(solution)/shard_map/ppermute | solution.py:449
  137.1 8.6 %collective-permute-start.8 = (f32[5,2,16,128]{3,2,1,0:T(8,128)S(1)}, f32[5,2,16,128]{3,2,1,0:T(8,128)S(1)}, u32[]{:S(2)}, u32[]{:S(2)}) collective-permute-start(f32[5,2,16,128]{3,2,1,0:T(8,128)S(1)} %get-tuple-element.83), channel_id=1, source_target_pairs={{1,2},{3,4},{5,6},{7,8},{9,10},{11,12},{13,14},{15,16},{17,18},{19... | collective-permute-start | bytes 245768 | tf_op jit(solution)/shard_map/ppermute | solution.py:447
  143.6 3.2 %collective-permute-start.9 = (f32[5,2,16,128]{3,2,1,0:T(8,128)S(1)}, f32[5,2,16,128]{3,2,1,0:T(8,128)S(1)}, u32[]{:S(2)}, u32[]{:S(2)}) collective-permute-start(f32[5,2,16,128]{3,2,1,0:T(8,128)S(1)} %get-tuple-element.84), channel_id=1, source_target_pairs={{0,1},{2,3},{4,5},{6,7},{8,9},{10,11},{12,13},{14,15},{16,17},{18,... | collective-permute-start | bytes 245768 | tf_op jit(solution)/shard_map/ppermute | solution.py:449

commit v6 on v4

--- a/solution.py
+++ b/solution.py
@@ -28,6 +28,9 @@
 PAIRS_ODD = [(i, i + 1) for i in range(1, DEVICES - 1, 2)] + [
     (i + 1, i) for i in range(1, DEVICES - 1, 2)
 ]
+
+ORDER = (9, 12, 5, 8, 14, 1, 13, 4, 6, 0, 11, 7, 2, 3, 10, 15)
+PLACE = [ORDER.index(j) for j in range(INSTANCES)]
 
 FIELD = (VARS, LAYERS, NY, NZ)
 HALO = (VARS, 2, NY, NZ)
@@ -337,11 +340,11 @@
     out = rest[-1]
     weights = weights_of(frequency[0], damping[0])
     for index in range(received.shape[1]):
-        values = [received[j, index] for j in range(INSTANCES)]
+        values = [received[PLACE[j], index] for j in range(INSTANCES)]
         for k, value in enumerate(combine(weights, values, 1)):
-            out[k, 2 * index] = value[0:4, :]
+            out[PLACE[k], 2 * index] = value[0:4, :]
             if 2 * index + 1 < VARS:
-                out[k, 2 * index + 1] = value[4:8, :]
+                out[PLACE[k], 2 * index + 1] = value[4:8, :]
 
 
 def middle_kernel(factor, frequency, damping, steps, received, out):
@@ -349,14 +352,14 @@
     weights = weights_of(frequency[0], damping[0])
 
     def tile(index, carry):
-        values = [received[j, index] for j in range(INSTANCES)]
+        values = [received[PLACE[j], index] for j in range(INSTANCES)]
         first = combine(weights, values, 1)
         moved = [
-            values[k] - (factor * steps[k, 2]) * pltpu.roll(first[k], 4, 0)
+            values[k] - (factor * steps[PLACE[k], 2]) * pltpu.roll(first[k], 4, 0)
             for k in range(INSTANCES)
         ]
         for k, value in enumerate(combine(weights, moved, 1)):
-            out[k, index] = jnp.where(low, pltpu.roll(value, 4, 0), moved[k])
+            out[PLACE[k], index] = jnp.where(low, pltpu.roll(value, 4, 0), moved[k])
         return carry
 
     lax.fori_loop(0, VARS, tile, 0)
@@ -367,7 +370,7 @@
 
 
 def across(message):
-    return lax.all_to_all(message, "inst", 0, 0, tiled=True)
+    return lax.all_to_all(message, "inst", 0, 0, axis_index_groups=[ORDER], tiled=True)
 
 
 def on_device(

time: 145 us -> 140 us (0.966)
  blocking collectives: 79.9 us -> 76.6 us
    all_to_all x5, blocking collectives: 79.9 us -> 76.6 us  [across(): lax.all_to_all(message, 'inst', 0, 0, axis_index_groups=[ORDER], tiled=True)]
    ppermute x5, starting transfers between devices: 31.6 us -> 29.5 us  [exchange(): lax.ppermute(odd, 'cells', PAIRS_ODD)]
  transfers between devices with their start and end apart: 11 -> 11, of which waited for: 5 -> 4; matrix products, arithmetic and copies ran while one was open for 0% -> 0% of each run, Pallas kernels for 4% -> 4%
where the time goes in v6:
time: 140 us; the launch traced here: 139 us
  blocking collectives  76.6 us (55%)
  starting transfers between devices  48.5 us (35%)
  Pallas kernels  11.1 us (8%)
  waiting for transfers between devices  1.78 us (1%)
  between operations  1.51 us (1%)
    all_to_all x5, blocking collectives, across(): lax.all_to_all(message, 'inst', 0, 0, axis_index_groups=[ORDER], tiled=True)  76.6 us
    ppermute x5, starting transfers between devices, exchange(): lax.ppermute(odd, 'cells', PAIRS_ODD)  29.5 us
    pallas_call x16, Pallas kernels, call(): pl.pallas_call(kernel, out_shape=outs, in_specs=specs or [VMEM] * len(arg...  11.1 us
    ppermute x5, starting transfers between devices, exchange(): lax.ppermute(even, 'cells', PAIRS_EVEN)  9.6 us
    all_to_all x1, starting transfers between devices, across(): lax.all_to_all(message, 'inst', 0, 0, axis_index_groups=[ORDER], tiled=True)  9.39 us
  transfers between devices with their start and end apart: 11, of which 4 were waited for; matrix products, arithmetic and copies ran while one was open for 0% of the time, Pallas kernels for 4%

profile of v6, /device:TPU:201, one launch (start us, length us, event | category | flops | bytes accessed | tf_op | source)
XLA Modules:
  0.0 139.5 jit_solution(2391056888992510963)
XLA Ops:
  0.0 1.8 %shard_map.82 = (f32[16,3,8,128]{3,2,1,0:T(8,128)}, f32[7,2,16,128]{3,2,1,0:T(8,128)}, f32[7,2,16,128]{3,2,1,0:T(8,128)S(1)}, f32[5,4,16,128]{3,2,1,0:T(8,128)S(...) custom-call(f32[5,4,16,128]{3,2,1,0:T(8,128)} %bitcast.9, ...), custom_call_target="tpu_custom_call" | custom-call | bytes 1212416 | tf_op jit(solution)/shard_map/pallas_call | solution.py:61
  1.8 9.4 %all-to-all-start = ((f32[16,3,8,128]{3,2,1,0:T(8,128)}), f32[16,3,8,128]{3,2,1,0:T(8,128)S(1)}, u32[]{:S(2)}, u32[]{:S(2)}) async-start(f32[16,3,8,128]{3,2,1,0:T(8,128)} %get-tuple-element.37), calls=%async_computation | async-start | bytes 393216 | tf_op jit(solution)/shard_map/all_to_all | solution.py:373
  11.2 6.7 %collective-permute-start = (f32[7,2,16,128]{3,2,1,0:T(8,128)}, f32[7,2,16,128]{3,2,1,0:T(8,128)S(1)}, u32[]{:S(2)}, u32[]{:S(2)}) collective-permute-start(f32[7,2,16,128]{3,2,1,0:T(8,128)} %get-tuple-element.35), channel_id=1, source_target_pairs={{1,2},{3,4},{5,6},{7,8},{9,10},{11,12},{13,14},{15,16},{17,18},{19... | collective-permute-start | bytes 344072 | tf_op jit(solution)/shard_map/ppermute | solution.py:369
  17.9 1.9 %collective-permute-start.1 = (f32[7,2,16,128]{3,2,1,0:T(8,128)S(1)}, f32[7,2,16,128]{3,2,1,0:T(8,128)S(1)}, u32[]{:S(2)}, u32[]{:S(2)}) collective-permute-start(f32[7,2,16,128]{3,2,1,0:T(8,128)S(1)} %get-tuple-element.36), channel_id=1, source_target_pairs={{0,1},{2,3},{4,5},{6,7},{8,9},{10,11},{12,13},{14,15},{16,17},{18,... | collective-permute-start | bytes 344072 | tf_op jit(solution)/shard_map/ppermute | solution.py:369
  21.1 1.8 %shard_map.83 = (f32[5,4,16,128]{3,2,1,0:T(8,128)S(1)}, f32[3,5,5,4,16,128]{5,4,3,2,1,0:T(8,128)S(1)}) custom-call(f32[5,4,16,128]{3,2,1,0:T(8,128)} %bitcast.8, f32[3,5,5,4,16,128]{5,4,3,2,1,0:T(8,128)} %bitcast.7), custom_call_target="tpu_custom_call" | custom-call | bytes 5242880 | tf_op jit(solution)/shard_map/pallas_call | solution.py:61
  23.1 13.6 %all_to_all.30.refs_8_ = f32[16,5,4,128]{3,2,1,0:T(4,128)S(1)} all-to-all(f32[16,5,4,128]{3,2,1,0:T(4,128)S(1)} %shard_map.84), channel_id=1, replica_groups={{288,384,160,256,448,32,416,128,192,0,352,224,64,96,320,480},{289,385,1..., dimensions={0} | all-to-all | bytes 327680 | tf_op jit(solution)/shard_map/all_to_all | solution.py:373
  36.6 1.2 shard_map.85
  37.8 5.1 %collective-permute-start.2 = (f32[5,2,16,128]{3,2,1,0:T(8,128)S(1)}, f32[5,2,16,128]{3,2,1,0:T(8,128)S(1)}, u32[]{:S(2)}, u32[]{:S(2)}) collective-permute-start(f32[5,2,16,128]{3,2,1,0:T(8,128)S(1)} %get-tuple-element.40), channel_id=1, source_target_pairs={{1,2},{3,4},{5,6},{7,8},{9,10},{11,12},{13,14},{15,16},{17,18},{19... | collective-permute-start | bytes 245768 | tf_op jit(solution)/shard_map/ppermute | solution.py:369
  42.9 1.9 %collective-permute-start.3 = (f32[5,2,16,128]{3,2,1,0:T(8,128)S(1)}, f32[5,2,16,128]{3,2,1,0:T(8,128)S(1)}, u32[]{:S(2)}, u32[]{:S(2)}) collective-permute-start(f32[5,2,16,128]{3,2,1,0:T(8,128)S(1)} %get-tuple-element.41), channel_id=1, source_target_pairs={{0,1},{2,3},{4,5},{6,7},{8,9},{10,11},{12,13},{14,15},{16,17},{18,... | collective-permute-start | bytes 245768 | tf_op jit(solution)/shard_map/ppermute | solution.py:369
  44.9 1.0 shard_map.86.refs_4_
  46.5 17.4 %all_to_all.31.refs_3_ = f32[16,5,8,128]{3,2,1,0:T(8,128)S(1)} all-to-all(f32[16,5,8,128]{3,2,1,0:T(8,128)S(1)} %shard_map.87), channel_id=1, replica_groups={{288,384,160,256,448,32,416,128,192,0,352,224,64,96,320,480},{289,385,1..., dimensions={0} | all-to-all | bytes 655360 | tf_op jit(solution)/shard_map/all_to_all | solution.py:373
  64.4 16.5 %all_to_all.32.back = f32[16,5,8,128]{3,2,1,0:T(8,128)S(1)} all-to-all(f32[16,5,8,128]{3,2,1,0:T(8,128)S(1)} %shard_map.88), channel_id=1, replica_groups={{288,384,160,256,448,32,416,128,192,0,352,224,64,96,320,480},{289,385,1..., dimensions={0} | all-to-all | bytes 655360 | tf_op jit(solution)/shard_map/all_to_all | solution.py:373
  81.0 4.3 %collective-permute-start.4 = (f32[5,2,16,128]{3,2,1,0:T(8,128)S(1)}, f32[5,2,16,128]{3,2,1,0:T(8,128)S(1)}, u32[]{:S(2)}, u32[]{:S(2)}) collective-permute-start(f32[5,2,16,128]{3,2,1,0:T(8,128)S(1)} %get-tuple-element.44), channel_id=1, source_target_pairs={{1,2},{3,4},{5,6},{7,8},{9,10},{11,12},{13,14},{15,16},{17,18},{19... | collective-permute-start | bytes 245768 | tf_op jit(solution)/shard_map/ppermute | solution.py:369
  85.3 1.9 %collective-permute-start.5 = (f32[5,2,16,128]{3,2,1,0:T(8,128)S(1)}, f32[5,2,16,128]{3,2,1,0:T(8,128)S(1)}, u32[]{:S(2)}, u32[]{:S(2)}) collective-permute-start(f32[5,2,16,128]{3,2,1,0:T(8,128)S(1)} %get-tuple-element.45), channel_id=1, source_target_pairs={{0,1},{2,3},{4,5},{6,7},{8,9},{10,11},{12,13},{14,15},{16,17},{18,... | collective-permute-start | bytes 245768 | tf_op jit(solution)/shard_map/ppermute | solution.py:369
  87.2 1.0 shard_map.90.refs_4_
  89.0 4.6 %collective-permute-start.6 = (f32[5,2,16,128]{3,2,1,0:T(8,128)S(1)}, f32[5,2,16,128]{3,2,1,0:T(8,128)S(1)}, u32[]{:S(2)}, u32[]{:S(2)}) collective-permute-start(f32[5,2,16,128]{3,2,1,0:T(8,128)S(1)} %get-tuple-element.47), channel_id=1, source_target_pairs={{1,2},{3,4},{5,6},{7,8},{9,10},{11,12},{13,14},{15,16},{17,18},{19... | collective-permute-start | bytes 245768 | tf_op jit(solution)/shard_map/ppermute | solution.py:369
  93.7 1.9 %collective-permute-start.7 = (f32[5,2,16,128]{3,2,1,0:T(8,128)S(1)}, f32[5,2,16,128]{3,2,1,0:T(8,128)S(1)}, u32[]{:S(2)}, u32[]{:S(2)}) collective-permute-start(f32[5,2,16,128]{3,2,1,0:T(8,128)S(1)} %get-tuple-element.48), channel_id=1, source_target_pairs={{0,1},{2,3},{4,5},{6,7},{8,9},{10,11},{12,13},{14,15},{16,17},{18,... | collective-permute-start | bytes 245768 | tf_op jit(solution)/shard_map/ppermute | solution.py:369
  95.6 1.0 shard_map.92.refs_4_
  97.1 15.3 %all_to_all.33.refs_3_ = f32[16,5,8,128]{3,2,1,0:T(8,128)S(1)} all-to-all(f32[16,5,8,128]{3,2,1,0:T(8,128)S(1)} %shard_map.93), channel_id=1, replica_groups={{288,384,160,256,448,32,416,128,192,0,352,224,64,96,320,480},{289,385,1..., dimensions={0} | all-to-all | bytes 655360 | tf_op jit(solution)/shard_map/all_to_all | solution.py:373
  112.8 13.8 %all_to_all.34.back = f32[16,5,8,128]{3,2,1,0:T(8,128)S(1)} all-to-all(f32[16,5,8,128]{3,2,1,0:T(8,128)S(1)} %shard_map.94), channel_id=1, replica_groups={{288,384,160,256,448,32,416,128,192,0,352,224,64,96,320,480},{289,385,1..., dimensions={0} | all-to-all | bytes 655360 | tf_op jit(solution)/shard_map/all_to_all | solution.py:373
  126.7 8.7 %collective-permute-start.8 = (f32[5,2,16,128]{3,2,1,0:T(8,128)S(1)}, f32[5,2,16,128]{3,2,1,0:T(8,128)S(1)}, u32[]{:S(2)}, u32[]{:S(2)}) collective-permute-start(f32[5,2,16,128]{3,2,1,0:T(8,128)S(1)} %get-tuple-element.51), channel_id=1, source_target_pairs={{1,2},{3,4},{5,6},{7,8},{9,10},{11,12},{13,14},{15,16},{17,18},{19... | collective-permute-start | bytes 245768 | tf_op jit(solution)/shard_map/ppermute | solution.py:369
  135.5 1.9 %collective-permute-start.9 = (f32[5,2,16,128]{3,2,1,0:T(8,128)S(1)}, f32[5,2,16,128]{3,2,1,0:T(8,128)S(1)}, u32[]{:S(2)}, u32[]{:S(2)}) collective-permute-start(f32[5,2,16,128]{3,2,1,0:T(8,128)S(1)} %get-tuple-element.52), channel_id=1, source_target_pairs={{0,1},{2,3},{4,5},{6,7},{8,9},{10,11},{12,13},{14,15},{16,17},{18,... | collective-permute-start | bytes 245768 | tf_op jit(solution)/shard_map/ppermute | solution.py:369
  137.4 1.0 shard_map.96.refs_4_
  138.7 0.8 shard_map.97
  (19 shorter events, 3.5 us)
Async XLA Ops:
  1.8 21.1 %all-to-all-start = ((f32[16,3,8,128]{3,2,1,0:T(8,128)}), f32[16,3,8,128]{3,2,1,0:T(8,128)S(1)}, u32[]{:S(2)}, u32[]{:S(2)}) async-start(f32[16,3,8,128]{3,2,1,0:T(8,128)} %get-tuple-element.37), calls=%async_computation | async-start | bytes 393216 | tf_op jit(solution)/shard_map/all_to_all | solution.py:373
  11.2 11.7 %collective-permute-start = (f32[7,2,16,128]{3,2,1,0:T(8,128)}, f32[7,2,16,128]{3,2,1,0:T(8,128)S(1)}, u32[]{:S(2)}, u32[]{:S(2)}) collective-permute-start(f32[7,2,16,128]{3,2,1,0:T(8,128)} %get-tuple-element.35), channel_id=1, source_target_pairs={{1,2},{3,4},{5,6},{7,8},{9,10},{11,12},{13,14},{15,16},{17,18},{19... | collective-permute-start | bytes 344072 | tf_op jit(solution)/shard_map/ppermute | solution.py:369
  17.9 5.1 %collective-permute-start.1 = (f32[7,2,16,128]{3,2,1,0:T(8,128)S(1)}, f32[7,2,16,128]{3,2,1,0:T(8,128)S(1)}, u32[]{:S(2)}, u32[]{:S(2)}) collective-permute-start(f32[7,2,16,128]{3,2,1,0:T(8,128)S(1)} %get-tuple-element.36), channel_id=1, source_target_pairs={{0,1},{2,3},{4,5},{6,7},{8,9},{10,11},{12,13},{14,15},{16,17},{18,... | collective-permute-start | bytes 344072 | tf_op jit(solution)/shard_map/ppermute | solution.py:369
  37.8 8.5 %collective-permute-start.2 = (f32[5,2,16,128]{3,2,1,0:T(8,128)S(1)}, f32[5,2,16,128]{3,2,1,0:T(8,128)S(1)}, u32[]{:S(2)}, u32[]{:S(2)}) collective-permute-start(f32[5,2,16,128]{3,2,1,0:T(8,128)S(1)} %get-tuple-element.40), channel_id=1, source_target_pairs={{1,2},{3,4},{5,6},{7,8},{9,10},{11,12},{13,14},{15,16},{17,18},{19... | collective-permute-start | bytes 245768 | tf_op jit(solution)/shard_map/ppermute | solution.py:369
  42.9 3.4 %collective-permute-start.3 = (f32[5,2,16,128]{3,2,1,0:T(8,128)S(1)}, f32[5,2,16,128]{3,2,1,0:T(8,128)S(1)}, u32[]{:S(2)}, u32[]{:S(2)}) collective-permute-start(f32[5,2,16,128]{3,2,1,0:T(8,128)S(1)} %get-tuple-element.41), channel_id=1, source_target_pairs={{0,1},{2,3},{4,5},{6,7},{8,9},{10,11},{12,13},{14,15},{16,17},{18,... | collective-permute-start | bytes 245768 | tf_op jit(solution)/shard_map/ppermute | solution.py:369
  81.0 7.9 %collective-permute-start.4 = (f32[5,2,16,128]{3,2,1,0:T(8,128)S(1)}, f32[5,2,16,128]{3,2,1,0:T(8,128)S(1)}, u32[]{:S(2)}, u32[]{:S(2)}) collective-permute-start(f32[5,2,16,128]{3,2,1,0:T(8,128)S(1)} %get-tuple-element.44), channel_id=1, source_target_pairs={{1,2},{3,4},{5,6},{7,8},{9,10},{11,12},{13,14},{15,16},{17,18},{19... | collective-permute-start | bytes 245768 | tf_op jit(solution)/shard_map/ppermute | solution.py:369
  85.3 3.5 %collective-permute-start.5 = (f32[5,2,16,128]{3,2,1,0:T(8,128)S(1)}, f32[5,2,16,128]{3,2,1,0:T(8,128)S(1)}, u32[]{:S(2)}, u32[]{:S(2)}) collective-permute-start(f32[5,2,16,128]{3,2,1,0:T(8,128)S(1)} %get-tuple-element.45), channel_id=1, source_target_pairs={{0,1},{2,3},{4,5},{6,7},{8,9},{10,11},{12,13},{14,15},{16,17},{18,... | collective-permute-start | bytes 245768 | tf_op jit(solution)/shard_map/ppermute | solution.py:369
  89.0 7.9 %collective-permute-start.6 = (f32[5,2,16,128]{3,2,1,0:T(8,128)S(1)}, f32[5,2,16,128]{3,2,1,0:T(8,128)S(1)}, u32[]{:S(2)}, u32[]{:S(2)}) collective-permute-start(f32[5,2,16,128]{3,2,1,0:T(8,128)S(1)} %get-tuple-element.47), channel_id=1, source_target_pairs={{1,2},{3,4},{5,6},{7,8},{9,10},{11,12},{13,14},{15,16},{17,18},{19... | collective-permute-start | bytes 245768 | tf_op jit(solution)/shard_map/ppermute | solution.py:369
  93.7 3.2 %collective-permute-start.7 = (f32[5,2,16,128]{3,2,1,0:T(8,128)S(1)}, f32[5,2,16,128]{3,2,1,0:T(8,128)S(1)}, u32[]{:S(2)}, u32[]{:S(2)}) collective-permute-start(f32[5,2,16,128]{3,2,1,0:T(8,128)S(1)} %get-tuple-element.48), channel_id=1, source_target_pairs={{0,1},{2,3},{4,5},{6,7},{8,9},{10,11},{12,13},{14,15},{16,17},{18,... | collective-permute-start | bytes 245768 | tf_op jit(solution)/shard_map/ppermute | solution.py:369
  126.7 11.7 %collective-permute-start.8 = (f32[5,2,16,128]{3,2,1,0:T(8,128)S(1)}, f32[5,2,16,128]{3,2,1,0:T(8,128)S(1)}, u32[]{:S(2)}, u32[]{:S(2)}) collective-permute-start(f32[5,2,16,128]{3,2,1,0:T(8,128)S(1)} %get-tuple-element.51), channel_id=1, source_target_pairs={{1,2},{3,4},{5,6},{7,8},{9,10},{11,12},{13,14},{15,16},{17,18},{19... | collective-permute-start | bytes 245768 | tf_op jit(solution)/shard_map/ppermute | solution.py:369
  135.5 3.2 %collective-permute-start.9 = (f32[5,2,16,128]{3,2,1,0:T(8,128)S(1)}, f32[5,2,16,128]{3,2,1,0:T(8,128)S(1)}, u32[]{:S(2)}, u32[]{:S(2)}) collective-permute-start(f32[5,2,16,128]{3,2,1,0:T(8,128)S(1)} %get-tuple-element.52), channel_id=1, source_target_pairs={{0,1},{2,3},{4,5},{6,7},{8,9},{10,11},{12,13},{14,15},{16,17},{18,... | collective-permute-start | bytes 245768 | tf_op jit(solution)/shard_map/ppermute | solution.py:369

commit v7 on v6

--- a/solution.py
+++ b/solution.py
@@ -92,9 +92,13 @@
         copy.wait()
 
 
-def load_kernel(*refs):
-    half = len(refs) // 2
-    load(refs[:half], refs[half:-1], refs[-1])
+def load_kernel(gradient, jacobian, gradient_out, jacobian_out, sems):
+    pieces = [(direction, a) for direction in range(3) for a in range(VARS)]
+    load(
+        [gradient] + [jacobian.at[piece] for piece in pieces],
+        [gradient_out] + [jacobian_out.at[piece] for piece in pieces],
+        sems,
+    )
 
 
 def pack_kernel(*refs):
@@ -168,7 +172,7 @@
             finish(var, layer, damped[var] + 0.5 * acc)
         return carry
 
-    lax.fori_loop(0, LAYERS, layer_step, 0)
+    lax.fori_loop(0, LAYERS, layer_step, 0, unroll=2)
 
 
 def spatial_x(field, staged, coefs, jacobian, damped, finish):
@@ -403,7 +407,7 @@
         [kept(*FIELD), kept(*jacobian.shape)],
         [in_hbm(gradient), in_hbm(jacobian)],
         [HBM] * 2,
-        scratch=(pltpu.SemaphoreType.DMA((2,)),),
+        scratch=(pltpu.SemaphoreType.DMA((16,)),),
     )
     (coupled,) = call(
         couple_kernel,

time: 140 us -> 140 us (level)
  Pallas kernels: 11.1 us -> 9.13 us
  waiting for transfers between devices: 1.78 us -> 3.3 us
    pallas_call x16, Pallas kernels: 11.1 us -> 9.13 us  [call(): pl.pallas_call(kernel, out_shape=outs, in_specs=specs or [VMEM] * len(arg...]
  transfers between devices with their start and end apart: 11 -> 11, of which waited for: 4 -> 5; matrix products, arithmetic and copies ran while one was open for 0% -> 0% of each run, Pallas kernels for 4% -> 3%
where the time goes in v7:
time: 140 us; the launch traced here: 139 us
  blocking collectives  76.4 us (55%)
  starting transfers between devices  48.8 us (35%)
  Pallas kernels  9.13 us (7%)
  waiting for transfers between devices  3.3 us (2%)
  between operations  1.51 us (1%)
    all_to_all x5, blocking collectives, across(): lax.all_to_all(message, 'inst', 0, 0, axis_index_groups=[ORDER], tiled=True)  76.4 us
    ppermute x5, starting transfers between devices, exchange(): lax.ppermute(odd, 'cells', PAIRS_ODD)  29.8 us
    ppermute x5, starting transfers between devices, exchange(): lax.ppermute(even, 'cells', PAIRS_EVEN)  9.6 us
    all_to_all x1, starting transfers between devices, across(): lax.all_to_all(message, 'inst', 0, 0, axis_index_groups=[ORDER], tiled=True)  9.39 us
    pallas_call x16, Pallas kernels, call(): pl.pallas_call(kernel, out_shape=outs, in_specs=specs or [VMEM] * len(arg...  9.13 us
  transfers between devices with their start and end apart: 11, of which 5 were waited for; matrix products, arithmetic and copies ran while one was open for 0% of the time, Pallas kernels for 3%

profile of v7, /device:TPU:201, one launch (start us, length us, event | category | flops | bytes accessed | tf_op | source)
XLA Modules:
  0.0 139.2 jit_solution(9348147047599646165)
XLA Ops:
  0.0 1.8 %shard_map.82 = (f32[16,3,8,128]{3,2,1,0:T(8,128)}, f32[7,2,16,128]{3,2,1,0:T(8,128)}, f32[7,2,16,128]{3,2,1,0:T(8,128)S(1)}, f32[5,4,16,128]{3,2,1,0:T(8,128)S(...) custom-call(f32[5,4,16,128]{3,2,1,0:T(8,128)} %bitcast.9, ...), custom_call_target="tpu_custom_call" | custom-call | bytes 1212416 | tf_op jit(solution)/shard_map/pallas_call | solution.py:61
  1.8 9.4 %all-to-all-start = ((f32[16,3,8,128]{3,2,1,0:T(8,128)}), f32[16,3,8,128]{3,2,1,0:T(8,128)S(1)}, u32[]{:S(2)}, u32[]{:S(2)}) async-start(f32[16,3,8,128]{3,2,1,0:T(8,128)} %get-tuple-element.37), calls=%async_computation | async-start | bytes 393216 | tf_op jit(solution)/shard_map/all_to_all | solution.py:377
  11.2 6.7 %collective-permute-start = (f32[7,2,16,128]{3,2,1,0:T(8,128)}, f32[7,2,16,128]{3,2,1,0:T(8,128)S(1)}, u32[]{:S(2)}, u32[]{:S(2)}) collective-permute-start(f32[7,2,16,128]{3,2,1,0:T(8,128)} %get-tuple-element.35), channel_id=1, source_target_pairs={{1,2},{3,4},{5,6},{7,8},{9,10},{11,12},{13,14},{15,16},{17,18},{19... | collective-permute-start | bytes 344072 | tf_op jit(solution)/shard_map/ppermute | solution.py:373
  17.9 1.9 %collective-permute-start.1 = (f32[7,2,16,128]{3,2,1,0:T(8,128)S(1)}, f32[7,2,16,128]{3,2,1,0:T(8,128)S(1)}, u32[]{:S(2)}, u32[]{:S(2)}) collective-permute-start(f32[7,2,16,128]{3,2,1,0:T(8,128)S(1)} %get-tuple-element.36), channel_id=1, source_target_pairs={{0,1},{2,3},{4,5},{6,7},{8,9},{10,11},{12,13},{14,15},{16,17},{18,... | collective-permute-start | bytes 344072 | tf_op jit(solution)/shard_map/ppermute | solution.py:373
  21.1 1.9 %shard_map.83 = (f32[5,4,16,128]{3,2,1,0:T(8,128)S(1)}, f32[3,5,5,4,16,128]{5,4,3,2,1,0:T(8,128)S(1)}) custom-call(f32[5,4,16,128]{3,2,1,0:T(8,128)} %bitcast.8, f32[3,5,5,4,16,128]{5,4,3,2,1,0:T(8,128)} %bitcast.7), custom_call_target="tpu_custom_call" | custom-call | bytes 5242880 | tf_op jit(solution)/shard_map/pallas_call | solution.py:61
  23.2 13.6 %all_to_all.30.refs_8_ = f32[16,5,4,128]{3,2,1,0:T(4,128)S(1)} all-to-all(f32[16,5,4,128]{3,2,1,0:T(4,128)S(1)} %shard_map.84), channel_id=1, replica_groups={{288,384,160,256,448,32,416,128,192,0,352,224,64,96,320,480},{289,385,1..., dimensions={0} | all-to-all | bytes 327680 | tf_op jit(solution)/shard_map/all_to_all | solution.py:377
  36.8 0.7 shard_map.85
  37.5 5.1 %collective-permute-start.2 = (f32[5,2,16,128]{3,2,1,0:T(8,128)S(1)}, f32[5,2,16,128]{3,2,1,0:T(8,128)S(1)}, u32[]{:S(2)}, u32[]{:S(2)}) collective-permute-start(f32[5,2,16,128]{3,2,1,0:T(8,128)S(1)} %get-tuple-element.40), channel_id=1, source_target_pairs={{1,2},{3,4},{5,6},{7,8},{9,10},{11,12},{13,14},{15,16},{17,18},{19... | collective-permute-start | bytes 245768 | tf_op jit(solution)/shard_map/ppermute | solution.py:373
  42.6 1.9 %collective-permute-start.3 = (f32[5,2,16,128]{3,2,1,0:T(8,128)S(1)}, f32[5,2,16,128]{3,2,1,0:T(8,128)S(1)}, u32[]{:S(2)}, u32[]{:S(2)}) collective-permute-start(f32[5,2,16,128]{3,2,1,0:T(8,128)S(1)} %get-tuple-element.41), channel_id=1, source_target_pairs={{0,1},{2,3},{4,5},{6,7},{8,9},{10,11},{12,13},{14,15},{16,17},{18,... | collective-permute-start | bytes 245768 | tf_op jit(solution)/shard_map/ppermute | solution.py:373
  45.1 1.0 collective-permute-done.2.refs_5_
  46.2 17.5 %all_to_all.31.refs_3_ = f32[16,5,8,128]{3,2,1,0:T(8,128)S(1)} all-to-all(f32[16,5,8,128]{3,2,1,0:T(8,128)S(1)} %shard_map.87), channel_id=1, replica_groups={{288,384,160,256,448,32,416,128,192,0,352,224,64,96,320,480},{289,385,1..., dimensions={0} | all-to-all | bytes 655360 | tf_op jit(solution)/shard_map/all_to_all | solution.py:377
  64.1 16.3 %all_to_all.32.back = f32[16,5,8,128]{3,2,1,0:T(8,128)S(1)} all-to-all(f32[16,5,8,128]{3,2,1,0:T(8,128)S(1)} %shard_map.88), channel_id=1, replica_groups={{288,384,160,256,448,32,416,128,192,0,352,224,64,96,320,480},{289,385,1..., dimensions={0} | all-to-all | bytes 655360 | tf_op jit(solution)/shard_map/all_to_all | solution.py:377
  80.6 4.5 %collective-permute-start.4 = (f32[5,2,16,128]{3,2,1,0:T(8,128)S(1)}, f32[5,2,16,128]{3,2,1,0:T(8,128)S(1)}, u32[]{:S(2)}, u32[]{:S(2)}) collective-permute-start(f32[5,2,16,128]{3,2,1,0:T(8,128)S(1)} %get-tuple-element.44), channel_id=1, source_target_pairs={{1,2},{3,4},{5,6},{7,8},{9,10},{11,12},{13,14},{15,16},{17,18},{19... | collective-permute-start | bytes 245768 | tf_op jit(solution)/shard_map/ppermute | solution.py:373
  85.0 1.9 %collective-permute-start.5 = (f32[5,2,16,128]{3,2,1,0:T(8,128)S(1)}, f32[5,2,16,128]{3,2,1,0:T(8,128)S(1)}, u32[]{:S(2)}, u32[]{:S(2)}) collective-permute-start(f32[5,2,16,128]{3,2,1,0:T(8,128)S(1)} %get-tuple-element.45), channel_id=1, source_target_pairs={{0,1},{2,3},{4,5},{6,7},{8,9},{10,11},{12,13},{14,15},{16,17},{18,... | collective-permute-start | bytes 245768 | tf_op jit(solution)/shard_map/ppermute | solution.py:373
  86.9 0.5 shard_map.90.refs_4_
  87.5 0.9 collective-permute-done.4.refs_5_
  88.6 4.8 %collective-permute-start.6 = (f32[5,2,16,128]{3,2,1,0:T(8,128)S(1)}, f32[5,2,16,128]{3,2,1,0:T(8,128)S(1)}, u32[]{:S(2)}, u32[]{:S(2)}) collective-permute-start(f32[5,2,16,128]{3,2,1,0:T(8,128)S(1)} %get-tuple-element.47), channel_id=1, source_target_pairs={{1,2},{3,4},{5,6},{7,8},{9,10},{11,12},{13,14},{15,16},{17,18},{19... | collective-permute-start | bytes 245768 | tf_op jit(solution)/shard_map/ppermute | solution.py:373
  93.5 1.9 %collective-permute-start.7 = (f32[5,2,16,128]{3,2,1,0:T(8,128)S(1)}, f32[5,2,16,128]{3,2,1,0:T(8,128)S(1)}, u32[]{:S(2)}, u32[]{:S(2)}) collective-permute-start(f32[5,2,16,128]{3,2,1,0:T(8,128)S(1)} %get-tuple-element.48), channel_id=1, source_target_pairs={{0,1},{2,3},{4,5},{6,7},{8,9},{10,11},{12,13},{14,15},{16,17},{18,... | collective-permute-start | bytes 245768 | tf_op jit(solution)/shard_map/ppermute | solution.py:373
  96.8 15.1 %all_to_all.33.refs_3_ = f32[16,5,8,128]{3,2,1,0:T(8,128)S(1)} all-to-all(f32[16,5,8,128]{3,2,1,0:T(8,128)S(1)} %shard_map.93), channel_id=1, replica_groups={{288,384,160,256,448,32,416,128,192,0,352,224,64,96,320,480},{289,385,1..., dimensions={0} | all-to-all | bytes 655360 | tf_op jit(solution)/shard_map/all_to_all | solution.py:377
  112.4 13.9 %all_to_all.34.back = f32[16,5,8,128]{3,2,1,0:T(8,128)S(1)} all-to-all(f32[16,5,8,128]{3,2,1,0:T(8,128)S(1)} %shard_map.94), channel_id=1, replica_groups={{288,384,160,256,448,32,416,128,192,0,352,224,64,96,320,480},{289,385,1..., dimensions={0} | all-to-all | bytes 655360 | tf_op jit(solution)/shard_map/all_to_all | solution.py:377
  126.4 8.8 %collective-permute-start.8 = (f32[5,2,16,128]{3,2,1,0:T(8,128)S(1)}, f32[5,2,16,128]{3,2,1,0:T(8,128)S(1)}, u32[]{:S(2)}, u32[]{:S(2)}) collective-permute-start(f32[5,2,16,128]{3,2,1,0:T(8,128)S(1)} %get-tuple-element.51), channel_id=1, source_target_pairs={{1,2},{3,4},{5,6},{7,8},{9,10},{11,12},{13,14},{15,16},{17,18},{19... | collective-permute-start | bytes 245768 | tf_op jit(solution)/shard_map/ppermute | solution.py:373
  135.2 1.9 %collective-permute-start.9 = (f32[5,2,16,128]{3,2,1,0:T(8,128)S(1)}, f32[5,2,16,128]{3,2,1,0:T(8,128)S(1)}, u32[]{:S(2)}, u32[]{:S(2)}) collective-permute-start(f32[5,2,16,128]{3,2,1,0:T(8,128)S(1)} %get-tuple-element.52), channel_id=1, source_target_pairs={{0,1},{2,3},{4,5},{6,7},{8,9},{10,11},{12,13},{14,15},{16,17},{18,... | collective-permute-start | bytes 245768 | tf_op jit(solution)/shard_map/ppermute | solution.py:373
  137.6 0.7 collective-permute-done.9.refs_6_
  138.3 0.8 shard_map.97
  (19 shorter events, 4.0 us)
Async XLA Ops:
  1.8 21.2 %all-to-all-start = ((f32[16,3,8,128]{3,2,1,0:T(8,128)}), f32[16,3,8,128]{3,2,1,0:T(8,128)S(1)}, u32[]{:S(2)}, u32[]{:S(2)}) async-start(f32[16,3,8,128]{3,2,1,0:T(8,128)} %get-tuple-element.37), calls=%async_computation | async-start | bytes 393216 | tf_op jit(solution)/shard_map/all_to_all | solution.py:377
  11.2 11.8 %collective-permute-start = (f32[7,2,16,128]{3,2,1,0:T(8,128)}, f32[7,2,16,128]{3,2,1,0:T(8,128)S(1)}, u32[]{:S(2)}, u32[]{:S(2)}) collective-permute-start(f32[7,2,16,128]{3,2,1,0:T(8,128)} %get-tuple-element.35), channel_id=1, source_target_pairs={{1,2},{3,4},{5,6},{7,8},{9,10},{11,12},{13,14},{15,16},{17,18},{19... | collective-permute-start | bytes 344072 | tf_op jit(solution)/shard_map/ppermute | solution.py:373
  17.9 5.2 %collective-permute-start.1 = (f32[7,2,16,128]{3,2,1,0:T(8,128)S(1)}, f32[7,2,16,128]{3,2,1,0:T(8,128)S(1)}, u32[]{:S(2)}, u32[]{:S(2)}) collective-permute-start(f32[7,2,16,128]{3,2,1,0:T(8,128)S(1)} %get-tuple-element.36), channel_id=1, source_target_pairs={{0,1},{2,3},{4,5},{6,7},{8,9},{10,11},{12,13},{14,15},{16,17},{18,... | collective-permute-start | bytes 344072 | tf_op jit(solution)/shard_map/ppermute | solution.py:373
  37.5 8.5 %collective-permute-start.2 = (f32[5,2,16,128]{3,2,1,0:T(8,128)S(1)}, f32[5,2,16,128]{3,2,1,0:T(8,128)S(1)}, u32[]{:S(2)}, u32[]{:S(2)}) collective-permute-start(f32[5,2,16,128]{3,2,1,0:T(8,128)S(1)} %get-tuple-element.40), channel_id=1, source_target_pairs={{1,2},{3,4},{5,6},{7,8},{9,10},{11,12},{13,14},{15,16},{17,18},{19... | collective-permute-start | bytes 245768 | tf_op jit(solution)/shard_map/ppermute | solution.py:373
  42.6 3.5 %collective-permute-start.3 = (f32[5,2,16,128]{3,2,1,0:T(8,128)S(1)}, f32[5,2,16,128]{3,2,1,0:T(8,128)S(1)}, u32[]{:S(2)}, u32[]{:S(2)}) collective-permute-start(f32[5,2,16,128]{3,2,1,0:T(8,128)S(1)} %get-tuple-element.41), channel_id=1, source_target_pairs={{0,1},{2,3},{4,5},{6,7},{8,9},{10,11},{12,13},{14,15},{16,17},{18,... | collective-permute-start | bytes 245768 | tf_op jit(solution)/shard_map/ppermute | solution.py:373
  80.6 7.9 %collective-permute-start.4 = (f32[5,2,16,128]{3,2,1,0:T(8,128)S(1)}, f32[5,2,16,128]{3,2,1,0:T(8,128)S(1)}, u32[]{:S(2)}, u32[]{:S(2)}) collective-permute-start(f32[5,2,16,128]{3,2,1,0:T(8,128)S(1)} %get-tuple-element.44), channel_id=1, source_target_pairs={{1,2},{3,4},{5,6},{7,8},{9,10},{11,12},{13,14},{15,16},{17,18},{19... | collective-permute-start | bytes 245768 | tf_op jit(solution)/shard_map/ppermute | solution.py:373
  85.0 3.4 %collective-permute-start.5 = (f32[5,2,16,128]{3,2,1,0:T(8,128)S(1)}, f32[5,2,16,128]{3,2,1,0:T(8,128)S(1)}, u32[]{:S(2)}, u32[]{:S(2)}) collective-permute-start(f32[5,2,16,128]{3,2,1,0:T(8,128)S(1)} %get-tuple-element.45), channel_id=1, source_target_pairs={{0,1},{2,3},{4,5},{6,7},{8,9},{10,11},{12,13},{14,15},{16,17},{18,... | collective-permute-start | bytes 245768 | tf_op jit(solution)/shard_map/ppermute | solution.py:373
  88.6 7.9 %collective-permute-start.6 = (f32[5,2,16,128]{3,2,1,0:T(8,128)S(1)}, f32[5,2,16,128]{3,2,1,0:T(8,128)S(1)}, u32[]{:S(2)}, u32[]{:S(2)}) collective-permute-start(f32[5,2,16,128]{3,2,1,0:T(8,128)S(1)} %get-tuple-element.47), channel_id=1, source_target_pairs={{1,2},{3,4},{5,6},{7,8},{9,10},{11,12},{13,14},{15,16},{17,18},{19... | collective-permute-start | bytes 245768 | tf_op jit(solution)/shard_map/ppermute | solution.py:373
  93.5 3.2 %collective-permute-start.7 = (f32[5,2,16,128]{3,2,1,0:T(8,128)S(1)}, f32[5,2,16,128]{3,2,1,0:T(8,128)S(1)}, u32[]{:S(2)}, u32[]{:S(2)}) collective-permute-start(f32[5,2,16,128]{3,2,1,0:T(8,128)S(1)} %get-tuple-element.48), channel_id=1, source_target_pairs={{0,1},{2,3},{4,5},{6,7},{8,9},{10,11},{12,13},{14,15},{16,17},{18,... | collective-permute-start | bytes 245768 | tf_op jit(solution)/shard_map/ppermute | solution.py:373
  126.4 11.3 %collective-permute-start.8 = (f32[5,2,16,128]{3,2,1,0:T(8,128)S(1)}, f32[5,2,16,128]{3,2,1,0:T(8,128)S(1)}, u32[]{:S(2)}, u32[]{:S(2)}) collective-permute-start(f32[5,2,16,128]{3,2,1,0:T(8,128)S(1)} %get-tuple-element.51), channel_id=1, source_target_pairs={{1,2},{3,4},{5,6},{7,8},{9,10},{11,12},{13,14},{15,16},{17,18},{19... | collective-permute-start | bytes 245768 | tf_op jit(solution)/shard_map/ppermute | solution.py:373
  135.2 3.2 %collective-permute-start.9 = (f32[5,2,16,128]{3,2,1,0:T(8,128)S(1)}, f32[5,2,16,128]{3,2,1,0:T(8,128)S(1)}, u32[]{:S(2)}, u32[]{:S(2)}) collective-permute-start(f32[5,2,16,128]{3,2,1,0:T(8,128)S(1)} %get-tuple-element.52), channel_id=1, source_target_pairs={{0,1},{2,3},{4,5},{6,7},{8,9},{10,11},{12,13},{14,15},{16,17},{18,... | collective-permute-start | bytes 245768 | tf_op jit(solution)/shard_map/ppermute | solution.py:373

commit v8 on v6

--- a/solution.py
+++ b/solution.py
@@ -81,33 +81,42 @@
             odd_ref[row, layer] = read(row, 2 - first + layer)
 
 
-def load(sources, targets, sems):
+def copies_of(sources, targets, sems):
     copies = [
         pltpu.make_async_copy(source, target, sems.at[i])
         for i, (source, target) in enumerate(zip(sources, targets))
     ]
     for copy in copies:
         copy.start()
-    for copy in copies:
+    return copies
+
+
+def load_kernel(gradient, jacobian, gradient_out, jacobian_out, sems):
+    for copy in copies_of((gradient, jacobian), (gradient_out, jacobian_out), sems):
         copy.wait()
 
 
-def load_kernel(*refs):
-    half = len(refs) // 2
-    load(refs[:half], refs[half:-1], refs[-1])
-
-
 def pack_kernel(*refs):
-    message, odd_ref, even_ref = refs[4:7]
+    message_out, odd_ref, even_ref = refs[4:7]
     adjoint, second, fourth, step = refs[7:11]
-    load(refs[:4], refs[7:11], refs[11])
+    sems, message, sent_sems = refs[11:]
+    copies = copies_of(refs[:4], refs[7:11], sems)
+    copies[0].wait()
+    copies[3].wait()
+    sent = []
     for layer in range(LAYERS):
-        for quarter in range(4):
-            rows = slice(4 * quarter, 4 * quarter + 4)
+        for chunk, rows in quarters(layer):
             for slot in range(VARS + 1):
                 source = step[layer] if slot == VARS else adjoint[slot, layer]
                 half = 4 * (slot % 2)
-                message[4 * layer + quarter, slot // 2, half : half + 4, :] = source[rows, :]
+                message[chunk, slot // 2, half : half + 4, :] = source[rows, :]
+        part = pl.ds(4 * layer, 4)
+        sent.append(
+            pltpu.make_async_copy(message.at[part], message_out.at[part], sent_sems.at[layer])
+        )
+        sent[-1].start()
+    copies[1].wait()
+    copies[2].wait()
 
     def read(row, layer):
         if row < VARS:
@@ -115,6 +124,8 @@
         return second[0, layer] if row == VARS else fourth[0, layer]
 
     write_halos(read, odd_ref, even_ref, VARS + 2)
+    for copy in sent:
+        copy.wait()
 
 
 def stage_halos(staged, odd, even):
@@ -168,7 +179,7 @@
             finish(var, layer, damped[var] + 0.5 * acc)
         return carry
 
-    lax.fori_loop(0, LAYERS, layer_step, 0)
+    lax.fori_loop(0, LAYERS, layer_step, 0, unroll=4)
 
 
 def spatial_x(field, staged, coefs, jacobian, damped, finish):
@@ -362,7 +373,7 @@
             out[PLACE[k], index] = jnp.where(low, pltpu.roll(value, 4, 0), moved[k])
         return carry
 
-    lax.fori_loop(0, VARS, tile, 0)
+    lax.fori_loop(0, VARS, tile, 0, unroll=True)
 
 
 def exchange(odd, even):
@@ -394,7 +405,12 @@
         + [kept(*FIELD), kept(*coef_shape), kept(*coef_shape), kept(LAYERS, NY, NZ)],
         [in_hbm(x) for x in (adjoint, second, fourth, step)],
         [HBM] * 4,
-        scratch=(pltpu.SemaphoreType.DMA((4,)),),
+        scratch=(
+            pltpu.SemaphoreType.DMA((4,)),
+            pltpu.VMEM((INSTANCES, 3, 8, NZ), F32),
+            pltpu.SemaphoreType.DMA((LAYERS,)),
+        ),
+        out_specs=[HBM] + [VMEM] * 6,
     )
     steps = across(message)
     odd_first, even_first = exchange(odd, even)

time: 140 us -> 140 us (level)
  Pallas kernels: 11.1 us -> 9.03 us
  waiting for transfers between devices: 1.78 us -> 3.59 us
    pallas_call x16, Pallas kernels: 11.1 us -> 9.03 us  [call(): pl.pallas_call(kernel, out_shape=outs, in_specs=specs or [VMEM] * len(arg...]
  transfers between devices with their start and end apart: 11 -> 11, of which waited for: 4 -> 5; matrix products, arithmetic and copies ran while one was open for 0% -> 0% of each run, Pallas kernels for 4% -> 3%
where the time goes in v8:
time: 140 us; the launch traced here: 139 us
  blocking collectives  76.4 us (55%)
  starting transfers between devices  48.9 us (35%)
  Pallas kernels  9.03 us (6%)
  waiting for transfers between devices  3.59 us (3%)
  between operations  1.5 us (1%)
    all_to_all x5, blocking collectives, across(): lax.all_to_all(message, 'inst', 0, 0, axis_index_groups=[ORDER], tiled=True)  76.4 us
    ppermute x5, starting transfers between devices, exchange(): lax.ppermute(odd, 'cells', PAIRS_ODD)  29.9 us
    ppermute x5, starting transfers between devices, exchange(): lax.ppermute(even, 'cells', PAIRS_EVEN)  9.6 us
    all_to_all x1, starting transfers between devices, across(): lax.all_to_all(message, 'inst', 0, 0, axis_index_groups=[ORDER], tiled=True)  9.39 us
    pallas_call x16, Pallas kernels, call(): pl.pallas_call(kernel, out_shape=outs, in_specs=specs or [VMEM] * len(arg...  9.03 us
  transfers between devices with their start and end apart: 11, of which 5 were waited for; matrix products, arithmetic and copies ran while one was open for 0% of the time, Pallas kernels for 3%

profile of v8, /device:TPU:201, one launch (start us, length us, event | category | flops | bytes accessed | tf_op | source)
XLA Modules:
  0.0 139.4 jit_solution(584134176092137807)
XLA Ops:
  0.0 2.3 %shard_map.82 = (f32[16,3,8,128]{3,2,1,0:T(8,128)}, f32[7,2,16,128]{3,2,1,0:T(8,128)}, f32[7,2,16,128]{3,2,1,0:T(8,128)S(1)}, f32[5,4,16,128]{3,2,1,0:T(8,128)S(...) custom-call(f32[5,4,16,128]{3,2,1,0:T(8,128)} %bitcast.9, ...), custom_call_target="tpu_custom_call" | custom-call | bytes 1212416 | tf_op jit(solution)/shard_map/pallas_call | solution.py:61
  2.3 9.4 %all-to-all-start = ((f32[16,3,8,128]{3,2,1,0:T(8,128)}), f32[16,3,8,128]{3,2,1,0:T(8,128)S(1)}, u32[]{:S(2)}, u32[]{:S(2)}) async-start(f32[16,3,8,128]{3,2,1,0:T(8,128)} %get-tuple-element.37), calls=%async_computation | async-start | bytes 393216 | tf_op jit(solution)/shard_map/all_to_all | solution.py:384
  11.7 6.7 %collective-permute-start = (f32[7,2,16,128]{3,2,1,0:T(8,128)}, f32[7,2,16,128]{3,2,1,0:T(8,128)S(1)}, u32[]{:S(2)}, u32[]{:S(2)}) collective-permute-start(f32[7,2,16,128]{3,2,1,0:T(8,128)} %get-tuple-element.35), channel_id=1, source_target_pairs={{1,2},{3,4},{5,6},{7,8},{9,10},{11,12},{13,14},{15,16},{17,18},{19... | collective-permute-start | bytes 344072 | tf_op jit(solution)/shard_map/ppermute | solution.py:380
  18.4 1.9 %collective-permute-start.1 = (f32[7,2,16,128]{3,2,1,0:T(8,128)S(1)}, f32[7,2,16,128]{3,2,1,0:T(8,128)S(1)}, u32[]{:S(2)}, u32[]{:S(2)}) collective-permute-start(f32[7,2,16,128]{3,2,1,0:T(8,128)S(1)} %get-tuple-element.36), channel_id=1, source_target_pairs={{0,1},{2,3},{4,5},{6,7},{8,9},{10,11},{12,13},{14,15},{16,17},{18,... | collective-permute-start | bytes 344072 | tf_op jit(solution)/shard_map/ppermute | solution.py:380
  21.6 1.8 %shard_map.83 = (f32[5,4,16,128]{3,2,1,0:T(8,128)S(1)}, f32[3,5,5,4,16,128]{5,4,3,2,1,0:T(8,128)S(1)}) custom-call(f32[5,4,16,128]{3,2,1,0:T(8,128)} %bitcast.8, f32[3,5,5,4,16,128]{5,4,3,2,1,0:T(8,128)} %bitcast.7), custom_call_target="tpu_custom_call" | custom-call | bytes 5242880 | tf_op jit(solution)/shard_map/pallas_call | solution.py:61
  23.6 13.6 %all_to_all.30.refs_8_ = f32[16,5,4,128]{3,2,1,0:T(4,128)S(1)} all-to-all(f32[16,5,4,128]{3,2,1,0:T(4,128)S(1)} %shard_map.84), channel_id=1, replica_groups={{288,384,160,256,448,32,416,128,192,0,352,224,64,96,320,480},{289,385,1..., dimensions={0} | all-to-all | bytes 327680 | tf_op jit(solution)/shard_map/all_to_all | solution.py:384
  37.2 0.7 shard_map.85
  37.8 5.1 %collective-permute-start.2 = (f32[5,2,16,128]{3,2,1,0:T(8,128)S(1)}, f32[5,2,16,128]{3,2,1,0:T(8,128)S(1)}, u32[]{:S(2)}, u32[]{:S(2)}) collective-permute-start(f32[5,2,16,128]{3,2,1,0:T(8,128)S(1)} %get-tuple-element.40), channel_id=1, source_target_pairs={{1,2},{3,4},{5,6},{7,8},{9,10},{11,12},{13,14},{15,16},{17,18},{19... | collective-permute-start | bytes 245768 | tf_op jit(solution)/shard_map/ppermute | solution.py:380
  42.9 1.9 %collective-permute-start.3 = (f32[5,2,16,128]{3,2,1,0:T(8,128)S(1)}, f32[5,2,16,128]{3,2,1,0:T(8,128)S(1)}, u32[]{:S(2)}, u32[]{:S(2)}) collective-permute-start(f32[5,2,16,128]{3,2,1,0:T(8,128)S(1)} %get-tuple-element.41), channel_id=1, source_target_pairs={{0,1},{2,3},{4,5},{6,7},{8,9},{10,11},{12,13},{14,15},{16,17},{18,... | collective-permute-start | bytes 245768 | tf_op jit(solution)/shard_map/ppermute | solution.py:380
  45.3 1.0 collective-permute-done.2.refs_5_
  46.5 17.5 %all_to_all.31.refs_3_ = f32[16,5,8,128]{3,2,1,0:T(8,128)S(1)} all-to-all(f32[16,5,8,128]{3,2,1,0:T(8,128)S(1)} %shard_map.87), channel_id=1, replica_groups={{288,384,160,256,448,32,416,128,192,0,352,224,64,96,320,480},{289,385,1..., dimensions={0} | all-to-all | bytes 655360 | tf_op jit(solution)/shard_map/all_to_all | solution.py:384
  64.4 16.3 %all_to_all.32.back = f32[16,5,8,128]{3,2,1,0:T(8,128)S(1)} all-to-all(f32[16,5,8,128]{3,2,1,0:T(8,128)S(1)} %shard_map.88), channel_id=1, replica_groups={{288,384,160,256,448,32,416,128,192,0,352,224,64,96,320,480},{289,385,1..., dimensions={0} | all-to-all | bytes 655360 | tf_op jit(solution)/shard_map/all_to_all | solution.py:384
  80.8 4.5 %collective-permute-start.4 = (f32[5,2,16,128]{3,2,1,0:T(8,128)S(1)}, f32[5,2,16,128]{3,2,1,0:T(8,128)S(1)}, u32[]{:S(2)}, u32[]{:S(2)}) collective-permute-start(f32[5,2,16,128]{3,2,1,0:T(8,128)S(1)} %get-tuple-element.44), channel_id=1, source_target_pairs={{1,2},{3,4},{5,6},{7,8},{9,10},{11,12},{13,14},{15,16},{17,18},{19... | collective-permute-start | bytes 245768 | tf_op jit(solution)/shard_map/ppermute | solution.py:380
  85.3 1.9 %collective-permute-start.5 = (f32[5,2,16,128]{3,2,1,0:T(8,128)S(1)}, f32[5,2,16,128]{3,2,1,0:T(8,128)S(1)}, u32[]{:S(2)}, u32[]{:S(2)}) collective-permute-start(f32[5,2,16,128]{3,2,1,0:T(8,128)S(1)} %get-tuple-element.45), channel_id=1, source_target_pairs={{0,1},{2,3},{4,5},{6,7},{8,9},{10,11},{12,13},{14,15},{16,17},{18,... | collective-permute-start | bytes 245768 | tf_op jit(solution)/shard_map/ppermute | solution.py:380
  87.7 1.0 collective-permute-done.4.refs_5_
  88.9 4.8 %collective-permute-start.6 = (f32[5,2,16,128]{3,2,1,0:T(8,128)S(1)}, f32[5,2,16,128]{3,2,1,0:T(8,128)S(1)}, u32[]{:S(2)}, u32[]{:S(2)}) collective-permute-start(f32[5,2,16,128]{3,2,1,0:T(8,128)S(1)} %get-tuple-element.47), channel_id=1, source_target_pairs={{1,2},{3,4},{5,6},{7,8},{9,10},{11,12},{13,14},{15,16},{17,18},{19... | collective-permute-start | bytes 245768 | tf_op jit(solution)/shard_map/ppermute | solution.py:380
  93.7 1.9 %collective-permute-start.7 = (f32[5,2,16,128]{3,2,1,0:T(8,128)S(1)}, f32[5,2,16,128]{3,2,1,0:T(8,128)S(1)}, u32[]{:S(2)}, u32[]{:S(2)}) collective-permute-start(f32[5,2,16,128]{3,2,1,0:T(8,128)S(1)} %get-tuple-element.48), channel_id=1, source_target_pairs={{0,1},{2,3},{4,5},{6,7},{8,9},{10,11},{12,13},{14,15},{16,17},{18,... | collective-permute-start | bytes 245768 | tf_op jit(solution)/shard_map/ppermute | solution.py:380
  96.1 0.6 collective-permute-done.6.refs_5_
  97.1 15.1 %all_to_all.33.refs_3_ = f32[16,5,8,128]{3,2,1,0:T(8,128)S(1)} all-to-all(f32[16,5,8,128]{3,2,1,0:T(8,128)S(1)} %shard_map.93), channel_id=1, replica_groups={{288,384,160,256,448,32,416,128,192,0,352,224,64,96,320,480},{289,385,1..., dimensions={0} | all-to-all | bytes 655360 | tf_op jit(solution)/shard_map/all_to_all | solution.py:384
  112.6 13.9 %all_to_all.34.back = f32[16,5,8,128]{3,2,1,0:T(8,128)S(1)} all-to-all(f32[16,5,8,128]{3,2,1,0:T(8,128)S(1)} %shard_map.94), channel_id=1, replica_groups={{288,384,160,256,448,32,416,128,192,0,352,224,64,96,320,480},{289,385,1..., dimensions={0} | all-to-all | bytes 655360 | tf_op jit(solution)/shard_map/all_to_all | solution.py:384
  126.6 8.8 %collective-permute-start.8 = (f32[5,2,16,128]{3,2,1,0:T(8,128)S(1)}, f32[5,2,16,128]{3,2,1,0:T(8,128)S(1)}, u32[]{:S(2)}, u32[]{:S(2)}) collective-permute-start(f32[5,2,16,128]{3,2,1,0:T(8,128)S(1)} %get-tuple-element.51), channel_id=1, source_target_pairs={{1,2},{3,4},{5,6},{7,8},{9,10},{11,12},{13,14},{15,16},{17,18},{19... | collective-permute-start | bytes 245768 | tf_op jit(solution)/shard_map/ppermute | solution.py:380
  135.4 1.9 %collective-permute-start.9 = (f32[5,2,16,128]{3,2,1,0:T(8,128)S(1)}, f32[5,2,16,128]{3,2,1,0:T(8,128)S(1)}, u32[]{:S(2)}, u32[]{:S(2)}) collective-permute-start(f32[5,2,16,128]{3,2,1,0:T(8,128)S(1)} %get-tuple-element.52), channel_id=1, source_target_pairs={{0,1},{2,3},{4,5},{6,7},{8,9},{10,11},{12,13},{14,15},{16,17},{18,... | collective-permute-start | bytes 245768 | tf_op jit(solution)/shard_map/ppermute | solution.py:380
  137.8 0.8 collective-permute-done.9.refs_6_
  138.5 0.8 shard_map.97
  (19 shorter events, 3.6 us)
Async XLA Ops:
  2.3 21.1 %all-to-all-start = ((f32[16,3,8,128]{3,2,1,0:T(8,128)}), f32[16,3,8,128]{3,2,1,0:T(8,128)S(1)}, u32[]{:S(2)}, u32[]{:S(2)}) async-start(f32[16,3,8,128]{3,2,1,0:T(8,128)} %get-tuple-element.37), calls=%async_computation | async-start | bytes 393216 | tf_op jit(solution)/shard_map/all_to_all | solution.py:384
  11.7 11.7 %collective-permute-start = (f32[7,2,16,128]{3,2,1,0:T(8,128)}, f32[7,2,16,128]{3,2,1,0:T(8,128)S(1)}, u32[]{:S(2)}, u32[]{:S(2)}) collective-permute-start(f32[7,2,16,128]{3,2,1,0:T(8,128)} %get-tuple-element.35), channel_id=1, source_target_pairs={{1,2},{3,4},{5,6},{7,8},{9,10},{11,12},{13,14},{15,16},{17,18},{19... | collective-permute-start | bytes 344072 | tf_op jit(solution)/shard_map/ppermute | solution.py:380
  18.4 5.1 %collective-permute-start.1 = (f32[7,2,16,128]{3,2,1,0:T(8,128)S(1)}, f32[7,2,16,128]{3,2,1,0:T(8,128)S(1)}, u32[]{:S(2)}, u32[]{:S(2)}) collective-permute-start(f32[7,2,16,128]{3,2,1,0:T(8,128)S(1)} %get-tuple-element.36), channel_id=1, source_target_pairs={{0,1},{2,3},{4,5},{6,7},{8,9},{10,11},{12,13},{14,15},{16,17},{18,... | collective-permute-start | bytes 344072 | tf_op jit(solution)/shard_map/ppermute | solution.py:380
  37.8 8.5 %collective-permute-start.2 = (f32[5,2,16,128]{3,2,1,0:T(8,128)S(1)}, f32[5,2,16,128]{3,2,1,0:T(8,128)S(1)}, u32[]{:S(2)}, u32[]{:S(2)}) collective-permute-start(f32[5,2,16,128]{3,2,1,0:T(8,128)S(1)} %get-tuple-element.40), channel_id=1, source_target_pairs={{1,2},{3,4},{5,6},{7,8},{9,10},{11,12},{13,14},{15,16},{17,18},{19... | collective-permute-start | bytes 245768 | tf_op jit(solution)/shard_map/ppermute | solution.py:380
  42.9 3.4 %collective-permute-start.3 = (f32[5,2,16,128]{3,2,1,0:T(8,128)S(1)}, f32[5,2,16,128]{3,2,1,0:T(8,128)S(1)}, u32[]{:S(2)}, u32[]{:S(2)}) collective-permute-start(f32[5,2,16,128]{3,2,1,0:T(8,128)S(1)} %get-tuple-element.41), channel_id=1, source_target_pairs={{0,1},{2,3},{4,5},{6,7},{8,9},{10,11},{12,13},{14,15},{16,17},{18,... | collective-permute-start | bytes 245768 | tf_op jit(solution)/shard_map/ppermute | solution.py:380
  80.8 7.9 %collective-permute-start.4 = (f32[5,2,16,128]{3,2,1,0:T(8,128)S(1)}, f32[5,2,16,128]{3,2,1,0:T(8,128)S(1)}, u32[]{:S(2)}, u32[]{:S(2)}) collective-permute-start(f32[5,2,16,128]{3,2,1,0:T(8,128)S(1)} %get-tuple-element.44), channel_id=1, source_target_pairs={{1,2},{3,4},{5,6},{7,8},{9,10},{11,12},{13,14},{15,16},{17,18},{19... | collective-permute-start | bytes 245768 | tf_op jit(solution)/shard_map/ppermute | solution.py:380
  85.3 3.4 %collective-permute-start.5 = (f32[5,2,16,128]{3,2,1,0:T(8,128)S(1)}, f32[5,2,16,128]{3,2,1,0:T(8,128)S(1)}, u32[]{:S(2)}, u32[]{:S(2)}) collective-permute-start(f32[5,2,16,128]{3,2,1,0:T(8,128)S(1)} %get-tuple-element.45), channel_id=1, source_target_pairs={{0,1},{2,3},{4,5},{6,7},{8,9},{10,11},{12,13},{14,15},{16,17},{18,... | collective-permute-start | bytes 245768 | tf_op jit(solution)/shard_map/ppermute | solution.py:380
  88.9 7.9 %collective-permute-start.6 = (f32[5,2,16,128]{3,2,1,0:T(8,128)S(1)}, f32[5,2,16,128]{3,2,1,0:T(8,128)S(1)}, u32[]{:S(2)}, u32[]{:S(2)}) collective-permute-start(f32[5,2,16,128]{3,2,1,0:T(8,128)S(1)} %get-tuple-element.47), channel_id=1, source_target_pairs={{1,2},{3,4},{5,6},{7,8},{9,10},{11,12},{13,14},{15,16},{17,18},{19... | collective-permute-start | bytes 245768 | tf_op jit(solution)/shard_map/ppermute | solution.py:380
  93.7 3.2 %collective-permute-start.7 = (f32[5,2,16,128]{3,2,1,0:T(8,128)S(1)}, f32[5,2,16,128]{3,2,1,0:T(8,128)S(1)}, u32[]{:S(2)}, u32[]{:S(2)}) collective-permute-start(f32[5,2,16,128]{3,2,1,0:T(8,128)S(1)} %get-tuple-element.48), channel_id=1, source_target_pairs={{0,1},{2,3},{4,5},{6,7},{8,9},{10,11},{12,13},{14,15},{16,17},{18,... | collective-permute-start | bytes 245768 | tf_op jit(solution)/shard_map/ppermute | solution.py:380
  126.6 11.2 %collective-permute-start.8 = (f32[5,2,16,128]{3,2,1,0:T(8,128)S(1)}, f32[5,2,16,128]{3,2,1,0:T(8,128)S(1)}, u32[]{:S(2)}, u32[]{:S(2)}) collective-permute-start(f32[5,2,16,128]{3,2,1,0:T(8,128)S(1)} %get-tuple-element.51), channel_id=1, source_target_pairs={{1,2},{3,4},{5,6},{7,8},{9,10},{11,12},{13,14},{15,16},{17,18},{19... | collective-permute-start | bytes 245768 | tf_op jit(solution)/shard_map/ppermute | solution.py:380
  135.4 3.2 %collective-permute-start.9 = (f32[5,2,16,128]{3,2,1,0:T(8,128)S(1)}, f32[5,2,16,128]{3,2,1,0:T(8,128)S(1)}, u32[]{:S(2)}, u32[]{:S(2)}) collective-permute-start(f32[5,2,16,128]{3,2,1,0:T(8,128)S(1)} %get-tuple-element.52), channel_id=1, source_target_pairs={{0,1},{2,3},{4,5},{6,7},{8,9},{10,11},{12,13},{14,15},{16,17},{18,... | collective-permute-start | bytes 245768 | tf_op jit(solution)/shard_map/ppermute | solution.py:380

commit v9 on v6

--- a/solution.py
+++ b/solution.py
@@ -81,26 +81,26 @@
             odd_ref[row, layer] = read(row, 2 - first + layer)
 
 
-def load(sources, targets, sems):
+def copies_of(sources, targets, sems):
     copies = [
         pltpu.make_async_copy(source, target, sems.at[i])
         for i, (source, target) in enumerate(zip(sources, targets))
     ]
     for copy in copies:
         copy.start()
-    for copy in copies:
+    return copies
+
+
+def load_kernel(gradient, jacobian, gradient_out, jacobian_out, sems):
+    for copy in copies_of((gradient, jacobian), (gradient_out, jacobian_out), sems):
         copy.wait()
-
-
-def load_kernel(*refs):
-    half = len(refs) // 2
-    load(refs[:half], refs[half:-1], refs[-1])
 
 
 def pack_kernel(*refs):
     message, odd_ref, even_ref = refs[4:7]
     adjoint, second, fourth, step = refs[7:11]
-    load(refs[:4], refs[7:11], refs[11])
+    for copy in copies_of(refs[:4], refs[7:11], refs[11]):
+        copy.wait()
     for layer in range(LAYERS):
         for quarter in range(4):
             rows = slice(4 * quarter, 4 * quarter + 4)
@@ -168,7 +168,7 @@
             finish(var, layer, damped[var] + 0.5 * acc)
         return carry
 
-    lax.fori_loop(0, LAYERS, layer_step, 0)
+    lax.fori_loop(0, LAYERS, layer_step, 0, unroll=4)
 
 
 def spatial_x(field, staged, coefs, jacobian, damped, finish):
@@ -362,7 +362,7 @@
             out[PLACE[k], index] = jnp.where(low, pltpu.roll(value, 4, 0), moved[k])
         return carry
 
-    lax.fori_loop(0, VARS, tile, 0)
+    lax.fori_loop(0, VARS, tile, 0, unroll=True)
 
 
 def exchange(odd, even):

time: 140 us -> 140 us (level)
  Pallas kernels: 11.1 us -> 8.5 us
  waiting for transfers between devices: 1.78 us -> 3.59 us
    pallas_call x16, Pallas kernels: 11.1 us -> 8.5 us  [call(): pl.pallas_call(kernel, out_shape=outs, in_specs=specs or [VMEM] * len(arg...]
  transfers between devices with their start and end apart: 11 -> 11, of which waited for: 4 -> 5; matrix products, arithmetic and copies ran while one was open for 0% -> 0% of each run, Pallas kernels for 4% -> 3%
where the time goes in v9:
time: 140 us; the launch traced here: 139 us
  blocking collectives  76.4 us (55%)
  starting transfers between devices  48.9 us (35%)
  Pallas kernels  8.5 us (6%)
  waiting for transfers between devices  3.59 us (3%)
  between operations  1.5 us (1%)
    all_to_all x5, blocking collectives, across(): lax.all_to_all(message, 'inst', 0, 0, axis_index_groups=[ORDER], tiled=True)  76.4 us
    ppermute x5, starting transfers between devices, exchange(): lax.ppermute(odd, 'cells', PAIRS_ODD)  29.9 us
    ppermute x5, starting transfers between devices, exchange(): lax.ppermute(even, 'cells', PAIRS_EVEN)  9.6 us
    all_to_all x1, starting transfers between devices, across(): lax.all_to_all(message, 'inst', 0, 0, axis_index_groups=[ORDER], tiled=True)  9.39 us
    pallas_call x16, Pallas kernels, call(): pl.pallas_call(kernel, out_shape=outs, in_specs=specs or [VMEM] * len(arg...  8.5 us
  transfers between devices with their start and end apart: 11, of which 5 were waited for; matrix products, arithmetic and copies ran while one was open for 0% of the time, Pallas kernels for 3%

profile of v9, /device:TPU:201, one launch (start us, length us, event | category | flops | bytes accessed | tf_op | source)
XLA Modules:
  0.0 138.8 jit_solution(4545138274864195771)
XLA Ops:
  0.0 1.8 %shard_map.82 = (f32[16,3,8,128]{3,2,1,0:T(8,128)}, f32[7,2,16,128]{3,2,1,0:T(8,128)}, f32[7,2,16,128]{3,2,1,0:T(8,128)S(1)}, f32[5,4,16,128]{3,2,1,0:T(8,128)S(...) custom-call(f32[5,4,16,128]{3,2,1,0:T(8,128)} %bitcast.9, ...), custom_call_target="tpu_custom_call" | custom-call | bytes 1212416 | tf_op jit(solution)/shard_map/pallas_call | solution.py:61
  1.8 9.4 %all-to-all-start = ((f32[16,3,8,128]{3,2,1,0:T(8,128)}), f32[16,3,8,128]{3,2,1,0:T(8,128)S(1)}, u32[]{:S(2)}, u32[]{:S(2)}) async-start(f32[16,3,8,128]{3,2,1,0:T(8,128)} %get-tuple-element.37), calls=%async_computation | async-start | bytes 393216 | tf_op jit(solution)/shard_map/all_to_all | solution.py:373
  11.2 6.7 %collective-permute-start = (f32[7,2,16,128]{3,2,1,0:T(8,128)}, f32[7,2,16,128]{3,2,1,0:T(8,128)S(1)}, u32[]{:S(2)}, u32[]{:S(2)}) collective-permute-start(f32[7,2,16,128]{3,2,1,0:T(8,128)} %get-tuple-element.35), channel_id=1, source_target_pairs={{1,2},{3,4},{5,6},{7,8},{9,10},{11,12},{13,14},{15,16},{17,18},{19... | collective-permute-start | bytes 344072 | tf_op jit(solution)/shard_map/ppermute | solution.py:369
  17.9 1.9 %collective-permute-start.1 = (f32[7,2,16,128]{3,2,1,0:T(8,128)S(1)}, f32[7,2,16,128]{3,2,1,0:T(8,128)S(1)}, u32[]{:S(2)}, u32[]{:S(2)}) collective-permute-start(f32[7,2,16,128]{3,2,1,0:T(8,128)S(1)} %get-tuple-element.36), channel_id=1, source_target_pairs={{0,1},{2,3},{4,5},{6,7},{8,9},{10,11},{12,13},{14,15},{16,17},{18,... | collective-permute-start | bytes 344072 | tf_op jit(solution)/shard_map/ppermute | solution.py:369
  21.1 1.8 %shard_map.83 = (f32[5,4,16,128]{3,2,1,0:T(8,128)S(1)}, f32[3,5,5,4,16,128]{5,4,3,2,1,0:T(8,128)S(1)}) custom-call(f32[5,4,16,128]{3,2,1,0:T(8,128)} %bitcast.8, f32[3,5,5,4,16,128]{5,4,3,2,1,0:T(8,128)} %bitcast.7), custom_call_target="tpu_custom_call" | custom-call | bytes 5242880 | tf_op jit(solution)/shard_map/pallas_call | solution.py:61
  23.1 13.6 %all_to_all.30.refs_8_ = f32[16,5,4,128]{3,2,1,0:T(4,128)S(1)} all-to-all(f32[16,5,4,128]{3,2,1,0:T(4,128)S(1)} %shard_map.84), channel_id=1, replica_groups={{288,384,160,256,448,32,416,128,192,0,352,224,64,96,320,480},{289,385,1..., dimensions={0} | all-to-all | bytes 327680 | tf_op jit(solution)/shard_map/all_to_all | solution.py:373
  36.6 0.7 shard_map.85
  37.3 5.1 %collective-permute-start.2 = (f32[5,2,16,128]{3,2,1,0:T(8,128)S(1)}, f32[5,2,16,128]{3,2,1,0:T(8,128)S(1)}, u32[]{:S(2)}, u32[]{:S(2)}) collective-permute-start(f32[5,2,16,128]{3,2,1,0:T(8,128)S(1)} %get-tuple-element.40), channel_id=1, source_target_pairs={{1,2},{3,4},{5,6},{7,8},{9,10},{11,12},{13,14},{15,16},{17,18},{19... | collective-permute-start | bytes 245768 | tf_op jit(solution)/shard_map/ppermute | solution.py:369
  42.4 1.9 %collective-permute-start.3 = (f32[5,2,16,128]{3,2,1,0:T(8,128)S(1)}, f32[5,2,16,128]{3,2,1,0:T(8,128)S(1)}, u32[]{:S(2)}, u32[]{:S(2)}) collective-permute-start(f32[5,2,16,128]{3,2,1,0:T(8,128)S(1)} %get-tuple-element.41), channel_id=1, source_target_pairs={{0,1},{2,3},{4,5},{6,7},{8,9},{10,11},{12,13},{14,15},{16,17},{18,... | collective-permute-start | bytes 245768 | tf_op jit(solution)/shard_map/ppermute | solution.py:369
  44.8 1.0 collective-permute-done.2.refs_5_
  46.0 17.5 %all_to_all.31.refs_3_ = f32[16,5,8,128]{3,2,1,0:T(8,128)S(1)} all-to-all(f32[16,5,8,128]{3,2,1,0:T(8,128)S(1)} %shard_map.87), channel_id=1, replica_groups={{288,384,160,256,448,32,416,128,192,0,352,224,64,96,320,480},{289,385,1..., dimensions={0} | all-to-all | bytes 655360 | tf_op jit(solution)/shard_map/all_to_all | solution.py:373
  63.9 16.3 %all_to_all.32.back = f32[16,5,8,128]{3,2,1,0:T(8,128)S(1)} all-to-all(f32[16,5,8,128]{3,2,1,0:T(8,128)S(1)} %shard_map.88), channel_id=1, replica_groups={{288,384,160,256,448,32,416,128,192,0,352,224,64,96,320,480},{289,385,1..., dimensions={0} | all-to-all | bytes 655360 | tf_op jit(solution)/shard_map/all_to_all | solution.py:373
  80.3 4.5 %collective-permute-start.4 = (f32[5,2,16,128]{3,2,1,0:T(8,128)S(1)}, f32[5,2,16,128]{3,2,1,0:T(8,128)S(1)}, u32[]{:S(2)}, u32[]{:S(2)}) collective-permute-start(f32[5,2,16,128]{3,2,1,0:T(8,128)S(1)} %get-tuple-element.44), channel_id=1, source_target_pairs={{1,2},{3,4},{5,6},{7,8},{9,10},{11,12},{13,14},{15,16},{17,18},{19... | collective-permute-start | bytes 245768 | tf_op jit(solution)/shard_map/ppermute | solution.py:369
  84.8 1.9 %collective-permute-start.5 = (f32[5,2,16,128]{3,2,1,0:T(8,128)S(1)}, f32[5,2,16,128]{3,2,1,0:T(8,128)S(1)}, u32[]{:S(2)}, u32[]{:S(2)}) collective-permute-start(f32[5,2,16,128]{3,2,1,0:T(8,128)S(1)} %get-tuple-element.45), channel_id=1, source_target_pairs={{0,1},{2,3},{4,5},{6,7},{8,9},{10,11},{12,13},{14,15},{16,17},{18,... | collective-permute-start | bytes 245768 | tf_op jit(solution)/shard_map/ppermute | solution.py:369
  87.2 1.0 collective-permute-done.4.refs_5_
  88.4 4.8 %collective-permute-start.6 = (f32[5,2,16,128]{3,2,1,0:T(8,128)S(1)}, f32[5,2,16,128]{3,2,1,0:T(8,128)S(1)}, u32[]{:S(2)}, u32[]{:S(2)}) collective-permute-start(f32[5,2,16,128]{3,2,1,0:T(8,128)S(1)} %get-tuple-element.47), channel_id=1, source_target_pairs={{1,2},{3,4},{5,6},{7,8},{9,10},{11,12},{13,14},{15,16},{17,18},{19... | collective-permute-start | bytes 245768 | tf_op jit(solution)/shard_map/ppermute | solution.py:369
  93.2 1.9 %collective-permute-start.7 = (f32[5,2,16,128]{3,2,1,0:T(8,128)S(1)}, f32[5,2,16,128]{3,2,1,0:T(8,128)S(1)}, u32[]{:S(2)}, u32[]{:S(2)}) collective-permute-start(f32[5,2,16,128]{3,2,1,0:T(8,128)S(1)} %get-tuple-element.48), channel_id=1, source_target_pairs={{0,1},{2,3},{4,5},{6,7},{8,9},{10,11},{12,13},{14,15},{16,17},{18,... | collective-permute-start | bytes 245768 | tf_op jit(solution)/shard_map/ppermute | solution.py:369
  95.6 0.6 collective-permute-done.6.refs_5_
  96.6 15.1 %all_to_all.33.refs_3_ = f32[16,5,8,128]{3,2,1,0:T(8,128)S(1)} all-to-all(f32[16,5,8,128]{3,2,1,0:T(8,128)S(1)} %shard_map.93), channel_id=1, replica_groups={{288,384,160,256,448,32,416,128,192,0,352,224,64,96,320,480},{289,385,1..., dimensions={0} | all-to-all | bytes 655360 | tf_op jit(solution)/shard_map/all_to_all | solution.py:373
  112.0 13.9 %all_to_all.34.back = f32[16,5,8,128]{3,2,1,0:T(8,128)S(1)} all-to-all(f32[16,5,8,128]{3,2,1,0:T(8,128)S(1)} %shard_map.94), channel_id=1, replica_groups={{288,384,160,256,448,32,416,128,192,0,352,224,64,96,320,480},{289,385,1..., dimensions={0} | all-to-all | bytes 655360 | tf_op jit(solution)/shard_map/all_to_all | solution.py:373
  126.0 8.8 %collective-permute-start.8 = (f32[5,2,16,128]{3,2,1,0:T(8,128)S(1)}, f32[5,2,16,128]{3,2,1,0:T(8,128)S(1)}, u32[]{:S(2)}, u32[]{:S(2)}) collective-permute-start(f32[5,2,16,128]{3,2,1,0:T(8,128)S(1)} %get-tuple-element.51), channel_id=1, source_target_pairs={{1,2},{3,4},{5,6},{7,8},{9,10},{11,12},{13,14},{15,16},{17,18},{19... | collective-permute-start | bytes 245768 | tf_op jit(solution)/shard_map/ppermute | solution.py:369
  134.8 1.9 %collective-permute-start.9 = (f32[5,2,16,128]{3,2,1,0:T(8,128)S(1)}, f32[5,2,16,128]{3,2,1,0:T(8,128)S(1)}, u32[]{:S(2)}, u32[]{:S(2)}) collective-permute-start(f32[5,2,16,128]{3,2,1,0:T(8,128)S(1)} %get-tuple-element.52), channel_id=1, source_target_pairs={{0,1},{2,3},{4,5},{6,7},{8,9},{10,11},{12,13},{14,15},{16,17},{18,... | collective-permute-start | bytes 245768 | tf_op jit(solution)/shard_map/ppermute | solution.py:369
  137.2 0.8 collective-permute-done.9.refs_6_
  138.0 0.8 shard_map.97
  (19 shorter events, 3.6 us)
Async XLA Ops:
  1.8 21.1 %all-to-all-start = ((f32[16,3,8,128]{3,2,1,0:T(8,128)}), f32[16,3,8,128]{3,2,1,0:T(8,128)S(1)}, u32[]{:S(2)}, u32[]{:S(2)}) async-start(f32[16,3,8,128]{3,2,1,0:T(8,128)} %get-tuple-element.37), calls=%async_computation | async-start | bytes 393216 | tf_op jit(solution)/shard_map/all_to_all | solution.py:373
  11.2 11.7 %collective-permute-start = (f32[7,2,16,128]{3,2,1,0:T(8,128)}, f32[7,2,16,128]{3,2,1,0:T(8,128)S(1)}, u32[]{:S(2)}, u32[]{:S(2)}) collective-permute-start(f32[7,2,16,128]{3,2,1,0:T(8,128)} %get-tuple-element.35), channel_id=1, source_target_pairs={{1,2},{3,4},{5,6},{7,8},{9,10},{11,12},{13,14},{15,16},{17,18},{19... | collective-permute-start | bytes 344072 | tf_op jit(solution)/shard_map/ppermute | solution.py:369
  17.9 5.1 %collective-permute-start.1 = (f32[7,2,16,128]{3,2,1,0:T(8,128)S(1)}, f32[7,2,16,128]{3,2,1,0:T(8,128)S(1)}, u32[]{:S(2)}, u32[]{:S(2)}) collective-permute-start(f32[7,2,16,128]{3,2,1,0:T(8,128)S(1)} %get-tuple-element.36), channel_id=1, source_target_pairs={{0,1},{2,3},{4,5},{6,7},{8,9},{10,11},{12,13},{14,15},{16,17},{18,... | collective-permute-start | bytes 344072 | tf_op jit(solution)/shard_map/ppermute | solution.py:369
  37.3 8.5 %collective-permute-start.2 = (f32[5,2,16,128]{3,2,1,0:T(8,128)S(1)}, f32[5,2,16,128]{3,2,1,0:T(8,128)S(1)}, u32[]{:S(2)}, u32[]{:S(2)}) collective-permute-start(f32[5,2,16,128]{3,2,1,0:T(8,128)S(1)} %get-tuple-element.40), channel_id=1, source_target_pairs={{1,2},{3,4},{5,6},{7,8},{9,10},{11,12},{13,14},{15,16},{17,18},{19... | collective-permute-start | bytes 245768 | tf_op jit(solution)/shard_map/ppermute | solution.py:369
  42.4 3.4 %collective-permute-start.3 = (f32[5,2,16,128]{3,2,1,0:T(8,128)S(1)}, f32[5,2,16,128]{3,2,1,0:T(8,128)S(1)}, u32[]{:S(2)}, u32[]{:S(2)}) collective-permute-start(f32[5,2,16,128]{3,2,1,0:T(8,128)S(1)} %get-tuple-element.41), channel_id=1, source_target_pairs={{0,1},{2,3},{4,5},{6,7},{8,9},{10,11},{12,13},{14,15},{16,17},{18,... | collective-permute-start | bytes 245768 | tf_op jit(solution)/shard_map/ppermute | solution.py:369
  80.3 7.9 %collective-permute-start.4 = (f32[5,2,16,128]{3,2,1,0:T(8,128)S(1)}, f32[5,2,16,128]{3,2,1,0:T(8,128)S(1)}, u32[]{:S(2)}, u32[]{:S(2)}) collective-permute-start(f32[5,2,16,128]{3,2,1,0:T(8,128)S(1)} %get-tuple-element.44), channel_id=1, source_target_pairs={{1,2},{3,4},{5,6},{7,8},{9,10},{11,12},{13,14},{15,16},{17,18},{19... | collective-permute-start | bytes 245768 | tf_op jit(solution)/shard_map/ppermute | solution.py:369
  84.8 3.4 %collective-permute-start.5 = (f32[5,2,16,128]{3,2,1,0:T(8,128)S(1)}, f32[5,2,16,128]{3,2,1,0:T(8,128)S(1)}, u32[]{:S(2)}, u32[]{:S(2)}) collective-permute-start(f32[5,2,16,128]{3,2,1,0:T(8,128)S(1)} %get-tuple-element.45), channel_id=1, source_target_pairs={{0,1},{2,3},{4,5},{6,7},{8,9},{10,11},{12,13},{14,15},{16,17},{18,... | collective-permute-start | bytes 245768 | tf_op jit(solution)/shard_map/ppermute | solution.py:369
  88.4 7.9 %collective-permute-start.6 = (f32[5,2,16,128]{3,2,1,0:T(8,128)S(1)}, f32[5,2,16,128]{3,2,1,0:T(8,128)S(1)}, u32[]{:S(2)}, u32[]{:S(2)}) collective-permute-start(f32[5,2,16,128]{3,2,1,0:T(8,128)S(1)} %get-tuple-element.47), channel_id=1, source_target_pairs={{1,2},{3,4},{5,6},{7,8},{9,10},{11,12},{13,14},{15,16},{17,18},{19... | collective-permute-start | bytes 245768 | tf_op jit(solution)/shard_map/ppermute | solution.py:369
  93.2 3.2 %collective-permute-start.7 = (f32[5,2,16,128]{3,2,1,0:T(8,128)S(1)}, f32[5,2,16,128]{3,2,1,0:T(8,128)S(1)}, u32[]{:S(2)}, u32[]{:S(2)}) collective-permute-start(f32[5,2,16,128]{3,2,1,0:T(8,128)S(1)} %get-tuple-element.48), channel_id=1, source_target_pairs={{0,1},{2,3},{4,5},{6,7},{8,9},{10,11},{12,13},{14,15},{16,17},{18,... | collective-permute-start | bytes 245768 | tf_op jit(solution)/shard_map/ppermute | solution.py:369
  126.0 11.2 %collective-permute-start.8 = (f32[5,2,16,128]{3,2,1,0:T(8,128)S(1)}, f32[5,2,16,128]{3,2,1,0:T(8,128)S(1)}, u32[]{:S(2)}, u32[]{:S(2)}) collective-permute-start(f32[5,2,16,128]{3,2,1,0:T(8,128)S(1)} %get-tuple-element.51), channel_id=1, source_target_pairs={{1,2},{3,4},{5,6},{7,8},{9,10},{11,12},{13,14},{15,16},{17,18},{19... | collective-permute-start | bytes 245768 | tf_op jit(solution)/shard_map/ppermute | solution.py:369
  134.8 3.2 %collective-permute-start.9 = (f32[5,2,16,128]{3,2,1,0:T(8,128)S(1)}, f32[5,2,16,128]{3,2,1,0:T(8,128)S(1)}, u32[]{:S(2)}, u32[]{:S(2)}) collective-permute-start(f32[5,2,16,128]{3,2,1,0:T(8,128)S(1)} %get-tuple-element.52), channel_id=1, source_target_pairs={{0,1},{2,3},{4,5},{6,7},{8,9},{10,11},{12,13},{14,15},{16,17},{18,... | collective-permute-start | bytes 245768 | tf_op jit(solution)/shard_map/ppermute | solution.py:369

commit v10 on v9

--- a/solution.py
+++ b/solution.py
@@ -29,7 +29,7 @@
     (i + 1, i) for i in range(1, DEVICES - 1, 2)
 ]
 
-ORDER = (9, 12, 5, 8, 14, 1, 13, 4, 6, 0, 11, 7, 2, 3, 10, 15)
+ORDER = (9, 7, 5, 8, 14, 1, 13, 4, 6, 0, 11, 12, 2, 3, 10, 15)
 PLACE = [ORDER.index(j) for j in range(INSTANCES)]
 
 FIELD = (VARS, LAYERS, NY, NZ)

time: 140 us -> 139 us (level)
  starting transfers between devices: 48.9 us -> 42.9 us
  blocking collectives: 76.4 us -> 79.7 us
  waiting for transfers between devices: 3.59 us -> 5.91 us
    ppermute x5, starting transfers between devices: 29.9 us -> 23.9 us  [exchange(): lax.ppermute(odd, 'cells', PAIRS_ODD)]
    all_to_all x5, blocking collectives: 76.4 us -> 79.7 us  [across(): lax.all_to_all(message, 'inst', 0, 0, axis_index_groups=[ORDER], tiled=True)]
    ppermute x5, waiting for transfers between devices: 2.66 us -> 5.9 us  [exchange(): lax.ppermute(odd, 'cells', PAIRS_ODD)]
  transfers between devices with their start and end apart: 11 -> 11, of which waited for: 5 -> 4; matrix products, arithmetic and copies ran while one was open for 0% -> 0% of each run, Pallas kernels for 3% -> 3%
where the time goes in v10:
time: 139 us; the launch traced here: 138 us
  blocking collectives  79.7 us (57%)
  starting transfers between devices  42.9 us (31%)
  Pallas kernels  8.5 us (6%)
  waiting for transfers between devices  5.91 us (4%)
  between operations  1.5 us (1%)
    all_to_all x5, blocking collectives, across(): lax.all_to_all(message, 'inst', 0, 0, axis_index_groups=[ORDER], tiled=True)  79.7 us
    ppermute x5, starting transfers between devices, exchange(): lax.ppermute(odd, 'cells', PAIRS_ODD)  23.9 us
    ppermute x5, starting transfers between devices, exchange(): lax.ppermute(even, 'cells', PAIRS_EVEN)  9.6 us
    all_to_all x1, starting transfers between devices, across(): lax.all_to_all(message, 'inst', 0, 0, axis_index_groups=[ORDER], tiled=True)  9.39 us
    pallas_call x16, Pallas kernels, call(): pl.pallas_call(kernel, out_shape=outs, in_specs=specs or [VMEM] * len(arg...  8.5 us
    ppermute x5, waiting for transfers between devices, exchange(): lax.ppermute(odd, 'cells', PAIRS_ODD)  5.9 us
  transfers between devices with their start and end apart: 11, of which 4 were waited for; matrix products, arithmetic and copies ran while one was open for 0% of the time, Pallas kernels for 3%

profile of v10, /device:TPU:201, one launch (start us, length us, event | category | flops | bytes accessed | tf_op | source)
XLA Modules:
  0.0 138.5 jit_solution(3893074275816753151)
XLA Ops:
  0.0 1.8 %shard_map.82 = (f32[16,3,8,128]{3,2,1,0:T(8,128)}, f32[7,2,16,128]{3,2,1,0:T(8,128)}, f32[7,2,16,128]{3,2,1,0:T(8,128)S(1)}, f32[5,4,16,128]{3,2,1,0:T(8,128)S(...) custom-call(f32[5,4,16,128]{3,2,1,0:T(8,128)} %bitcast.9, ...), custom_call_target="tpu_custom_call" | custom-call | bytes 1212416 | tf_op jit(solution)/shard_map/pallas_call | solution.py:61
  1.8 9.4 %all-to-all-start = ((f32[16,3,8,128]{3,2,1,0:T(8,128)}), f32[16,3,8,128]{3,2,1,0:T(8,128)S(1)}, u32[]{:S(2)}, u32[]{:S(2)}) async-start(f32[16,3,8,128]{3,2,1,0:T(8,128)} %get-tuple-element.37), calls=%async_computation | async-start | bytes 393216 | tf_op jit(solution)/shard_map/all_to_all | solution.py:373
  11.2 6.7 %collective-permute-start = (f32[7,2,16,128]{3,2,1,0:T(8,128)}, f32[7,2,16,128]{3,2,1,0:T(8,128)S(1)}, u32[]{:S(2)}, u32[]{:S(2)}) collective-permute-start(f32[7,2,16,128]{3,2,1,0:T(8,128)} %get-tuple-element.35), channel_id=1, source_target_pairs={{1,2},{3,4},{5,6},{7,8},{9,10},{11,12},{13,14},{15,16},{17,18},{19... | collective-permute-start | bytes 344072 | tf_op jit(solution)/shard_map/ppermute | solution.py:369
  17.9 1.9 %collective-permute-start.1 = (f32[7,2,16,128]{3,2,1,0:T(8,128)S(1)}, f32[7,2,16,128]{3,2,1,0:T(8,128)S(1)}, u32[]{:S(2)}, u32[]{:S(2)}) collective-permute-start(f32[7,2,16,128]{3,2,1,0:T(8,128)S(1)} %get-tuple-element.36), channel_id=1, source_target_pairs={{0,1},{2,3},{4,5},{6,7},{8,9},{10,11},{12,13},{14,15},{16,17},{18,... | collective-permute-start | bytes 344072 | tf_op jit(solution)/shard_map/ppermute | solution.py:369
  21.1 1.8 %shard_map.83 = (f32[5,4,16,128]{3,2,1,0:T(8,128)S(1)}, f32[3,5,5,4,16,128]{5,4,3,2,1,0:T(8,128)S(1)}) custom-call(f32[5,4,16,128]{3,2,1,0:T(8,128)} %bitcast.8, f32[3,5,5,4,16,128]{5,4,3,2,1,0:T(8,128)} %bitcast.7), custom_call_target="tpu_custom_call" | custom-call | bytes 5242880 | tf_op jit(solution)/shard_map/pallas_call | solution.py:61
  23.1 13.4 %all_to_all.30.refs_8_ = f32[16,5,4,128]{3,2,1,0:T(4,128)S(1)} all-to-all(f32[16,5,4,128]{3,2,1,0:T(4,128)S(1)} %shard_map.84), channel_id=1, replica_groups={{288,224,160,256,448,32,416,128,192,0,352,384,64,96,320,480},{289,225,1..., dimensions={0} | all-to-all | bytes 327680 | tf_op jit(solution)/shard_map/all_to_all | solution.py:373
  36.5 0.7 shard_map.85
  37.1 5.3 %collective-permute-start.2 = (f32[5,2,16,128]{3,2,1,0:T(8,128)S(1)}, f32[5,2,16,128]{3,2,1,0:T(8,128)S(1)}, u32[]{:S(2)}, u32[]{:S(2)}) collective-permute-start(f32[5,2,16,128]{3,2,1,0:T(8,128)S(1)} %get-tuple-element.40), channel_id=1, source_target_pairs={{1,2},{3,4},{5,6},{7,8},{9,10},{11,12},{13,14},{15,16},{17,18},{19... | collective-permute-start | bytes 245768 | tf_op jit(solution)/shard_map/ppermute | solution.py:369
  42.4 1.9 %collective-permute-start.3 = (f32[5,2,16,128]{3,2,1,0:T(8,128)S(1)}, f32[5,2,16,128]{3,2,1,0:T(8,128)S(1)}, u32[]{:S(2)}, u32[]{:S(2)}) collective-permute-start(f32[5,2,16,128]{3,2,1,0:T(8,128)S(1)} %get-tuple-element.41), channel_id=1, source_target_pairs={{0,1},{2,3},{4,5},{6,7},{8,9},{10,11},{12,13},{14,15},{16,17},{18,... | collective-permute-start | bytes 245768 | tf_op jit(solution)/shard_map/ppermute | solution.py:369
  44.8 0.8 collective-permute-done.2.refs_5_
  45.8 17.5 %all_to_all.31.refs_3_ = f32[16,5,8,128]{3,2,1,0:T(8,128)S(1)} all-to-all(f32[16,5,8,128]{3,2,1,0:T(8,128)S(1)} %shard_map.87), channel_id=1, replica_groups={{288,224,160,256,448,32,416,128,192,0,352,384,64,96,320,480},{289,225,1..., dimensions={0} | all-to-all | bytes 655360 | tf_op jit(solution)/shard_map/all_to_all | solution.py:373
  63.6 16.4 %all_to_all.32.back = f32[16,5,8,128]{3,2,1,0:T(8,128)S(1)} all-to-all(f32[16,5,8,128]{3,2,1,0:T(8,128)S(1)} %shard_map.88), channel_id=1, replica_groups={{288,224,160,256,448,32,416,128,192,0,352,384,64,96,320,480},{289,225,1..., dimensions={0} | all-to-all | bytes 655360 | tf_op jit(solution)/shard_map/all_to_all | solution.py:373
  80.1 3.3 %collective-permute-start.4 = (f32[5,2,16,128]{3,2,1,0:T(8,128)S(1)}, f32[5,2,16,128]{3,2,1,0:T(8,128)S(1)}, u32[]{:S(2)}, u32[]{:S(2)}) collective-permute-start(f32[5,2,16,128]{3,2,1,0:T(8,128)S(1)} %get-tuple-element.44), channel_id=1, source_target_pairs={{1,2},{3,4},{5,6},{7,8},{9,10},{11,12},{13,14},{15,16},{17,18},{19... | collective-permute-start | bytes 245768 | tf_op jit(solution)/shard_map/ppermute | solution.py:369
  83.4 1.9 %collective-permute-start.5 = (f32[5,2,16,128]{3,2,1,0:T(8,128)S(1)}, f32[5,2,16,128]{3,2,1,0:T(8,128)S(1)}, u32[]{:S(2)}, u32[]{:S(2)}) collective-permute-start(f32[5,2,16,128]{3,2,1,0:T(8,128)S(1)} %get-tuple-element.45), channel_id=1, source_target_pairs={{0,1},{2,3},{4,5},{6,7},{8,9},{10,11},{12,13},{14,15},{16,17},{18,... | collective-permute-start | bytes 245768 | tf_op jit(solution)/shard_map/ppermute | solution.py:369
  85.9 2.2 %collective-permute-done.4.refs_5_ = f32[5,2,16,128]{3,2,1,0:T(8,128)S(1)} collective-permute-done((f32[5,2,16,128]{3,2,1,0:T(8,128)S(1)}, f32[5,2,16,128]{3,2,1,0:T(8,128)S(1)}, u32[]{:S(2)}, u32[]{:S(2)}) %collective-permute-start.4) | collective-permute-done | bytes 81952 | tf_op jit(solution)/shard_map/ppermute | solution.py:369
  88.2 4.1 %collective-permute-start.6 = (f32[5,2,16,128]{3,2,1,0:T(8,128)S(1)}, f32[5,2,16,128]{3,2,1,0:T(8,128)S(1)}, u32[]{:S(2)}, u32[]{:S(2)}) collective-permute-start(f32[5,2,16,128]{3,2,1,0:T(8,128)S(1)} %get-tuple-element.47), channel_id=1, source_target_pairs={{1,2},{3,4},{5,6},{7,8},{9,10},{11,12},{13,14},{15,16},{17,18},{19... | collective-permute-start | bytes 245768 | tf_op jit(solution)/shard_map/ppermute | solution.py:369
  92.3 1.9 %collective-permute-start.7 = (f32[5,2,16,128]{3,2,1,0:T(8,128)S(1)}, f32[5,2,16,128]{3,2,1,0:T(8,128)S(1)}, u32[]{:S(2)}, u32[]{:S(2)}) collective-permute-start(f32[5,2,16,128]{3,2,1,0:T(8,128)S(1)} %get-tuple-element.48), channel_id=1, source_target_pairs={{0,1},{2,3},{4,5},{6,7},{8,9},{10,11},{12,13},{14,15},{16,17},{18,... | collective-permute-start | bytes 245768 | tf_op jit(solution)/shard_map/ppermute | solution.py:369
  94.7 1.4 %collective-permute-done.6.refs_5_ = f32[5,2,16,128]{3,2,1,0:T(8,128)S(1)} collective-permute-done((f32[5,2,16,128]{3,2,1,0:T(8,128)S(1)}, f32[5,2,16,128]{3,2,1,0:T(8,128)S(1)}, u32[]{:S(2)}, u32[]{:S(2)}) %collective-permute-start.6) | collective-permute-done | bytes 81952 | tf_op jit(solution)/shard_map/ppermute | solution.py:369
  96.3 15.6 %all_to_all.33.refs_3_ = f32[16,5,8,128]{3,2,1,0:T(8,128)S(1)} all-to-all(f32[16,5,8,128]{3,2,1,0:T(8,128)S(1)} %shard_map.93), channel_id=1, replica_groups={{288,224,160,256,448,32,416,128,192,0,352,384,64,96,320,480},{289,225,1..., dimensions={0} | all-to-all | bytes 655360 | tf_op jit(solution)/shard_map/all_to_all | solution.py:373
  112.3 16.8 %all_to_all.34.back = f32[16,5,8,128]{3,2,1,0:T(8,128)S(1)} all-to-all(f32[16,5,8,128]{3,2,1,0:T(8,128)S(1)} %shard_map.94), channel_id=1, replica_groups={{288,224,160,256,448,32,416,128,192,0,352,384,64,96,320,480},{289,225,1..., dimensions={0} | all-to-all | bytes 655360 | tf_op jit(solution)/shard_map/all_to_all | solution.py:373
  129.2 4.6 %collective-permute-start.8 = (f32[5,2,16,128]{3,2,1,0:T(8,128)S(1)}, f32[5,2,16,128]{3,2,1,0:T(8,128)S(1)}, u32[]{:S(2)}, u32[]{:S(2)}) collective-permute-start(f32[5,2,16,128]{3,2,1,0:T(8,128)S(1)} %get-tuple-element.51), channel_id=1, source_target_pairs={{1,2},{3,4},{5,6},{7,8},{9,10},{11,12},{13,14},{15,16},{17,18},{19... | collective-permute-start | bytes 245768 | tf_op jit(solution)/shard_map/ppermute | solution.py:369
  133.7 1.9 %collective-permute-start.9 = (f32[5,2,16,128]{3,2,1,0:T(8,128)S(1)}, f32[5,2,16,128]{3,2,1,0:T(8,128)S(1)}, u32[]{:S(2)}, u32[]{:S(2)}) collective-permute-start(f32[5,2,16,128]{3,2,1,0:T(8,128)S(1)} %get-tuple-element.52), channel_id=1, source_target_pairs={{0,1},{2,3},{4,5},{6,7},{8,9},{10,11},{12,13},{14,15},{16,17},{18,... | collective-permute-start | bytes 245768 | tf_op jit(solution)/shard_map/ppermute | solution.py:369
  136.1 1.5 %collective-permute-done.8.refs_5_ = f32[5,2,16,128]{3,2,1,0:T(8,128)S(1)} collective-permute-done((f32[5,2,16,128]{3,2,1,0:T(8,128)S(1)}, f32[5,2,16,128]{3,2,1,0:T(8,128)S(1)}, u32[]{:S(2)}, u32[]{:S(2)}) %collective-permute-start.8) | collective-permute-done | bytes 81952 | tf_op jit(solution)/shard_map/ppermute | solution.py:369
  137.7 0.8 shard_map.97
  (19 shorter events, 3.4 us)
Async XLA Ops:
  1.8 21.1 %all-to-all-start = ((f32[16,3,8,128]{3,2,1,0:T(8,128)}), f32[16,3,8,128]{3,2,1,0:T(8,128)S(1)}, u32[]{:S(2)}, u32[]{:S(2)}) async-start(f32[16,3,8,128]{3,2,1,0:T(8,128)} %get-tuple-element.37), calls=%async_computation | async-start | bytes 393216 | tf_op jit(solution)/shard_map/all_to_all | solution.py:373
  11.2 11.7 %collective-permute-start = (f32[7,2,16,128]{3,2,1,0:T(8,128)}, f32[7,2,16,128]{3,2,1,0:T(8,128)S(1)}, u32[]{:S(2)}, u32[]{:S(2)}) collective-permute-start(f32[7,2,16,128]{3,2,1,0:T(8,128)} %get-tuple-element.35), channel_id=1, source_target_pairs={{1,2},{3,4},{5,6},{7,8},{9,10},{11,12},{13,14},{15,16},{17,18},{19... | collective-permute-start | bytes 344072 | tf_op jit(solution)/shard_map/ppermute | solution.py:369
  17.9 5.1 %collective-permute-start.1 = (f32[7,2,16,128]{3,2,1,0:T(8,128)S(1)}, f32[7,2,16,128]{3,2,1,0:T(8,128)S(1)}, u32[]{:S(2)}, u32[]{:S(2)}) collective-permute-start(f32[7,2,16,128]{3,2,1,0:T(8,128)S(1)} %get-tuple-element.36), channel_id=1, source_target_pairs={{0,1},{2,3},{4,5},{6,7},{8,9},{10,11},{12,13},{14,15},{16,17},{18,... | collective-permute-start | bytes 344072 | tf_op jit(solution)/shard_map/ppermute | solution.py:369
  37.1 8.5 %collective-permute-start.2 = (f32[5,2,16,128]{3,2,1,0:T(8,128)S(1)}, f32[5,2,16,128]{3,2,1,0:T(8,128)S(1)}, u32[]{:S(2)}, u32[]{:S(2)}) collective-permute-start(f32[5,2,16,128]{3,2,1,0:T(8,128)S(1)} %get-tuple-element.40), channel_id=1, source_target_pairs={{1,2},{3,4},{5,6},{7,8},{9,10},{11,12},{13,14},{15,16},{17,18},{19... | collective-permute-start | bytes 245768 | tf_op jit(solution)/shard_map/ppermute | solution.py:369
  42.4 3.2 %collective-permute-start.3 = (f32[5,2,16,128]{3,2,1,0:T(8,128)S(1)}, f32[5,2,16,128]{3,2,1,0:T(8,128)S(1)}, u32[]{:S(2)}, u32[]{:S(2)}) collective-permute-start(f32[5,2,16,128]{3,2,1,0:T(8,128)S(1)} %get-tuple-element.41), channel_id=1, source_target_pairs={{0,1},{2,3},{4,5},{6,7},{8,9},{10,11},{12,13},{14,15},{16,17},{18,... | collective-permute-start | bytes 245768 | tf_op jit(solution)/shard_map/ppermute | solution.py:369
  80.1 7.9 %collective-permute-start.4 = (f32[5,2,16,128]{3,2,1,0:T(8,128)S(1)}, f32[5,2,16,128]{3,2,1,0:T(8,128)S(1)}, u32[]{:S(2)}, u32[]{:S(2)}) collective-permute-start(f32[5,2,16,128]{3,2,1,0:T(8,128)S(1)} %get-tuple-element.44), channel_id=1, source_target_pairs={{1,2},{3,4},{5,6},{7,8},{9,10},{11,12},{13,14},{15,16},{17,18},{19... | collective-permute-start | bytes 245768 | tf_op jit(solution)/shard_map/ppermute | solution.py:369
  83.4 4.6 %collective-permute-start.5 = (f32[5,2,16,128]{3,2,1,0:T(8,128)S(1)}, f32[5,2,16,128]{3,2,1,0:T(8,128)S(1)}, u32[]{:S(2)}, u32[]{:S(2)}) collective-permute-start(f32[5,2,16,128]{3,2,1,0:T(8,128)S(1)} %get-tuple-element.45), channel_id=1, source_target_pairs={{0,1},{2,3},{4,5},{6,7},{8,9},{10,11},{12,13},{14,15},{16,17},{18,... | collective-permute-start | bytes 245768 | tf_op jit(solution)/shard_map/ppermute | solution.py:369
  88.2 7.9 %collective-permute-start.6 = (f32[5,2,16,128]{3,2,1,0:T(8,128)S(1)}, f32[5,2,16,128]{3,2,1,0:T(8,128)S(1)}, u32[]{:S(2)}, u32[]{:S(2)}) collective-permute-start(f32[5,2,16,128]{3,2,1,0:T(8,128)S(1)} %get-tuple-element.47), channel_id=1, source_target_pairs={{1,2},{3,4},{5,6},{7,8},{9,10},{11,12},{13,14},{15,16},{17,18},{19... | collective-permute-start | bytes 245768 | tf_op jit(solution)/shard_map/ppermute | solution.py:369
  92.3 3.8 %collective-permute-start.7 = (f32[5,2,16,128]{3,2,1,0:T(8,128)S(1)}, f32[5,2,16,128]{3,2,1,0:T(8,128)S(1)}, u32[]{:S(2)}, u32[]{:S(2)}) collective-permute-start(f32[5,2,16,128]{3,2,1,0:T(8,128)S(1)} %get-tuple-element.48), channel_id=1, source_target_pairs={{0,1},{2,3},{4,5},{6,7},{8,9},{10,11},{12,13},{14,15},{16,17},{18,... | collective-permute-start | bytes 245768 | tf_op jit(solution)/shard_map/ppermute | solution.py:369
  129.2 8.5 %collective-permute-start.8 = (f32[5,2,16,128]{3,2,1,0:T(8,128)S(1)}, f32[5,2,16,128]{3,2,1,0:T(8,128)S(1)}, u32[]{:S(2)}, u32[]{:S(2)}) collective-permute-start(f32[5,2,16,128]{3,2,1,0:T(8,128)S(1)} %get-tuple-element.51), channel_id=1, source_target_pairs={{1,2},{3,4},{5,6},{7,8},{9,10},{11,12},{13,14},{15,16},{17,18},{19... | collective-permute-start | bytes 245768 | tf_op jit(solution)/shard_map/ppermute | solution.py:369
  133.7 3.9 %collective-permute-start.9 = (f32[5,2,16,128]{3,2,1,0:T(8,128)S(1)}, f32[5,2,16,128]{3,2,1,0:T(8,128)S(1)}, u32[]{:S(2)}, u32[]{:S(2)}) collective-permute-start(f32[5,2,16,128]{3,2,1,0:T(8,128)S(1)} %get-tuple-element.52), channel_id=1, source_target_pairs={{0,1},{2,3},{4,5},{6,7},{8,9},{10,11},{12,13},{14,15},{16,17},{18,... | collective-permute-start | bytes 245768 | tf_op jit(solution)/shard_map/ppermute | solution.py:369
